TPU v7x, 32 devices: a whole 2x2x4 slice. The times are simulated.
32 devices in a mesh: expert: 16 (over z, y, x), tensor: 2 (over core).
Axes of the slice: x: 2, y: 2, z: 4, core: 2. Of those that a mesh axis runs over, the one named last changes fastest.
Arguments:
- tokens: bfloat16 [6144, 768], P(('expert', 'tensor')), may hold values from -6 to 6
- lengths: int32 [16, 3], P('expert'), may hold values from 1 to 256, 384 in all within a row
- routes: int32 [6144, 1], P(('expert', 'tensor')), may hold values from 0 to 15; in each aligned block of 192 rows (0 to 191, 192 to 383, ...) at most 16 rows name the same one
- norm_gain: bfloat16 [768], replicated, may hold values from 0.5 to 1.5
- w_qkv: bfloat16 [3, 768, 768], P(None, None, 'tensor'), may hold values from -0.21875 to 0.21875
- rel_bias: bfloat16 [32, 12], P(None, 'tensor'), may hold values from -4 to 4
- w_out: bfloat16 [768, 768], P('tensor'), may hold values from -2.5 to 2.5
- moe_gain: bfloat16 [768], replicated, may hold values from 0.5 to 1.5
- w_router: bfloat16 [768, 16], replicated, may hold values from -0.109375 to 0.109375
- w_in: bfloat16 [16, 768, 3072], P('expert'), may hold values from -0.21875 to 0.21875
- w_down: bfloat16 [16, 3072, 768], P('expert')
- cotangent: bfloat16 [6144, 768], P(('expert', 'tensor')), may hold values from -6 to 6
Outputs:
- output: bfloat16 [6144, 768], P(('expert', 'tensor'))
- grad_tokens: float32 [6144, 768], P(('expert', 'tensor'))
- grad_norm_gain: float32 [768], replicated
- grad_w_qkv: float32 [3, 768, 768], P(None, None, 'tensor')
- grad_rel_bias: float32 [32, 12], P(None, 'tensor')
- grad_w_out: float32 [768, 768], P('tensor')
- grad_moe_gain: float32 [768], replicated
- grad_w_router: float32 [768, 16], replicated
- grad_w_in: float32 [16, 768, 3072], P('expert', None, 'tensor')
- grad_w_down: float32 [16, 3072, 768], P('expert', 'tensor')
Inputs may be any that keep to these rules, and one draw needn't show every extreme that they name: Each row packs 3 sequences into a group of 384 tokens: the lengths sum to 384, and the longest is exactly 256. `routes`: among the 192 rows of one device no expert is named more than 16 times.
All inputs are finite; a program needn't handle non-finite values.
Results may differ from a plain program's by a relative error of at most 0.012.
Values may be sent and summed in bfloat16 or wider, within the bound.
No kernel may reach another device: no remote copies, remote signals or barrier semaphores. Data moves between devices by JAX's collectives and lax.ppermute only.
A program may use at most 128 MiB of HBM per device.

v0:
```python
import functools

import jax
import jax.numpy as jnp
from jax import lax
from jax.experimental import pallas as pl
from jax.experimental.pallas import tpu as pltpu
from jax.sharding import PartitionSpec as P

HEAD = 64
TILE = 128
FF_TILE = 512

epsilon = 1e-06
THRESHOLDS = (1, 2, 3, 4, 5, 6, 7, 8, 12, 16, 23, 32, 46, 64, 91)
halfway = 16
BF = jnp.bfloat16
F32 = jnp.float32
HIGH = lax.Precision.HIGHEST
MIB = 1 << 20


def mm(a, b):
    return lax.dot_general(a, b, (((1,), (0,)), ((), ())), preferred_element_type=F32)


def mm_nt(a, b):
    return lax.dot_general(a, b, (((1,), (1,)), ((), ())), preferred_element_type=F32)


def mm_tn(a, b):
    return lax.dot_general(a, b, (((0,), (0,)), ((), ())), preferred_element_type=F32)


def iota(shape, dim):
    return lax.broadcasted_iota(jnp.int32, shape, dim)


def vmem_specs(count):
    return [pl.BlockSpec(memory_space=pltpu.VMEM)] * count


SMEM = pl.BlockSpec(memory_space=pltpu.SMEM)


def shape_of(*pairs):
    return tuple(jax.ShapeDtypeStruct(shape, dtype) for shape, dtype in pairs)


def params(mib):
    return pltpu.CompilerParams(vmem_limit_bytes=mib * MIB)


def bucket_of(distance):
    magnitude = jnp.abs(distance)
    bucket = jnp.zeros(distance.shape, jnp.int32)
    for border in THRESHOLDS:
        bucket = bucket + (magnitude >= border).astype(jnp.int32)
    return bucket + jnp.where(distance > 0, halfway, 0).astype(jnp.int32)


def distance_hot(buckets, delta):
    distance = iota((buckets, 2 * TILE), 1) + (TILE * delta - (TILE - 1))
    return bucket_of(distance) == iota((buckets, 2 * TILE), 0)


def prep_body(capacity, experts, routes_ref, cot_ref, place_ref, out_ref):
    rows = cot_ref.shape[0]
    chosen = routes_ref[...]
    hot = chosen == iota((rows, experts), 1)
    below = (iota((rows, rows), 1) < iota((rows, rows), 0)).astype(F32).astype(BF)
    earlier = mm(below, hot.astype(F32).astype(BF))
    ordinal = jnp.sum(jnp.where(hot, earlier, 0.0), axis=1, keepdims=True)
    slot = chosen * capacity + ordinal.astype(jnp.int32)
    place = (slot == iota((rows, experts * capacity), 1)).astype(F32).astype(BF)
    place_ref[...] = place
    out_ref[...] = mm_tn(place, cot_ref[...]).astype(BF)


def attend_body(
    half_ref, lengths_ref, x_ref, gain_ref, w_ref, bias_ref,
    own_ref, other_ref, context_ref, qkv_ref, probs_ref, normed_ref,
):
    group = x_ref.shape[0]
    rows = own_ref.shape[0]
    local = w_ref.shape[2]
    heads = local // HEAD
    blocks = group // TILE
    x = x_ref[...].astype(F32)
    factor = lax.rsqrt(jnp.mean(x * x, axis=-1, keepdims=True) + epsilon)
    normed = (x * factor * gain_ref[...].astype(F32)).astype(BF)
    normed_ref[...] = normed
    for c in range(3):
        qkv_ref[:, c * local : (c + 1) * local] = mm(normed, w_ref[c]).astype(BF)
    buckets = bias_ref.shape[1]
    tables = [
        mm(bias_ref[...], distance_hot(buckets, delta).astype(F32).astype(BF))
        for delta in range(1 - blocks, blocks)
    ]
    segment_rows = jnp.zeros((group, 1), jnp.int32)
    segment_lanes = jnp.zeros((1, group), jnp.int32)
    border = jnp.int32(0)
    for s in range(lengths_ref.shape[1]):
        border = border + lengths_ref[0, s]
        segment_rows = segment_rows + (iota((group, 1), 0) >= border).astype(jnp.int32)
        segment_lanes = segment_lanes + (iota((1, group), 1) >= border).astype(jnp.int32)
    for h in range(heads):
        lo = h * HEAD
        keys = qkv_ref[:, local + lo : local + lo + HEAD]
        values = qkv_ref[:, 2 * local + lo : 2 * local + lo + HEAD]
        bands = []
        for number, delta in enumerate(range(1 - blocks, blocks)):
            row = tables[number][h : h + 1, :]
            if abs(delta) > 1:
                bands.append(jnp.broadcast_to(row[:, :1], (TILE, TILE)))
            else:
                wide = jnp.broadcast_to(row, (TILE, 2 * TILE))
                band = pltpu.roll(wide, TILE + 1, 1, stride=1, stride_axis=0)
                bands.append(band[:, :TILE])
        for b in range(blocks):
            at = slice(b * TILE, (b + 1) * TILE)
            queries = qkv_ref[at, lo : lo + HEAD]
            scores = mm_nt(queries, keys) * (HEAD**-0.5)
            scores = scores + jnp.concatenate(
                [bands[k - b + blocks - 1] for k in range(blocks)], axis=1
            )
            scores = jnp.where(segment_rows[at] == segment_lanes, scores, -1e30)
            exponent = jnp.exp(scores - jnp.max(scores, axis=-1, keepdims=True))
            probs = exponent * (1.0 / jnp.sum(exponent, axis=-1, keepdims=True))
            low = probs.astype(BF)
            probs_ref[h, at, :] = low
            context_ref[at, lo : lo + HEAD] = mm(low, values).astype(BF)
    own_at = pl.multiple_of(half_ref[0] * rows, rows)
    other_at = pl.multiple_of((1 - half_ref[0]) * rows, rows)
    own_ref[...] = context_ref[pl.ds(own_at, rows), :]
    other_ref[...] = context_ref[pl.ds(other_at, rows), :]


def project_body(
    own_ref, other_ref, w_own_ref, w_other_ref, x_ref, gain_ref, place_ref, residual_ref, out_ref
):
    attended = mm(own_ref[...], w_own_ref[...]) + mm(other_ref[...], w_other_ref[...])
    residual = x_ref[...].astype(F32) + attended
    residual_ref[...] = residual
    factor = lax.rsqrt(jnp.mean(residual * residual, axis=-1, keepdims=True) + epsilon)
    moe_rows = (residual * factor * gain_ref[...].astype(F32)).astype(BF)
    out_ref[...] = mm_tn(place_ref[...], moe_rows).astype(BF)


def expert_body(
    half_ref, expert_ref, rows_ref, cot_ref, router_ref, up_ref, down_ref,
    scaled_ref, back_ref, router_grad_ref, gp_ref, send_ref, act_ref, pre_ref,
    out_acc, back_acc, gating_ref, chances_ref,
):
    step = pl.program_id(0)
    steps = pl.num_programs(0)
    half_steps = steps // 2
    tile = up_ref.shape[1]
    width = rows_ref.shape[1]
    ff_half = act_ref.shape[1]
    rows = rows_ref[...]

    @pl.when(step == 0)
    def _():
        logits = mm(rows, router_ref[...])
        exponent = jnp.exp(logits - jnp.max(logits, axis=-1, keepdims=True))
        chances = exponent / jnp.sum(exponent, axis=-1, keepdims=True)
        mine = iota(chances.shape, 1) == expert_ref[0]
        gating = jnp.sum(jnp.where(mine, chances, 0.0), axis=-1, keepdims=True)
        gating_ref[...] = jnp.broadcast_to(gating, gating_ref.shape)
        chances_ref[...] = chances
        gp = (gating * cot_ref[...].astype(F32)).astype(BF)
        gp_ref[...] = gp
        send_ref[:, 2 * ff_half : 2 * ff_half + width] = rows
        send_ref[:, 2 * ff_half + width :] = gp
        out_acc[...] = jnp.zeros_like(out_acc)
        back_acc[...] = jnp.zeros_like(back_acc)

    hidden = mm(rows, up_ref[...])
    phi = 0.5 * (1.0 + lax.erf(hidden * (2.0**-0.5)))
    act = (hidden * phi).astype(BF)
    slope = phi + hidden * (jnp.exp(-0.5 * hidden * hidden) * 0.3989422804014327)
    pre = (mm_nt(gp_ref[...], down_ref[...]) * slope).astype(BF)
    out_acc[...] += mm(act, down_ref[...])
    back_acc[...] += mm_nt(pre, up_ref[...])

    @pl.when(step < half_steps)
    def _():
        at = pl.multiple_of(step * tile, tile)
        send_ref[:, pl.ds(at, tile)] = act
        send_ref[:, pl.ds(pl.multiple_of(ff_half + step * tile, tile), tile)] = pre

    @pl.when(step >= half_steps)
    def _():
        at = pl.multiple_of((step - half_steps) * tile, tile)
        act_ref[:, pl.ds(at, tile)] = act
        pre_ref[:, pl.ds(at, tile)] = pre

    @pl.when(step == steps - 1)
    def _():
        gating = gating_ref[:, :1]
        produced = out_acc[...].astype(BF).astype(F32)
        scaled_ref[...] = (gating * produced).astype(BF)
        grad_gate = jnp.sum(cot_ref[...].astype(F32) * produced, axis=-1, keepdims=True)
        chances = chances_ref[...]
        mine = (iota(chances.shape, 1) == expert_ref[0]).astype(F32)
        grad_logits = gating * (mine - chances) * grad_gate
        low = grad_logits.astype(BF)
        rest = (grad_logits - low.astype(F32)).astype(BF)
        back = back_acc[...] + (mm_nt(low, router_ref[...]) + mm_nt(rest, router_ref[...]))
        back_ref[...] = back.astype(BF)
        router_grad_ref[...] = mm_tn(low, rows) + mm_tn(rest, rows)


def expert_grads_body(
    act_ref, pre_ref, rows_ref, gp_ref, act2_ref, pre2_ref, rows2_ref, gp2_ref, down_ref, up_ref
):
    down_ref[...] = mm_tn(act_ref[...], gp_ref[...]) + mm_tn(act2_ref[...], gp2_ref[...])
    up_ref[...] = mm_tn(rows_ref[...], pre_ref[...]) + mm_tn(rows2_ref[...], pre2_ref[...])


def norm_back(grad, source, gain):
    factor = lax.rsqrt(jnp.mean(source * source, axis=-1, keepdims=True) + epsilon)
    unit = source * factor
    scaled = grad * gain
    inner = jnp.mean(scaled * unit, axis=-1, keepdims=True)
    return factor * (scaled - unit * inner), grad * unit


def moe_back_body(place_ref, back_ref, residual_ref, gain_ref, cot_ref, grad_ref, low_ref, gain_grad_ref):
    grad_in = mm(place_ref[...], back_ref[...])
    passed, terms = norm_back(grad_in, residual_ref[...], gain_ref[...].astype(F32))
    grad = cot_ref[...].astype(F32) + passed
    grad_ref[...] = grad
    low_ref[...] = grad.astype(BF)
    gain_grad_ref[...] = jnp.sum(terms, axis=0, keepdims=True)


def fold_diagonals(square):
    wide = jnp.concatenate([square, jnp.zeros_like(square)], axis=1)
    count = TILE
    while count > 8:
        count //= 2
        wide = wide[:count] + pltpu.roll(wide[count:], 2 * TILE - count, 1)
    total = wide[:1]
    for i in range(1, 8):
        total = total + pltpu.roll(wide[i : i + 1], 2 * TILE - i, 1)
    return total


def attend_back_body(
    half_ref, bit_ref, grad_ref, w_out_ref, context_ref, qkv_ref, probs_ref, normed_ref, w_ref, x_ref, gain_ref,
    router_grad_ref, moe_gain_grad_ref,
    send_ref, keep_ref, own_ref, other_ref,
    gqkv_ref, all_ref, gctx_ref,
):
    group = x_ref.shape[0]
    width = x_ref.shape[1]
    rows = own_ref.shape[0]
    local = w_ref.shape[2]
    heads = local // HEAD
    blocks = group // TILE
    grad = grad_ref[...]
    gctx_ref[...] = mm_nt(grad, w_out_ref[...]).astype(BF)
    heads_distance = []
    scale = HEAD**-0.5
    buckets = 2 * halfway
    table = jnp.zeros((8, buckets), F32)
    per_distance = [[] for _ in range(3)]
    edges = [[], []]
    for h in range(heads):
        lo = h * HEAD
        queries = qkv_ref[:, lo : lo + HEAD]
        keys = qkv_ref[:, local + lo : local + lo + HEAD]
        values = qkv_ref[:, 2 * local + lo : 2 * local + lo + HEAD]
        gctx = gctx_ref[:, lo : lo + HEAD]
        low_probs = probs_ref[h]
        grad_probs = mm_nt(gctx, values)
        probs = low_probs.astype(F32)
        inner = jnp.sum(probs * grad_probs, axis=-1, keepdims=True)
        grad_scores = probs * (grad_probs - inner)
        low = grad_scores.astype(BF)
        gqkv_ref[:, lo : lo + HEAD] = (mm(low, keys) * scale).astype(BF)
        gqkv_ref[:, local + lo : local + lo + HEAD] = (mm_tn(low, queries) * scale).astype(BF)
        gqkv_ref[:, 2 * local + lo : 2 * local + lo + HEAD] = mm_tn(low_probs, gctx).astype(BF)
        for number, delta in enumerate((-1, 0, 1)):
            band = None
            for b in range(blocks):
                k = b + delta
                if 0 <= k < blocks:
                    piece = grad_scores[
                        b * TILE : (b + 1) * TILE, k * TILE : (k + 1) * TILE
                    ]
                    band = piece if band is None else band + piece
            per_distance[number].append(fold_diagonals(band))
        for number, sign in enumerate((-1, 1)):
            total = jnp.zeros((1, 1), F32)
            for b in range(blocks):
                for k in range(blocks):
                    if (k - b) * sign > 1:
                        piece = grad_scores[
                            b * TILE : (b + 1) * TILE, k * TILE : (k + 1) * TILE
                        ]
                        total = total + jnp.sum(
                            jnp.sum(piece, axis=0, keepdims=True), axis=1, keepdims=True
                        )
            edges[number].append(total)
    pad = [jnp.zeros((8 - heads, 2 * TILE), F32)]
    for number, delta in enumerate((-1, 0, 1)):
        sums = jnp.concatenate(per_distance[number] + pad, axis=0)
        distance = iota((buckets, 2 * TILE), 1)
        distance = jnp.where(distance >= TILE, distance - 2 * TILE, distance) + TILE * delta
        hot = (bucket_of(distance) == iota((buckets, 2 * TILE), 0)).astype(F32)
        table = table + lax.dot_general(
            sums, hot, (((1,), (1,)), ((), ())), precision=HIGH, preferred_element_type=F32
        )
    for number, bucket in enumerate((halfway - 1, 2 * halfway - 1)):
        column = jnp.concatenate(edges[number] + [jnp.zeros((8 - heads, 1), F32)], axis=0)
        table = table + jnp.where(iota((8, buckets), 1) == bucket, column, 0.0)
    total = None
    for c in range(3):
        part = mm_nt(gqkv_ref[:, c * local : (c + 1) * local], w_ref[c])
        total = part if total is None else total + part
    all_ref[...] = total
    own_at = pl.multiple_of(half_ref[0] * rows, rows)
    other_at = pl.multiple_of((1 - half_ref[0]) * rows, rows)
    own_ref[...] = all_ref[pl.ds(own_at, rows), :]
    other_ref[...] = all_ref[pl.ds(other_at, rows), :]
    x = x_ref[...].astype(F32)
    factor = lax.rsqrt(jnp.mean(x * x, axis=-1, keepdims=True) + epsilon)
    gain_grad = jnp.sum(total * (x * factor), axis=0, keepdims=True)
    first = iota((8, width), 0)
    gains = jnp.where(first == 0, moe_gain_grad_ref[...], jnp.where(first == 1, gain_grad, 0.0))
    experts = router_grad_ref.shape[0]
    small = send_ref.shape[1] - 4 * local
    stacked = jnp.concatenate(
        [
            router_grad_ref[...],
            gains,
            jnp.concatenate([table, jnp.zeros((8, width - buckets), F32)], axis=1),
            jnp.zeros((small - experts - 16, width), F32),
        ],
        axis=0,
    )
    columns = stacked.T
    half_width = width // 2
    for part in range(2):
        at = slice(part * half_width, (part + 1) * half_width)
        w_qkv = mm_tn(normed_ref[:, at], gqkv_ref[...]).astype(BF)
        w_out = mm_tn(grad_ref[:, at], context_ref[...]).astype(BF)
        low = columns[at].astype(BF)
        for wanted, target in ((True, keep_ref), (False, send_ref)):

            @pl.when((bit_ref[0] == part) == wanted)
            def _(target=target, w_qkv=w_qkv, w_out=w_out, low=low):
                target[:, : 3 * local] = w_qkv
                target[:, 3 * local : 4 * local] = w_out
                target[:, 4 * local :] = low


def tokens_body(
    place_ref, scaled_ref, residual_ref, own_ref, got_ref, x_ref, gain_ref, grad_res_ref, out_ref, grad_ref
):
    out_ref[...] = (residual_ref[...] + mm(place_ref[...], scaled_ref[...])).astype(BF)
    passed, _ = norm_back(
        own_ref[...] + got_ref[...], x_ref[...].astype(F32), gain_ref[...].astype(F32)
    )
    grad_ref[...] = grad_res_ref[...] + passed


def unpack_body(bit_ref, own_ref, got_ref, small_ref, qkv_ref, out_ref, router_ref, rows_ref):
    local = qkv_ref.shape[2]
    half = own_ref.shape[0]
    experts = router_ref.shape[1]
    own_at = pl.multiple_of(bit_ref[0] * half, half)
    got_at = pl.multiple_of((1 - bit_ref[0]) * half, half)
    for ref, at in ((own_ref, own_at), (got_ref, got_at)):
        for c in range(3):
            qkv_ref[c, pl.ds(at, half), :] = ref[:, c * local : (c + 1) * local].astype(F32)
        out_ref[:, pl.ds(at, half)] = ref[:, 3 * local : 4 * local].astype(F32).T
    small = small_ref[...]
    router_ref[...] = small[:, :experts]
    rows_ref[...] = small.T[experts : experts + 16]


def per_device(
    tokens, lengths, routes, norm_gain, w_qkv, rel_bias, w_out, moe_gain, w_router, w_in, w_down, cotangent
):
    rows, width = tokens.shape
    sources = lax.axis_size("expert")
    group = rows * lax.axis_size("tensor")
    experts = w_router.shape[1]
    capacity = max(2, 4 * rows // (3 * experts))
    slots = experts * capacity
    local = w_qkv.shape[2]
    heads = local // HEAD
    buckets = rel_bias.shape[0]
    ff = w_in.shape[2]
    ff_half = ff // 2
    half = lax.axis_index("tensor").astype(jnp.int32)
    expert = lax.axis_index("expert").astype(jnp.int32)
    half_one = half.reshape(1)
    gain_a = norm_gain.reshape(1, width)
    gain_b = moe_gain.reshape(1, width)
    small = TILE * -(-(experts + 16) // TILE)
    packed = 4 * local + small

    def swap(value):
        return lax.ppermute(value, "tensor", [(0, 1), (1, 0)])

    def exchange(value):
        return lax.all_to_all(
            value.reshape(experts, capacity, width), "expert", split_axis=0, concat_axis=0, tiled=True
        ).reshape(slots, width)

    w_out_other = swap(w_out)
    place, cot_slots = pl.pallas_call(
        functools.partial(prep_body, capacity, experts),
        out_shape=shape_of(((rows, slots), BF), ((slots, width), BF)),
        in_specs=vmem_specs(2),
        out_specs=vmem_specs(2),
        name="place_cotangent",
    )(routes, cotangent)
    cot_rows = exchange(cot_slots)

    x_group = lax.all_gather(tokens, "tensor", axis=0, tiled=True)
    bias_rows = jnp.pad(rel_bias.T, ((0, 8 - heads), (0, 0)))
    own_ctx, other_ctx, context, qkv, probs, normed = pl.pallas_call(
        attend_body,
        out_shape=shape_of(
            ((rows, local), BF),
            ((rows, local), BF),
            ((group, local), BF),
            ((group, 3 * local), BF),
            ((heads, group, group), BF),
            ((group, width), BF),
        ),
        in_specs=[SMEM, SMEM] + vmem_specs(4),
        out_specs=vmem_specs(6),
        compiler_params=params(40),
        name="attention",
    )(half_one, lengths, x_group, gain_a, w_qkv, bias_rows)
    got_ctx = swap(other_ctx)

    residual, moe_slots = pl.pallas_call(
        project_body,
        out_shape=shape_of(((rows, width), F32), ((slots, width), BF)),
        in_specs=vmem_specs(7),
        out_specs=vmem_specs(2),
        compiler_params=params(24),
        name="projection",
    )(own_ctx, got_ctx, w_out, w_out_other, tokens, gain_b, place)
    stacked = exchange(moe_slots)

    count = sources * capacity
    tile = FF_TILE
    steps = ff // tile
    half_steps = steps // 2

    def weight_tile(step, half_ref, _):
        first = jnp.where(step < half_steps, 1 - half_ref[0], half_ref[0])
        return first * half_steps + lax.rem(step, half_steps)

    whole = lambda shape: pl.BlockSpec(shape, lambda i, *_: (0, 0))
    scaled, back, router_grad, gp, send, act, pre = pl.pallas_call(
        expert_body,
        grid_spec=pltpu.PrefetchScalarGridSpec(
            num_scalar_prefetch=2,
            grid=(steps,),
            in_specs=[
                whole((count, width)),
                whole((count, width)),
                whole((width, experts)),
                pl.BlockSpec((width, tile), lambda i, a, b: (0, weight_tile(i, a, b))),
                pl.BlockSpec((tile, width), lambda i, a, b: (weight_tile(i, a, b), 0)),
            ],
            out_specs=[
                whole((count, width)),
                whole((count, width)),
                whole((experts, width)),
                whole((count, width)),
                whole((count, 2 * ff_half + 2 * width)),
                whole((count, ff_half)),
                whole((count, ff_half)),
            ],
            scratch_shapes=[
                pltpu.VMEM((count, width), F32),
                pltpu.VMEM((count, width), F32),
                pltpu.VMEM((count, TILE), F32),
                pltpu.VMEM((count, experts), F32),
            ],
        ),
        out_shape=shape_of(
            ((count, width), BF),
            ((count, width), BF),
            ((experts, width), F32),
            ((count, width), BF),
            ((count, 2 * ff_half + 2 * width), BF),
            ((count, ff_half), BF),
            ((count, ff_half), BF),
        ),
        compiler_params=params(40),
        name="expert",
    )(half_one, expert.reshape(1), stacked, cot_rows, w_router, w_in[0], w_down[0])
    back_rows = exchange(back)
    peer = swap(send)
    scaled_rows = exchange(scaled)

    grad_res, grad_low, moe_gain_grad = pl.pallas_call(
        moe_back_body,
        out_shape=shape_of(((rows, width), F32), ((rows, width), BF), ((1, width), F32)),
        in_specs=vmem_specs(5),
        out_specs=vmem_specs(3),
        compiler_params=params(24),
        name="norm_back",
    )(place, back_rows, residual, gain_b, cotangent)
    grad_att = lax.all_gather(grad_low, "tensor", axis=0, tiled=True)

    bits = sources.bit_length() - 1
    bit_at = lambda b: (expert >> b) & 1
    first_bit = jnp.where(half == 0, bit_at(0), bit_at(1))
    second_bit = jnp.where(half == 0, bit_at(1), bit_at(0))
    half_width = width // 2
    send_a, keep_a, own_gn, other_gn = pl.pallas_call(
        attend_back_body,
        out_shape=shape_of(
            ((half_width, packed), BF),
            ((half_width, packed), BF),
            ((rows, width), F32),
            ((rows, width), F32),
        ),
        in_specs=[SMEM, SMEM] + vmem_specs(11),
        out_specs=vmem_specs(4),
        scratch_shapes=[
            pltpu.VMEM((group, 3 * local), BF),
            pltpu.VMEM((group, width), F32),
            pltpu.VMEM((group, local), BF),
        ],
        compiler_params=params(48),
        name="attention_back",
    )(
        half_one, first_bit.reshape(1), grad_att, w_out, context, qkv, probs, normed, w_qkv, x_group,
        gain_a, router_grad, moe_gain_grad,
    )
    got_gn = swap(other_gn)

    def pair(value, step):
        moves = []
        for e in range(sources):
            for t in range(2):
                b = step if step > 1 or t == 0 else 1 - step
                moves.append((2 * e + t, 2 * (e ^ (1 << b)) + t))
        return lax.ppermute(value, ("expert", "tensor"), moves)

    def add(a, b):
        return (a.astype(F32) + b.astype(F32)).astype(BF)

    got = pair(send_a, 0)
    step_bits = [first_bit, second_bit] + [bit_at(b) for b in range(2, bits)]
    held = [keep_a, got]
    size = half_width
    depth = 1
    while depth < bits and size % 32 == 0:
        size //= 2
        bit = step_bits[depth]
        cut = lambda v, at: lax.dynamic_slice_in_dim(v, at * size, size, axis=0)
        sent = add(cut(held[0], 1 - bit), cut(held[1], 1 - bit))
        kept = add(cut(held[0], bit), cut(held[1], bit))
        held = [kept, pair(sent, depth)]
        depth += 1
    total = add(*held)
    for later in range(depth, bits):
        total = add(total, pair(total, later))
    for back_step in range(depth - 1, 0, -1):
        received = pair(total, back_step)
        bit = step_bits[back_step]
        total = jnp.concatenate(
            [jnp.where(bit == 0, total, received), jnp.where(bit == 0, received, total)], axis=0
        )
    other_half = pair(total, 0)
    mine_small = total[:, 4 * local :].astype(F32)
    got_small = other_half[:, 4 * local :].astype(F32)
    small_all = jnp.concatenate(
        [jnp.where(first_bit == 0, mine_small, got_small), jnp.where(first_bit == 0, got_small, mine_small)],
        axis=0,
    )
    from_other = swap(small_all.astype(BF)).astype(F32)
    shared = (lax.iota(jnp.int32, small) < experts + 8)[None, :]
    small_sum = small_all + jnp.where(shared, from_other, 0.0)

    grad_qkv, grad_out, grad_router, small_rows = pl.pallas_call(
        unpack_body,
        out_shape=shape_of(
            ((3, width, local), F32),
            ((local, width), F32),
            ((width, experts), F32),
            ((16, width), F32),
        ),
        in_specs=[SMEM] + vmem_specs(3),
        out_specs=vmem_specs(4),
        compiler_params=params(40),
        name="unpack",
    )(first_bit.reshape(1), total, other_half, small_sum)

    output, grad_tokens = pl.pallas_call(
        tokens_body,
        out_shape=shape_of(((rows, width), BF), ((rows, width), F32)),
        in_specs=vmem_specs(8),
        out_specs=vmem_specs(2),
        compiler_params=params(24),
        name="token_outputs",
    )(place, scaled_rows, residual, own_gn, got_gn, tokens, gain_a, grad_res)

    col = lambda first: pl.BlockSpec((count, tile), lambda i: (0, first + i))
    fixed = lambda block: pl.BlockSpec((count, width), lambda i: (0, block))
    grad_down, grad_up = pl.pallas_call(
        expert_grads_body,
        grid=(half_steps,),
        in_specs=[
            col(0), col(0), fixed(0), fixed(0),
            col(0), col(half_steps), fixed(2 * ff_half // width), fixed(2 * ff_half // width + 1),
        ],
        out_specs=[
            pl.BlockSpec((tile, width), lambda i: (i, 0)),
            pl.BlockSpec((width, tile), lambda i: (0, i)),
        ],
        out_shape=shape_of(((ff_half, width), F32), ((width, ff_half), F32)),
        compiler_params=params(32),
        name="expert_grads",
    )(act, pre, stacked, gp, peer, peer, peer, peer)

    return (
        output,
        grad_tokens,
        small_rows[1],
        grad_qkv,
        small_rows[8 : 8 + heads, :buckets].T,
        grad_out,
        small_rows[0],
        grad_router,
        grad_up[None],
        grad_down[None],
    )


def solution(mesh):
    return jax.shard_map(
        per_device,
        mesh=mesh,
        in_specs=(
            P(("expert", "tensor"), None),
            P("expert", None),
            P(("expert", "tensor"), None),
            P(),
            P(None, None, "tensor"),
            P(None, "tensor"),
            P("tensor", None),
            P(),
            P(),
            P("expert", None, None),
            P("expert", None, None),
            P(("expert", "tensor"), None),
        ),
        out_specs=(
            P(("expert", "tensor"), None),
            P(("expert", "tensor"), None),
            P(),
            P(None, None, "tensor"),
            P(None, "tensor"),
            P("tensor", None),
            P(),
            P(),
            P("expert", None, "tensor"),
            P("expert", "tensor", None),
        ),
        check_vma=False,
    )
```

profile of v0, /device:TPU:0, one launch (start us, length us, event | category | flops | bytes accessed | tf_op | source)
XLA Modules:
  0.0 221.0 jit_solution(2188251022640349146)
XLA Ops:
  2.3 2.5 %place_cotangent.1 = (bf16[192,256]{1,0:T(8,128)(2,1)}, bf16[256,768]{1,0:T(8,128)(2,1)}) custom-call(s32[192,1]{1,0:T(8,128)} %copy.22.routes_ref, bf16[192,768]{1,0:T(8,128)(2,1)} %cot_ref.3), custom_call_target="tpu_custom_call" | custom-call | tf_op jit(solution)/shard_map/place_cotangent/pallas_call | solution.py:417
  4.8 8.3 %all-to-all-start.1 = ((bf16[16,16,768]{2,1,0:T(8,128)(2,1)}), bf16[16,16,768]{2,1,0:T(8,128)(2,1)S(1)}, u32[]{:S(2)}, u32[]{:S(2)}) async-start(bf16[16,16,768]{2,1,0:T(8,128)(2,1)} %bitcast.26), calls=%async_computation.1 | async-start | bytes 786432 | tf_op jit(solution)/shard_map/all_to_all | solution.py:412
  15.6 8.3 %attention.1 = (bf16[192,384]{1,0:T(8,128)(2,1)S(1)}, bf16[192,384]{1,0:T(8,128)(2,1)S(1)}, bf16[384,384]{1,0:T(8,128)(2,1)S(1)}, bf16[384,1152]{1,0:T(8,128)(2,...) custom-call(s32[1]{0:T(128)} %bitcast.half_ref, s32[1,3]{1,0:T(1,128)S(1)} %copy-done.27, ...), custom_call_target="tpu_custom_call" | custom-call | tf_op jit(solution)/shard_map/attention/pallas_call | solution.py:428
  29.0 2.8 %projection.1 = (f32[192,768]{1,0:T(8,128)S(1)}, bf16[256,768]{1,0:T(8,128)(2,1)}) custom-call(bf16[192,384]{1,0:T(8,128)(2,1)S(1)} %get-tuple-element.43.own_ref, bf16[192,384]{1,0:T(8,128)(2,1)S(1)} %collective-permute-done.other_ref, bf16[384,768]{1,0:T(8,128)(2,1)S(1)} %copy-done.5, bf16[384,768]{1,0:T(8,128)(2,1)} %collective-permute-done.1.w_other_ref, ...), custom_call_target="tpu_custom_call" | custom-call | tf_op jit(solution)/shard_map/projection/pallas_call | solution.py:445
  31.8 6.8 %all-to-all-start = ((bf16[16,16,768]{2,1,0:T(8,128)(2,1)}), bf16[16,16,768]{2,1,0:T(8,128)(2,1)S(1)}, u32[]{:S(2)}, u32[]{:S(2)}) async-start(bf16[16,16,768]{2,1,0:T(8,128)(2,1)} %bitcast.3), calls=%async_computation | async-start | bytes 786432 | tf_op jit(solution)/shard_map/all_to_all | solution.py:412
  38.8 12.9 %all-to-all-done = bf16[16,16,768]{2,1,0:T(8,128)(2,1)S(1)} async-done(((bf16[16,16,768]{2,1,0:T(8,128)(2,1)}), bf16[16,16,768]{2,1,0:T(8,128)(2,1)S(1)}, u32[]{:S(2)}, u32[]{:S(2)}) %all-to-all-start) | async-done | bytes 393248 | tf_op jit(solution)/shard_map/all_to_all | solution.py:412
  54.1 10.1 %expert.1 = (bf16[256,768]{1,0:T(8,128)(2,1)S(1)}, bf16[256,768]{1,0:T(8,128)(2,1)}, f32[16,768]{1,0:T(8,128)S(1)}, bf16[256,768]{1,0:T(8,128)(2,1)S(1)}, bf16[2...) custom-call(s32[1]{0:T(128)} %bitcast.half_ref, s32[1]{0:T(128)} %bitcast.1.expert_ref, ...), custom_call_target="tpu_custom_call" | custom-call | tf_op jit(solution)/shard_map/expert/pallas_call | solution.py:465
  68.9 3.8 %all-to-all-start.3 = ((bf16[16,16,768]{2,1,0:T(8,128)(2,1)}), bf16[16,16,768]{2,1,0:T(8,128)(2,1)S(1)}, u32[]{:S(2)}, u32[]{:S(2)}) async-start(bf16[16,16,768]{2,1,0:T(8,128)(2,1)} %bitcast.12), calls=%async_computation.3 | async-start | bytes 786432 | tf_op jit(solution)/shard_map/all_to_all | solution.py:412
  72.7 12.0 %all-to-all-done.3 = bf16[16,16,768]{2,1,0:T(8,128)(2,1)S(1)} async-done(((bf16[16,16,768]{2,1,0:T(8,128)(2,1)}), bf16[16,16,768]{2,1,0:T(8,128)(2,1)S(1)}, u32[]{:S(2)}, u32[]{:S(2)}) %all-to-all-start.3) | async-done | bytes 393248 | tf_op jit(solution)/shard_map/all_to_all | solution.py:412
  87.0 2.4 %all_gather.7.grad_ref = bf16[384,768]{1,0:T(8,128)(2,1)S(1)} all-gather(bf16[192,768]{1,0:T(8,128)(2,1)S(1)} %get-tuple-element.50), channel_id=1, replica_groups=mesh['expert'=16,'tensor'=2] {'tensor'}, dimensions={0}, use_global_device_ids=true | all-gather | bytes 884736 | tf_op jit(solution)/shard_map/all_gather | solution.py:517
  90.5 11.1 %attention_back.1 = (bf16[384,1664]{1,0:T(8,128)(2,1)}, bf16[384,1664]{1,0:T(8,128)(2,1)}, f32[192,768]{1,0:T(8,128)S(1)}, f32[192,768]{1,0:T(8,128)S(1)}) custom-call(s32[1]{0:T(128)} %bitcast.half_ref, s32[1]{0:T(128)} %bitcast.11.bit_ref, bf16[384,768]{1,0:T(8,128)(2,1)S(1)} %all_gather.7.grad_ref, bf16[384,768]{1,0:T(8,128)(2,1)S(1)} %copy-done.6, ...), custom_call_target="tpu_custom_call" | custom-call | tf_op jit(solution)/shard_map/attention_back/pallas_call | solution.py:524
  103.7 16.9 %collective-permute-done.3 = bf16[384,1664]{1,0:T(8,128)(2,1)S(1)} collective-permute-done((bf16[384,1664]{1,0:T(8,128)(2,1)}, bf16[384,1664]{1,0:T(8,128)(2,1)S(1)}, u32[]{:S(2)}, u32[]{:S(2)}) %collective-permute-start.3) | collective-permute-done | bytes 1277984 | tf_op jit(solution)/shard_map/ppermute | solution.py:553
  123.2 9.5 %collective-permute-done.4 = bf16[192,1664]{1,0:T(8,128)(2,1)S(1)} collective-permute-done((bf16[192,1664]{1,0:T(8,128)(2,1)S(1)}, bf16[192,1664]{1,0:T(8,128)(2,1)S(1)}, u32[]{:S(2)}, u32[]{:S(2)}) %collective-permute-start.4) | collective-permute-done | bytes 639008 | tf_op jit(solution)/shard_map/ppermute | solution.py:553
  134.1 6.8 %collective-permute-done.5 = bf16[96,1664]{1,0:T(8,128)(2,1)S(1)} collective-permute-done((bf16[96,1664]{1,0:T(8,128)(2,1)S(1)}, bf16[96,1664]{1,0:T(8,128)(2,1)S(1)}, u32[]{:S(2)}, u32[]{:S(2)}) %collective-permute-start.5) | collective-permute-done | bytes 319520 | tf_op jit(solution)/shard_map/ppermute | solution.py:553
  141.5 7.3 %collective-permute-done.6 = bf16[48,1664]{1,0:T(8,128)(2,1)S(1)} collective-permute-done((bf16[48,1664]{1,0:T(8,128)(2,1)S(1)}, bf16[48,1664]{1,0:T(8,128)(2,1)S(1)}, u32[]{:S(2)}, u32[]{:S(2)}) %collective-permute-start.6) | collective-permute-done | bytes 159776 | tf_op jit(solution)/shard_map/ppermute | solution.py:553
  149.0 8.0 %collective-permute-done.7 = bf16[48,1664]{1,0:T(8,128)(2,1)S(1)} collective-permute-done((bf16[48,1664]{1,0:T(8,128)(2,1)S(1)}, bf16[48,1664]{1,0:T(8,128)(2,1)S(1)}, u32[]{:S(2)}, u32[]{:S(2)}) %collective-permute-start.7) | collective-permute-done | bytes 159776 | tf_op jit(solution)/shard_map/ppermute | solution.py:553
  157.2 7.0 %collective-permute-done.8 = bf16[96,1664]{1,0:T(8,128)(2,1)S(1)} collective-permute-done((bf16[96,1664]{1,0:T(8,128)(2,1)S(1)}, bf16[96,1664]{1,0:T(8,128)(2,1)S(1)}, u32[]{:S(2)}, u32[]{:S(2)}) %collective-permute-start.8) | collective-permute-done | bytes 319520 | tf_op jit(solution)/shard_map/ppermute | solution.py:553
  166.1 9.8 %collective-permute-done.9 = bf16[192,1664]{1,0:T(8,128)(2,1)} collective-permute-done((bf16[192,1664]{1,0:T(8,128)(2,1)}, bf16[192,1664]{1,0:T(8,128)(2,1)}, u32[]{:S(2)}, u32[]{:S(2)}) %collective-permute-start.9) | collective-permute-done | bytes 639008 | tf_op jit(solution)/shard_map/ppermute | solution.py:553
  178.8 3.3 %collective-permute-start.10 = (bf16[384,1664]{1,0:T(8,128)(2,1)}, bf16[384,1664]{1,0:T(8,128)(2,1)}, u32[]{:S(2)}, u32[]{:S(2)}) collective-permute-start(bf16[384,1664]{1,0:T(8,128)(2,1)} %pad_maximum_fusion.own_ref), channel_id=1, source_target_pairs={{0,2},{1,5},{2,0},{3,7},{4,6},{5,1},{6,4},{7,3},{8,10},{9,13},{10,... | collective-permute-start | bytes 3833864 | tf_op jit(solution)/shard_map/ppermute | solution.py:553
  182.1 3.8 %all-to-all-start.2 = ((bf16[16,16,768]{2,1,0:T(8,128)(2,1)}), bf16[16,16,768]{2,1,0:T(8,128)(2,1)S(1)}, u32[]{:S(2)}, u32[]{:S(2)}) async-start(bf16[16,16,768]{2,1,0:T(8,128)(2,1)} %bitcast.24), calls=%async_computation.2 | async-start | bytes 786432 | tf_op jit(solution)/shard_map/all_to_all | solution.py:412
  186.1 14.3 %collective-permute-done.10.got_ref = bf16[384,1664]{1,0:T(8,128)(2,1)} collective-permute-done((bf16[384,1664]{1,0:T(8,128)(2,1)}, bf16[384,1664]{1,0:T(8,128)(2,1)}, u32[]{:S(2)}, u32[]{:S(2)}) %collective-permute-start.10) | collective-permute-done | bytes 1277984 | tf_op jit(solution)/shard_map/ppermute | solution.py:553
  206.2 2.5 %token_outputs.1 = (bf16[192,768]{1,0:T(8,128)(2,1)}, f32[192,768]{1,0:T(8,128)}) custom-call(bf16[192,256]{1,0:T(8,128)(2,1)S(1)} %copy-done.9, bf16[256,768]{1,0:T(8,128)(2,1)S(1)} %bitcast.22, f32[192,768]{1,0:T(8,128)S(1)} %copy-done.4, f32[192,768]{1,0:T(8,128)S(1)} %copy-done.19, f32[192,768]{1,0:T(8,128)} %collective-permute-done.2.got_ref, ...), custom_call_target="tpu_custom_call" | custom-call | tf_op jit(solution)/shard_map/token_outputs/pallas_call | solution.py:605
  208.8 5.2 %expert_grads.1 = (f32[1536,768]{1,0:T(8,128)}, f32[768,1536]{1,0:T(8,128)}) custom-call(bf16[256,1536]{1,0:T(8,128)(2,1)S(1)} %copy-done.13, bf16[256,1536]{1,0:T(8,128)(2,1)S(1)} %copy-done.15, bf16[256,768]{1,0:T(8,128)(2,1)S(1)} %bitcast.20, bf16[256,768]{1,0:T(8,128)(2,1)S(1)} %copy-done.23, ...), custom_call_target="tpu_custom_call" | custom-call | tf_op jit(solution)/shard_map/expert_grads/pallas_call | solution.py:616
  214.9 4.1 %unpack.1 = (f32[3,768,384]{2,1,0:T(8,128)}, f32[384,768]{1,0:T(8,128)}, f32[768,16]{1,0:T(8,128)S(1)}, f32[16,768]{1,0:T(8,128)S(1)}) custom-call(s32[1]{0:T(128)} %bitcast.11.bit_ref, bf16[384,1664]{1,0:T(8,128)(2,1)} %pad_maximum_fusion.own_ref, bf16[384,1664]{1,0:T(8,128)(2,1)} %collective-permute-done.10.got_ref, f32[768,128]{1,0:T(8,128)S(1)} %select_add_fusion.small_ref), custom_call_target="tpu_custom_call" | custom-call | tf_op jit(solution)/shard_map/unpack/pallas_call | solution.py:591
  (126 shorter events, 40.4 us)
Async XLA Ops:
  0.7 14.9 %copy-start = (bf16[3,768,384]{2,1,0:T(8,128)(2,1)S(1)}, bf16[3,768,384]{2,1,0:T(8,128)(2,1)}, u32[]{:S(2)}) copy-start(bf16[3,768,384]{2,1,0:T(8,128)(2,1)} %w_ref.3) | copy-start | bytes 5308420
  0.7 14.9 %copy-start.27 = (s32[1,3]{1,0:T(1,128)S(1)}, s32[1,3]{1,0:T(1,128)}, u32[]{:S(2)}) copy-start(s32[1,3]{1,0:T(1,128)} %lengths_ref.1) | copy-start | bytes 40
  4.8 27.0 %all-to-all-start.1 = ((bf16[16,16,768]{2,1,0:T(8,128)(2,1)}), bf16[16,16,768]{2,1,0:T(8,128)(2,1)S(1)}, u32[]{:S(2)}, u32[]{:S(2)}) async-start(bf16[16,16,768]{2,1,0:T(8,128)(2,1)} %bitcast.26), calls=%async_computation.1 | async-start | bytes 786432 | tf_op jit(solution)/shard_map/all_to_all | solution.py:412
  13.1 15.9 %collective-permute-start.1 = (bf16[384,768]{1,0:T(8,128)(2,1)}, bf16[384,768]{1,0:T(8,128)(2,1)}, u32[]{:S(2)}, u32[]{:S(2)}) collective-permute-start(bf16[384,768]{1,0:T(8,128)(2,1)} %w_out_ref.1), channel_id=1, source_target_pairs={{0,1},{1,0},{2,3},{3,2},{4,5},{5,4},{6,7},{7,6},{8,9},{9,8},{10,11... | collective-permute-start | bytes 1769480 | tf_op jit(solution)/shard_map/ppermute | solution.py:409
  15.6 13.4 %copy-start.5 = (bf16[384,768]{1,0:T(8,128)(2,1)S(1)}, bf16[384,768]{1,0:T(8,128)(2,1)}, u32[]{:S(2)}) copy-start(bf16[384,768]{1,0:T(8,128)(2,1)} %w_out_ref.1) | copy-start | bytes 1769476
  15.6 13.4 %copy-start.9 = (bf16[192,256]{1,0:T(8,128)(2,1)S(1)}, bf16[192,256]{1,0:T(8,128)(2,1)}, u32[]{:S(2)}) copy-start(bf16[192,256]{1,0:T(8,128)(2,1)} %get-tuple-element.42.place_ref) | copy-start | bytes 294916
  27.6 1.4 collective-permute-start
  31.8 52.9 %copy-start.3 = (f32[192,768]{1,0:T(8,128)}, f32[192,768]{1,0:T(8,128)S(1)}, u32[]{:S(2)}) copy-start(f32[192,768]{1,0:T(8,128)S(1)} %get-tuple-element.48.residual_ref) | copy-start | bytes 1769476
  31.8 20.0 %all-to-all-start = ((bf16[16,16,768]{2,1,0:T(8,128)(2,1)}), bf16[16,16,768]{2,1,0:T(8,128)(2,1)S(1)}, u32[]{:S(2)}, u32[]{:S(2)}) async-start(bf16[16,16,768]{2,1,0:T(8,128)(2,1)} %bitcast.3), calls=%async_computation | async-start | bytes 786432 | tf_op jit(solution)/shard_map/all_to_all | solution.py:412
  68.9 20.5 %copy-start.26 = (bf16[384,384]{1,0:T(8,128)(2,1)S(1)}, bf16[384,384]{1,0:T(8,128)(2,1)}, u32[]{:S(2)}) copy-start(bf16[384,384]{1,0:T(8,128)(2,1)} %copy-done.25) | copy-start | bytes 884740
  68.9 15.8 %all-to-all-start.3 = ((bf16[16,16,768]{2,1,0:T(8,128)(2,1)}), bf16[16,16,768]{2,1,0:T(8,128)(2,1)S(1)}, u32[]{:S(2)}, u32[]{:S(2)}) async-start(bf16[16,16,768]{2,1,0:T(8,128)(2,1)} %bitcast.12), calls=%async_computation.3 | async-start | bytes 786432 | tf_op jit(solution)/shard_map/all_to_all | solution.py:412
  72.7 16.7 %copy-start.6 = (bf16[384,768]{1,0:T(8,128)(2,1)S(1)}, bf16[384,768]{1,0:T(8,128)(2,1)}, u32[]{:S(2)}) copy-start(bf16[384,768]{1,0:T(8,128)(2,1)} %w_out_ref.1) | copy-start | bytes 1769476
  103.2 17.5 %collective-permute-start.3 = (bf16[384,1664]{1,0:T(8,128)(2,1)}, bf16[384,1664]{1,0:T(8,128)(2,1)S(1)}, u32[]{:S(2)}, u32[]{:S(2)}) collective-permute-start(bf16[384,1664]{1,0:T(8,128)(2,1)} %get-tuple-element.63), channel_id=1, source_target_pairs={{0,2},{1,5},{2,0},{3,7},{4,6},{5,1},{6,4},{7,3},{8,10},{9,13},{10,... | collective-permute-start | bytes 3833864 | tf_op jit(solution)/shard_map/ppermute | solution.py:553
  122.3 10.5 %collective-permute-start.4 = (bf16[192,1664]{1,0:T(8,128)(2,1)S(1)}, bf16[192,1664]{1,0:T(8,128)(2,1)S(1)}, u32[]{:S(2)}, u32[]{:S(2)}) collective-permute-start(bf16[192,1664]{1,0:T(8,128)(2,1)S(1)} %get-tuple-element.89), channel_id=1, source_target_pairs={{0,4},{1,3},{2,6},{3,1},{4,0},{5,7},{6,2},{7,5},{8,12},{9,11},{10,... | collective-permute-start | bytes 1916936 | tf_op jit(solution)/shard_map/ppermute | solution.py:553
  133.0 7.9 %collective-permute-start.5 = (bf16[96,1664]{1,0:T(8,128)(2,1)S(1)}, bf16[96,1664]{1,0:T(8,128)(2,1)S(1)}, u32[]{:S(2)}, u32[]{:S(2)}) collective-permute-start(bf16[96,1664]{1,0:T(8,128)(2,1)S(1)} %get-tuple-element.93), channel_id=1, source_target_pairs={{0,8},{1,9},{2,10},{3,11},{4,12},{5,13},{6,14},{7,15},{8,0},{9,1},... | collective-permute-start | bytes 958472 | tf_op jit(solution)/shard_map/ppermute | solution.py:553
  140.9 8.0 %collective-permute-start.6 = (bf16[48,1664]{1,0:T(8,128)(2,1)S(1)}, bf16[48,1664]{1,0:T(8,128)(2,1)S(1)}, u32[]{:S(2)}, u32[]{:S(2)}) collective-permute-start(bf16[48,1664]{1,0:T(8,128)(2,1)S(1)} %add_convert_fusion.5), channel_id=1, source_target_pairs={{0,16},{1,17},{2,18},{3,19},{4,20},{5,21},{6,22},{7,23},{8,24},{9,... | collective-permute-start | bytes 479240 | tf_op jit(solution)/shard_map/ppermute | solution.py:553
  149.0 8.1 %collective-permute-start.7 = (bf16[48,1664]{1,0:T(8,128)(2,1)S(1)}, bf16[48,1664]{1,0:T(8,128)(2,1)S(1)}, u32[]{:S(2)}, u32[]{:S(2)}) collective-permute-start(bf16[48,1664]{1,0:T(8,128)(2,1)S(1)} %add_convert_fusion.4), channel_id=1, source_target_pairs={{0,16},{1,17},{2,18},{3,19},{4,20},{5,21},{6,22},{7,23},{8,24},{9,... | collective-permute-start | bytes 479240 | tf_op jit(solution)/shard_map/ppermute | solution.py:553
  157.1 7.1 %collective-permute-start.8 = (bf16[96,1664]{1,0:T(8,128)(2,1)S(1)}, bf16[96,1664]{1,0:T(8,128)(2,1)S(1)}, u32[]{:S(2)}, u32[]{:S(2)}) collective-permute-start(bf16[96,1664]{1,0:T(8,128)(2,1)S(1)} %pad_maximum_fusion.3), channel_id=1, source_target_pairs={{0,8},{1,9},{2,10},{3,11},{4,12},{5,13},{6,14},{7,15},{8,0},{9,1},... | collective-permute-start | bytes 958472 | tf_op jit(solution)/shard_map/ppermute | solution.py:553
  165.2 10.7 %collective-permute-start.9 = (bf16[192,1664]{1,0:T(8,128)(2,1)}, bf16[192,1664]{1,0:T(8,128)(2,1)}, u32[]{:S(2)}, u32[]{:S(2)}) collective-permute-start(bf16[192,1664]{1,0:T(8,128)(2,1)} %pad_maximum_fusion.1), channel_id=1, source_target_pairs={{0,4},{1,3},{2,6},{3,1},{4,0},{5,7},{6,2},{7,5},{8,12},{9,11},{10,... | collective-permute-start | bytes 1916936 | tf_op jit(solution)/shard_map/ppermute | solution.py:553
  166.1 42.6 %collective-permute-start.12 = (bf16[256,4608]{1,0:T(8,128)(2,1)}, bf16[256,4608]{1,0:T(8,128)(2,1)S(1)}, u32[]{:S(2)}, u32[]{:S(2)}) collective-permute-start(bf16[256,4608]{1,0:T(8,128)(2,1)} %copy-done.28), channel_id=1, source_target_pairs={{0,1},{1,0},{2,3},{3,2},{4,5},{5,4},{6,7},{7,6},{8,9},{9,8},{10,11... | collective-permute-start | bytes 7077896 | tf_op jit(solution)/shard_map/ppermute | solution.py:409
  178.8 21.5 %collective-permute-start.10 = (bf16[384,1664]{1,0:T(8,128)(2,1)}, bf16[384,1664]{1,0:T(8,128)(2,1)}, u32[]{:S(2)}, u32[]{:S(2)}) collective-permute-start(bf16[384,1664]{1,0:T(8,128)(2,1)} %pad_maximum_fusion.own_ref), channel_id=1, source_target_pairs={{0,2},{1,5},{2,0},{3,7},{4,6},{5,1},{6,4},{7,3},{8,10},{9,13},{10,... | collective-permute-start | bytes 3833864 | tf_op jit(solution)/shard_map/ppermute | solution.py:553
  182.1 20.9 %all-to-all-start.2 = ((bf16[16,16,768]{2,1,0:T(8,128)(2,1)}), bf16[16,16,768]{2,1,0:T(8,128)(2,1)S(1)}, u32[]{:S(2)}, u32[]{:S(2)}) async-start(bf16[16,16,768]{2,1,0:T(8,128)(2,1)} %bitcast.24), calls=%async_computation.2 | async-start | bytes 786432 | tf_op jit(solution)/shard_map/all_to_all | solution.py:412
  186.0 17.1 %collective-permute-start.2 = (f32[192,768]{1,0:T(8,128)}, f32[192,768]{1,0:T(8,128)}, u32[]{:S(2)}, u32[]{:S(2)}) collective-permute-start(f32[192,768]{1,0:T(8,128)} %copy-done.29), channel_id=1, source_target_pairs={{0,1},{1,0},{2,3},{3,2},{4,5},{5,4},{6,7},{7,6},{8,9},{9,8},{10,11... | collective-permute-start | bytes 1769480 | tf_op jit(solution)/shard_map/ppermute | solution.py:409
  203.0 11.0 %collective-permute-start.11 = (bf16[768,128]{1,0:T(8,128)(2,1)}, bf16[768,128]{1,0:T(8,128)(2,1)}, u32[]{:S(2)}, u32[]{:S(2)}) collective-permute-start(bf16[768,128]{1,0:T(8,128)(2,1)} %fusion), channel_id=1, source_target_pairs={{0,1},{1,0},{2,3},{3,2},{4,5},{5,4},{6,7},{7,6},{8,9},{9,8},{10,11... | collective-permute-start | bytes 589832 | tf_op jit(solution)/shard_map/ppermute | solution.py:409
  (34 other events, 106.8 us)
where the time goes:
time: 222 us; the launch traced here: 221 us
  waiting for transfers between devices  106 us (48%)
  Pallas kernels  47 us (21%)
  starting transfers between devices  30.9 us (14%)
  local copies, waits for them, and re-layouts  22.4 us (10%)
  other arithmetic  9.35 us (4%)
  blocking collectives  4.74 us (2%)
    ppermute x8, waiting for transfers between devices, pair(): return lax.ppermute(value, ('expert', 'tensor'), moves)  79.6 us
    all_to_all x4, waiting for transfers between devices, exchange(): lax.all_to_all(value.reshape(experts, capacity, width), 'expert', split_a...  24.9 us
    all_to_all x4, starting transfers between devices, exchange(): lax.all_to_all(value.reshape(experts, capacity, width), 'expert', split_a...  22.7 us
    unnamed x85, local copies, waits for them, and re-layouts  21.2 us
    pallas_call x1, Pallas kernels, per_device(): pl.pallas_call(attend_back_body, out_shape=shape_of(((half_width, packed)...  11.1 us
    pallas_call x1, Pallas kernels, per_device(): pl.pallas_call(expert_body, grid_spec=pltpu.PrefetchScalarGridSpec(num_sc...  10.1 us
    pallas_call x1, Pallas kernels, per_device(): pl.pallas_call(attend_body, out_shape=shape_of(((rows, local), BF), ((row...  8.33 us
    ppermute x8, starting transfers between devices, pair(): return lax.ppermute(value, ('expert', 'tensor'), moves)  7.6 us
  transfers between devices with their start and end apart: 17, of which 11 were waited for; matrix products, arithmetic and copies ran while one was open for 2% of the time, Pallas kernels for 9%

commit v1 on v0

v1 whole, which is shorter than its diff:
```python
import functools

import jax
import jax.numpy as jnp
from jax import lax
from jax.experimental import pallas as pl
from jax.experimental.pallas import tpu as pltpu
from jax.sharding import PartitionSpec as P

HEAD = 64
TILE = 128
FF_TILE = 512

epsilon = 1e-06
THRESHOLDS = (1, 2, 3, 4, 5, 6, 7, 8, 12, 16, 23, 32, 46, 64, 91)
halfway = 16
BF = jnp.bfloat16
F32 = jnp.float32
HIGH = lax.Precision.HIGHEST
MIB = 1 << 20


def mm(a, b):
    return lax.dot_general(a, b, (((1,), (0,)), ((), ())), preferred_element_type=F32)


def mm_nt(a, b):
    return lax.dot_general(a, b, (((1,), (1,)), ((), ())), preferred_element_type=F32)


def mm_tn(a, b):
    return lax.dot_general(a, b, (((0,), (0,)), ((), ())), preferred_element_type=F32)


def iota(shape, dim):
    return lax.broadcasted_iota(jnp.int32, shape, dim)


def vmem_specs(count):
    return [pl.BlockSpec(memory_space=pltpu.VMEM)] * count


SMEM = pl.BlockSpec(memory_space=pltpu.SMEM)


def shape_of(*pairs):
    return tuple(jax.ShapeDtypeStruct(shape, dtype) for shape, dtype in pairs)


ANY = pl.BlockSpec(memory_space=pl.ANY)


def params(mib):
    return pltpu.CompilerParams(vmem_limit_bytes=mib * MIB)


def hbm(shape, dtype):
    return pltpu.HBM(shape, dtype)


def in_hbm(value):
    return pltpu.with_memory_space_constraint(value, pltpu.HBM)


def fetch(sources, targets, sems):
    copies = []
    for number, (source, target) in enumerate(zip(sources, targets, strict=True)):
        copies.append(pltpu.make_async_copy(source, target, sems.at[number]))
        copies[-1].start()
    return copies


def cost(flops, loaded):
    return pl.CostEstimate(flops=int(flops), bytes_accessed=int(loaded), transcendentals=0)


def bucket_of(distance):
    magnitude = jnp.abs(distance)
    bucket = jnp.zeros(distance.shape, jnp.int32)
    for border in THRESHOLDS:
        bucket = bucket + (magnitude >= border).astype(jnp.int32)
    return bucket + jnp.where(distance > 0, halfway, 0).astype(jnp.int32)


def distance_hot(buckets, delta):
    distance = iota((buckets, 2 * TILE), 1) + (TILE * delta - (TILE - 1))
    return bucket_of(distance) == iota((buckets, 2 * TILE), 0)


def prep_body(capacity, experts, routes_ref, cot_ref, place_out, out_ref, place_ref, sem):
    rows = cot_ref.shape[0]
    chosen = routes_ref[...]
    hot = chosen == iota((experts, rows), 0)
    above = (iota((rows, rows), 0) < iota((rows, rows), 1)).astype(F32).astype(BF)
    earlier = mm(hot.astype(F32).astype(BF), above)
    ordinal = jnp.sum(jnp.where(hot, earlier, 0.0), axis=0, keepdims=True)
    slot = chosen * capacity + ordinal.astype(jnp.int32)
    place = (slot == iota((experts * capacity, rows), 0)).astype(F32).astype(BF)
    place_ref[...] = place
    store = pltpu.make_async_copy(place_ref, place_out, sem)
    store.start()
    out_ref[...] = mm(place, cot_ref[...]).astype(BF)
    store.wait()


def attend_body(
    half_ref, lengths_ref, x_ref, x_other_ref, gain_ref, w_ref, bias_ref,
    own_ref, other_ref, context_out, qkv_out, probs_out, normed_out,
    w_vmem, context_ref, qkv_ref, probs_ref, normed_ref, load_sems, store_sems,
):
    loads = fetch([w_ref.at[c] for c in range(3)], [w_vmem.at[c] for c in range(3)], load_sems)
    stores = []

    def store(source, target):
        stores.append(pltpu.make_async_copy(source, target, store_sems.at[len(stores)]))
        stores[-1].start()

    group = normed_ref.shape[0]
    rows = own_ref.shape[0]
    local = w_ref.shape[2]
    heads = local // HEAD
    blocks = group // TILE
    own_at = pl.multiple_of(half_ref[0] * rows, rows)
    other_at = pl.multiple_of((1 - half_ref[0]) * rows, rows)
    for ref, at in ((x_ref, own_at), (x_other_ref, other_at)):
        x = ref[...].astype(F32)
        factor = lax.rsqrt(jnp.mean(x * x, axis=-1, keepdims=True) + epsilon)
        normed_ref[pl.ds(at, rows), :] = (x * factor * gain_ref[...].astype(F32)).astype(BF)
    normed = normed_ref[...]
    store(normed_ref, normed_out)
    for c in range(3):
        loads[c].wait()
        qkv_ref[:, c * local : (c + 1) * local] = mm(normed, w_vmem[c]).astype(BF)
    store(qkv_ref, qkv_out)
    buckets = bias_ref.shape[1]
    tables = [
        mm(bias_ref[...], distance_hot(buckets, delta).astype(F32).astype(BF))
        for delta in range(1 - blocks, blocks)
    ]
    segment_rows = jnp.zeros((group, 1), jnp.int32)
    segment_lanes = jnp.zeros((1, group), jnp.int32)
    border = jnp.int32(0)
    for s in range(lengths_ref.shape[1]):
        border = border + lengths_ref[0, s]
        segment_rows = segment_rows + (iota((group, 1), 0) >= border).astype(jnp.int32)
        segment_lanes = segment_lanes + (iota((1, group), 1) >= border).astype(jnp.int32)
    for h in range(heads):
        lo = h * HEAD
        keys = qkv_ref[:, local + lo : local + lo + HEAD]
        values = qkv_ref[:, 2 * local + lo : 2 * local + lo + HEAD]
        bands = []
        for number, delta in enumerate(range(1 - blocks, blocks)):
            row = tables[number][h : h + 1, :]
            if abs(delta) > 1:
                bands.append(jnp.broadcast_to(row[:, :1], (TILE, TILE)))
            else:
                wide = jnp.broadcast_to(row, (TILE, 2 * TILE))
                band = pltpu.roll(wide, TILE + 1, 1, stride=1, stride_axis=0)
                bands.append(band[:, :TILE])
        for b in range(blocks):
            at = slice(b * TILE, (b + 1) * TILE)
            queries = qkv_ref[at, lo : lo + HEAD]
            scores = mm_nt(queries, keys) * (HEAD**-0.5)
            scores = scores + jnp.concatenate(
                [bands[k - b + blocks - 1] for k in range(blocks)], axis=1
            )
            scores = jnp.where(segment_rows[at] == segment_lanes, scores, -1e30)
            exponent = jnp.exp(scores - jnp.max(scores, axis=-1, keepdims=True))
            probs = exponent * (1.0 / jnp.sum(exponent, axis=-1, keepdims=True))
            low = probs.astype(BF)
            probs_ref[h, at, :] = low
            context_ref[at, lo : lo + HEAD] = mm(low, values).astype(BF)
        store(probs_ref.at[h], probs_out.at[h])
    store(context_ref, context_out)
    own_ref[...] = context_ref[pl.ds(own_at, rows), :]
    other_ref[...] = context_ref[pl.ds(other_at, rows), :]
    for copy in stores:
        copy.wait()


def project_body(
    own_ref, other_ref, w_other_ref, w_own_hbm, x_hbm, gain_ref, place_hbm, out_ref, residual_out,
    w_own_ref, x_ref, place_ref, residual_ref, sems,
):
    loads = fetch([w_own_hbm, x_hbm, place_hbm], [w_own_ref, x_ref, place_ref], sems)
    attended = mm(other_ref[...], w_other_ref[...])
    loads[0].wait()
    attended = attended + mm(own_ref[...], w_own_ref[...])
    loads[1].wait()
    residual = x_ref[...].astype(F32) + attended
    residual_ref[...] = residual
    store = pltpu.make_async_copy(residual_ref, residual_out, sems.at[3])
    store.start()
    factor = lax.rsqrt(jnp.mean(residual * residual, axis=-1, keepdims=True) + epsilon)
    moe_rows = (residual * factor * gain_ref[...].astype(F32)).astype(BF)
    loads[2].wait()
    out_ref[...] = mm(place_ref[...], moe_rows).astype(BF)
    store.wait()


def expert_body(
    half_ref, expert_ref, rows_ref, cot_ref, router_ref, up_ref, down_ref,
    back_ref, router_grad_ref, scaled_out, gp_out, send_out, act_out, pre_out,
    up_vmem, down_vmem, scaled_ref, gp_ref, send_ref, act_ref, pre_ref, out_acc, back_acc, load_sems, store_sems,
):
    steps, _, tile = up_vmem.shape
    half_steps = steps // 2
    width = rows_ref.shape[1]
    ff_half = act_ref.shape[1]
    loads = []
    for step in range(steps):
        side = 1 - half_ref[0] if step < half_steps else half_ref[0]
        at = pl.multiple_of((side * half_steps + step % half_steps) * tile, tile)
        loads.append(
            fetch(
                [up_ref.at[:, pl.ds(at, tile)], down_ref.at[pl.ds(at, tile), :]],
                [up_vmem.at[step], down_vmem.at[step]],
                load_sems.at[step],
            )
        )
    stores = []

    def store(source, target):
        stores.append(pltpu.make_async_copy(source, target, store_sems.at[len(stores)]))
        stores[-1].start()

    rows = rows_ref[...]
    logits = mm(rows, router_ref[...])
    exponent = jnp.exp(logits - jnp.max(logits, axis=-1, keepdims=True))
    chances = exponent / jnp.sum(exponent, axis=-1, keepdims=True)
    mine = iota(chances.shape, 1) == expert_ref[0]
    gating = jnp.sum(jnp.where(mine, chances, 0.0), axis=-1, keepdims=True)
    gp = (gating * cot_ref[...].astype(F32)).astype(BF)
    gp_ref[...] = gp
    store(gp_ref, gp_out)
    send_ref[:, 2 * ff_half : 2 * ff_half + width] = rows
    send_ref[:, 2 * ff_half + width :] = gp
    for step in range(steps):
        for copy in loads[step]:
            copy.wait()
        hidden = mm(rows, up_vmem[step])
        phi = 0.5 * (1.0 + lax.erf(hidden * (2.0**-0.5)))
        act = (hidden * phi).astype(BF)
        slope = phi + hidden * (jnp.exp(-0.5 * hidden * hidden) * 0.3989422804014327)
        pre = (mm_nt(gp, down_vmem[step]) * slope).astype(BF)
        if step == 0:
            out_acc[...] = mm(act, down_vmem[step])
            back_acc[...] = mm_nt(pre, up_vmem[step])
        else:
            out_acc[...] += mm(act, down_vmem[step])
            back_acc[...] += mm_nt(pre, up_vmem[step])
        if step < half_steps:
            send_ref[:, step * tile : (step + 1) * tile] = act
            send_ref[:, ff_half + step * tile : ff_half + (step + 1) * tile] = pre
        else:
            at = (step - half_steps) * tile
            act_ref[:, at : at + tile] = act
            pre_ref[:, at : at + tile] = pre
        if step == half_steps - 1:
            store(send_ref, send_out)
    store(act_ref, act_out)
    store(pre_ref, pre_out)
    produced = out_acc[...].astype(BF).astype(F32)
    scaled_ref[...] = (gating * produced).astype(BF)
    store(scaled_ref, scaled_out)
    grad_gate = jnp.sum(cot_ref[...].astype(F32) * produced, axis=-1, keepdims=True)
    grad_logits = gating * (mine.astype(F32) - chances) * grad_gate
    low = grad_logits.astype(BF)
    rest = (grad_logits - low.astype(F32)).astype(BF)
    back = back_acc[...] + (mm_nt(low, router_ref[...]) + mm_nt(rest, router_ref[...]))
    back_ref[...] = back.astype(BF)
    router_grad_ref[...] = mm_tn(low, rows) + mm_tn(rest, rows)
    for copy in stores:
        copy.wait()


def expert_grads_body(
    act_ref, pre_ref, rows_ref, gp_ref, act2_ref, pre2_ref, rows2_ref, gp2_ref, down_ref, up_ref
):
    down_ref[...] = mm_tn(act_ref[...], gp_ref[...]) + mm_tn(act2_ref[...], gp2_ref[...])
    up_ref[...] = mm_tn(rows_ref[...], pre_ref[...]) + mm_tn(rows2_ref[...], pre2_ref[...])


def norm_back(grad, source, gain):
    factor = lax.rsqrt(jnp.mean(source * source, axis=-1, keepdims=True) + epsilon)
    unit = source * factor
    scaled = grad * gain
    inner = jnp.mean(scaled * unit, axis=-1, keepdims=True)
    return factor * (scaled - unit * inner), grad * unit


def moe_back_body(
    place_hbm, back_ref, residual_hbm, gain_ref, cot_hbm, _scaled, _after,
    low_ref, gain_grad_ref, grad_out, _passed,
    place_ref, residual_ref, cot_ref, grad_ref, sems,
):
    loads = fetch([place_hbm, residual_hbm, cot_hbm], [place_ref, residual_ref, cot_ref], sems)
    loads[0].wait()
    grad_in = mm_tn(place_ref[...], back_ref[...])
    loads[1].wait()
    passed, terms = norm_back(grad_in, residual_ref[...], gain_ref[...].astype(F32))
    loads[2].wait()
    grad = cot_ref[...].astype(F32) + passed
    grad_ref[...] = grad
    store = pltpu.make_async_copy(grad_ref, grad_out, sems.at[3])
    store.start()
    low_ref[...] = grad.astype(BF)
    gain_grad_ref[...] = jnp.sum(terms, axis=0, keepdims=True)
    store.wait()


def fold_diagonals(square):
    wide = jnp.concatenate([square, jnp.zeros_like(square)], axis=1)
    count = TILE
    while count > 8:
        count //= 2
        wide = wide[:count] + pltpu.roll(wide[count:], 2 * TILE - count, 1)
    total = wide[:1]
    for i in range(1, 8):
        total = total + pltpu.roll(wide[i : i + 1], 2 * TILE - i, 1)
    return total


def attend_back_body(
    half_ref, bits_ref, grad_own_ref, grad_other_ref, w_out_hbm, qkv_hbm, probs_hbm, context_hbm, normed_hbm, w_hbm,
    x_hbm, x_other_hbm, router_grad_ref, moe_gain_grad_ref,
    a0_out, a1_out, a2_out, a3_out, c0_out, c1_out, c2_out, c3_out, small_out, own_out, other_out,
    a0_ref, a1_ref, a2_ref, a3_ref, c0_ref, c1_ref, c2_ref, c3_ref, small_ref, own_ref, other_ref,
    gqkv_ref, all_ref, gctx_ref, grad_ref,
    w_out_ref, qkv_ref, probs_ref, context_ref, normed_ref, w_ref, x_ref, x_other_ref, sems, store_sems,
):
    heads = probs_ref.shape[0]
    w_out_in, qkv_in, *probs_in = fetch(
        [w_out_hbm, qkv_hbm] + [probs_hbm.at[h] for h in range(heads)],
        [w_out_ref, qkv_ref] + [probs_ref.at[h] for h in range(heads)],
        sems,
    )
    context_in, *rest = fetch(
        [context_hbm, w_hbm, x_hbm, x_other_hbm, normed_hbm],
        [context_ref, w_ref, x_ref, x_other_ref, normed_ref],
        sems.at[pl.ds(2 + heads, 5)],
    )
    stores = []

    def store(source, target):
        stores.append(pltpu.make_async_copy(source, target, store_sems.at[len(stores)]))
        stores[-1].start()

    group, width = normed_ref.shape
    rows = own_ref.shape[0]
    local = w_ref.shape[2]
    heads = local // HEAD
    blocks = group // TILE
    own_at = pl.multiple_of(half_ref[0] * rows, rows)
    other_at = pl.multiple_of((1 - half_ref[0]) * rows, rows)
    grad_ref[pl.ds(own_at, rows), :] = grad_own_ref[...]
    grad_ref[pl.ds(other_at, rows), :] = grad_other_ref[...]
    grad = grad_ref[...]
    w_out_in.wait()
    gctx_ref[...] = mm_nt(grad, w_out_ref[...]).astype(BF)
    qkv_in.wait()
    heads_distance = []
    scale = HEAD**-0.5
    buckets = 2 * halfway
    table = jnp.zeros((8, buckets), F32)
    per_distance = [[] for _ in range(3)]
    edges = [[], []]
    for h in range(heads):
        lo = h * HEAD
        queries = qkv_ref[:, lo : lo + HEAD]
        keys = qkv_ref[:, local + lo : local + lo + HEAD]
        values = qkv_ref[:, 2 * local + lo : 2 * local + lo + HEAD]
        gctx = gctx_ref[:, lo : lo + HEAD]
        probs_in[h].wait()
        low_probs = probs_ref[h]
        grad_probs = mm_nt(gctx, values)
        probs = low_probs.astype(F32)
        inner = jnp.sum(probs * grad_probs, axis=-1, keepdims=True)
        grad_scores = probs * (grad_probs - inner)
        low = grad_scores.astype(BF)
        gqkv_ref[:, lo : lo + HEAD] = (mm(low, keys) * scale).astype(BF)
        gqkv_ref[:, local + lo : local + lo + HEAD] = (mm_tn(low, queries) * scale).astype(BF)
        gqkv_ref[:, 2 * local + lo : 2 * local + lo + HEAD] = mm_tn(low_probs, gctx).astype(BF)
        for number, delta in enumerate((-1, 0, 1)):
            band = None
            for b in range(blocks):
                k = b + delta
                if 0 <= k < blocks:
                    piece = grad_scores[
                        b * TILE : (b + 1) * TILE, k * TILE : (k + 1) * TILE
                    ]
                    band = piece if band is None else band + piece
            per_distance[number].append(fold_diagonals(band))
        for number, sign in enumerate((-1, 1)):
            total = jnp.zeros((1, 1), F32)
            for b in range(blocks):
                for k in range(blocks):
                    if (k - b) * sign > 1:
                        piece = grad_scores[
                            b * TILE : (b + 1) * TILE, k * TILE : (k + 1) * TILE
                        ]
                        total = total + jnp.sum(
                            jnp.sum(piece, axis=0, keepdims=True), axis=1, keepdims=True
                        )
            edges[number].append(total)
    plane, depth = bits_ref[0], bits_ref[1]
    shard = width // 16
    half = width // 2
    targets = (c0_ref, c1_ref, c2_ref, c3_ref)
    context_in.wait()
    for a in range(2):
        block = mm_tn(context_ref[...], grad_ref[:, a * half : (a + 1) * half]).astype(BF)
        for z in range(2):
            for number, target in enumerate(targets):

                @pl.when((depth ^ (2 * a + z)) == number)
                def _(target=target, block=block, z=z):
                    for p in range(4):
                        piece = block[(z * 4 + p) * shard : (z * 4 + p + 1) * shard]
                        at = pl.multiple_of((plane ^ p) * shard, shard)
                        target[pl.ds(at, shard), :] = piece
    for target, out in zip(targets, (c0_out, c1_out, c2_out, c3_out)):
        store(target, out)
    pad = [jnp.zeros((8 - heads, 2 * TILE), F32)]
    for number, delta in enumerate((-1, 0, 1)):
        sums = jnp.concatenate(per_distance[number] + pad, axis=0)
        distance = iota((buckets, 2 * TILE), 1)
        distance = jnp.where(distance >= TILE, distance - 2 * TILE, distance) + TILE * delta
        hot = (bucket_of(distance) == iota((buckets, 2 * TILE), 0)).astype(F32)
        table = table + lax.dot_general(
            sums, hot, (((1,), (1,)), ((), ())), precision=HIGH, preferred_element_type=F32
        )
    for number, bucket in enumerate((halfway - 1, 2 * halfway - 1)):
        column = jnp.concatenate(edges[number] + [jnp.zeros((8 - heads, 1), F32)], axis=0)
        table = table + jnp.where(iota((8, buckets), 1) == bucket, column, 0.0)
    for copy in rest:
        copy.wait()
    total = None
    for c in range(3):
        part = mm_nt(gqkv_ref[:, c * local : (c + 1) * local], w_ref[c])
        total = part if total is None else total + part
    all_ref[...] = total
    own_ref[...] = all_ref[pl.ds(own_at, rows), :]
    other_ref[...] = all_ref[pl.ds(other_at, rows), :]
    store(own_ref, own_out)
    store(other_ref, other_out)
    gain_grad = jnp.zeros((1, width), F32)
    for ref, part in ((x_ref, own_ref), (x_other_ref, other_ref)):
        x = ref[...].astype(F32)
        factor = lax.rsqrt(jnp.mean(x * x, axis=-1, keepdims=True) + epsilon)
        gain_grad = gain_grad + jnp.sum(part[...] * (x * factor), axis=0, keepdims=True)
    targets = (a0_ref, a1_ref, a2_ref, a3_ref)
    for a in range(2):
        block = mm_tn(normed_ref[:, a * half : (a + 1) * half], gqkv_ref[...]).astype(BF)
        for p in range(2):
            for number, target in enumerate(targets):

                @pl.when((plane ^ (2 * a + p)) == number)
                def _(target=target, block=block, p=p):
                    for z in range(4):
                        piece = block[(p * 4 + z) * shard : (p * 4 + z + 1) * shard]
                        at = pl.multiple_of((depth ^ z) * shard, shard)
                        target[pl.ds(at, shard), :] = piece
    for target, out in zip(targets, (a0_out, a1_out, a2_out, a3_out)):
        store(target, out)
    moe_gain_grad = moe_gain_grad_ref[...]
    row = iota((16, local), 0)
    extra = jnp.concatenate([table, jnp.zeros((8, local - buckets), F32)], axis=1)
    extra = jnp.concatenate([jnp.zeros((8, local), F32), extra], axis=0)
    for number, value in enumerate((moe_gain_grad, gain_grad)):
        for part in range(2):
            piece = value[:, part * local : (part + 1) * local]
            extra = extra + jnp.where(row == 2 * number + part, piece, 0.0)
    small = jnp.concatenate(
        [router_grad_ref[:, :local], router_grad_ref[:, local:], extra], axis=0
    ).astype(BF)
    small_ref[...] = small
    store(small_ref, small_out)
    for copy in stores:
        copy.wait()


def order_body(_value, _after, _out):
    pass


def total_of(*values):
    return functools.reduce(jnp.add, [v.astype(F32) for v in values]).astype(BF)


def pairs_of(a, b, c, d):
    return ((a.astype(F32) + b.astype(F32)) + (c.astype(F32) + d.astype(F32))).astype(BF)


def fold_first_body(
    a1_ref, a2_ref, a3_ref, c1_ref, c2_ref, c3_ref, a0_hbm, c0_hbm, small_hbm,
    s0_ref, s1_ref, s2_ref, s3_ref, e0_ref, e1_ref, e2_ref, e3_ref,
    a0_ref, c0_ref, small_ref, sems,
):
    for copy in fetch([a0_hbm, c0_hbm, small_hbm], [a0_ref, c0_ref, small_ref], sems):
        copy.wait()
    shard, lead = s0_ref.shape[0], small_ref.shape[0]
    for d, target in enumerate((s0_ref, s1_ref, s2_ref, s3_ref)):
        at = slice(d * shard, (d + 1) * shard)
        target[...] = pairs_of(a0_ref[at], a1_ref[at], a2_ref[at], a3_ref[at])
    for d, target in enumerate((e0_ref, e1_ref, e2_ref, e3_ref)):
        at = slice(d * shard, (d + 1) * shard)
        target[:lead] = small_ref[...]
        target[lead:] = pairs_of(c0_ref[at], c1_ref[at], c2_ref[at], c3_ref[at])


def fold_last_body(
    s0_ref, s1_ref, s2_ref, s3_ref, e0_ref, e1_ref, e2_ref, e3_ref, _after, total_ref, c_ref, small_ref
):
    lead = small_ref.shape[0]
    total_ref[...] = pairs_of(s0_ref[...], s1_ref[...], s2_ref[...], s3_ref[...])
    small_ref[...] = pairs_of(e0_ref[:lead], e1_ref[:lead], e2_ref[:lead], e3_ref[:lead])
    c_ref[...] = pairs_of(e0_ref[lead:], e1_ref[lead:], e2_ref[lead:], e3_ref[lead:])


def join_body(shared, *refs):
    total_refs, c_refs = refs[:4], refs[4:8]
    small_ref, other_ref, mine_ref, c_mine_ref = refs[8:]
    shard = c_refs[0].shape[0]
    for d in range(4):
        mine_ref[d * shard : (d + 1) * shard] = total_refs[d][...]
        c_mine_ref[d * shard : (d + 1) * shard] = c_refs[d][...]
    own = small_ref[...].astype(F32)
    both = own + other_ref[...].astype(F32)
    c_mine_ref[4 * shard :] = jnp.where(iota(own.shape, 0) < shared, both, own).astype(BF)


def tokens_body(
    place_ref, scaled_ref, residual_ref, own_ref, got_ref, x_ref, gain_ref, grad_res_ref, _after, out_ref, grad_ref
):
    out_ref[...] = (residual_ref[...] + mm_tn(place_ref[...], scaled_ref[...])).astype(BF)
    passed, _ = norm_back(
        own_ref[...] + got_ref[...], x_ref[...].astype(F32), gain_ref[...].astype(F32)
    )
    grad_ref[...] = grad_res_ref[...] + passed


def unpack_body(
    bits_ref, a0_ref, a1_ref, a2_ref, a3_ref, c0_ref, c1_ref, c2_ref, c3_ref,
    router_ref, norm_gain_ref, moe_gain_ref, bias_ref, qkv_out, w_out_out,
    wide_ref, w_out_ref, qkv_sems, out_sems,
):
    local = qkv_out.shape[2]
    shard = a0_ref.shape[0] // 4
    plane, depth = bits_ref[0], bits_ref[1]
    copies = []
    for number, ref in enumerate((a0_ref, a1_ref, a2_ref, a3_ref)):
        quarter = plane ^ number
        wide_ref[number] = ref[...].astype(F32)
        for d in range(4):
            at = pl.multiple_of((quarter * 4 + (depth ^ d)) * shard, shard)
            for c in range(3):
                copy = pltpu.make_async_copy(
                    wide_ref.at[number, pl.ds(d * shard, shard), pl.ds(c * local, local)],
                    qkv_out.at[c, pl.ds(at, shard), :],
                    qkv_sems.at[number, d, c],
                )
                copy.start()
                copies.append(copy)
    others = (c0_ref, c1_ref, c2_ref, c3_ref)
    for number, ref in enumerate(others):
        w_out_ref[number] = ref[: 4 * shard].astype(F32)
        slab = depth ^ number
        lane = pl.multiple_of((slab // 2) * local, local)
        for b in range(4):
            place = (slab % 2) * 4 + (plane ^ b)
            at = pl.multiple_of(place * shard, shard)
            copy = pltpu.make_async_copy(
                w_out_ref.at[number, pl.ds(b * shard, shard), :],
                w_out_out.at[pl.ds(at, shard), pl.ds(lane, local)],
                out_sems.at[number, b],
            )
            copy.start()
            copies.append(copy)
    parts = [ref[4 * shard :].astype(F32) for ref in others]
    small = (parts[0] + parts[1]) + (parts[2] + parts[3])
    experts = router_ref.shape[0]
    router_ref[:, :local] = small[:experts]
    router_ref[:, local:] = small[experts : 2 * experts]
    rest = small[2 * experts :]
    for number, ref in enumerate((moe_gain_ref, norm_gain_ref)):
        ref[:, :local] = rest[2 * number : 2 * number + 1]
        ref[:, local:] = rest[2 * number + 1 : 2 * number + 2]
    bias_ref[...] = rest[8 : 8 + bias_ref.shape[0], : bias_ref.shape[1]]
    for copy in copies:
        copy.wait()


def per_device(
    tokens, lengths, routes, norm_gain, w_qkv, rel_bias, w_out, moe_gain, w_router, w_in, w_down, cotangent
):
    rows, width = tokens.shape
    sources = lax.axis_size("expert")
    group = rows * lax.axis_size("tensor")
    experts = w_router.shape[1]
    capacity = max(2, 4 * rows // (3 * experts))
    slots = experts * capacity
    local = w_qkv.shape[2]
    heads = local // HEAD
    buckets = rel_bias.shape[0]
    ff = w_in.shape[2]
    ff_half = ff // 2
    half = lax.axis_index("tensor").astype(jnp.int32)
    expert = lax.axis_index("expert").astype(jnp.int32)
    half_one = half.reshape(1)
    gain_a = norm_gain.reshape(1, width)
    gain_b = moe_gain.reshape(1, width)

    def swap(value):
        return lax.ppermute(value, "tensor", [(0, 1), (1, 0)])

    def exchange(value):
        return lax.all_to_all(
            value.reshape(experts, capacity, width), "expert", split_axis=0, concat_axis=0, tiled=True
        ).reshape(slots, width)

    x_other = swap(tokens)
    w_out_other = swap(w_out)
    place, cot_slots = pl.pallas_call(
        functools.partial(prep_body, capacity, experts),
        out_shape=(hbm((slots, rows), BF),) + shape_of(((slots, width), BF)),
        in_specs=vmem_specs(2),
        out_specs=[ANY] + vmem_specs(1),
        scratch_shapes=[pltpu.VMEM((slots, rows), BF), pltpu.SemaphoreType.DMA],
        cost_estimate=cost(2e9, 1e6),
        name="place_cotangent",
    )(routes.reshape(1, rows), cotangent)
    cot_rows = exchange(cot_slots)

    bias_rows = jnp.pad(rel_bias.T, ((0, 8 - heads), (0, 0)))
    own_ctx, other_ctx, context, qkv, probs, normed = pl.pallas_call(
        attend_body,
        out_shape=shape_of(((rows, local), BF), ((rows, local), BF))
        + (
            hbm((group, local), BF),
            hbm((group, 3 * local), BF),
            hbm((heads, group, group), BF),
            hbm((group, width), BF),
        ),
        in_specs=[SMEM, SMEM] + vmem_specs(3) + [ANY] + vmem_specs(1),
        out_specs=vmem_specs(2) + [ANY] * 4,
        scratch_shapes=[
            pltpu.VMEM((3, width, local), BF),
            pltpu.VMEM((group, local), BF),
            pltpu.VMEM((group, 3 * local), BF),
            pltpu.VMEM((heads, group, group), BF),
            pltpu.VMEM((group, width), BF),
            pltpu.SemaphoreType.DMA((3,)),
            pltpu.SemaphoreType.DMA((heads + 3,)),
        ],
        compiler_params=params(20),
        cost_estimate=cost(8e9, 4e6),
        name="attention",
    )(half_one, lengths, tokens, x_other, gain_a, in_hbm(w_qkv), bias_rows)
    got_ctx = swap(other_ctx)

    moe_slots, residual = pl.pallas_call(
        project_body,
        out_shape=shape_of(((slots, width), BF)) + (hbm((rows, width), F32),),
        in_specs=vmem_specs(3) + [ANY] * 2 + vmem_specs(1) + [ANY],
        out_specs=vmem_specs(1) + [ANY],
        scratch_shapes=[
            pltpu.VMEM((local, width), BF),
            pltpu.VMEM((rows, width), BF),
            pltpu.VMEM((slots, rows), BF),
            pltpu.VMEM((rows, width), F32),
            pltpu.SemaphoreType.DMA((4,)),
        ],
        compiler_params=params(12),
        cost_estimate=cost(2e9, 2e6),
        name="projection",
    )(own_ctx, got_ctx, w_out_other, in_hbm(w_out), in_hbm(tokens), gain_b, in_hbm(place))
    stacked = exchange(moe_slots)

    count = sources * capacity
    tile = FF_TILE
    steps = ff // tile
    half_steps = steps // 2

    back, router_grad, scaled, gp, send, act, pre = pl.pallas_call(
        expert_body,
        out_shape=shape_of(((count, width), BF), ((experts, width), F32))
        + (
            hbm((count, width), BF),
            hbm((count, width), BF),
            hbm((count, 2 * ff_half + 2 * width), BF),
            hbm((count, ff_half), BF),
            hbm((count, ff_half), BF),
        ),
        in_specs=[SMEM, SMEM] + vmem_specs(3) + [ANY, ANY],
        out_specs=vmem_specs(2) + [ANY] * 5,
        scratch_shapes=[
            pltpu.VMEM((steps, width, tile), BF),
            pltpu.VMEM((steps, tile, width), BF),
            pltpu.VMEM((count, width), BF),
            pltpu.VMEM((count, width), BF),
            pltpu.VMEM((count, 2 * ff_half + 2 * width), BF),
            pltpu.VMEM((count, ff_half), BF),
            pltpu.VMEM((count, ff_half), BF),
            pltpu.VMEM((count, width), F32),
            pltpu.VMEM((count, width), F32),
            pltpu.SemaphoreType.DMA((steps, 2)),
            pltpu.SemaphoreType.DMA((5,)),
        ],
        compiler_params=params(32),
        cost_estimate=cost(10e9, 14e6),
        name="expert",
    )(half_one, expert.reshape(1), stacked, cot_rows, w_router, in_hbm(w_in[0]), in_hbm(w_down[0]))
    back_rows = exchange(back)
    peer = swap(send)

    col = lambda first: pl.BlockSpec((count, tile), lambda i: (0, first + i))
    fixed = lambda block: pl.BlockSpec((count, width), lambda i: (0, block))
    grad_down, grad_up = pl.pallas_call(
        expert_grads_body,
        grid=(half_steps,),
        in_specs=[
            col(0), col(0), fixed(0), fixed(0),
            col(0), col(half_steps), fixed(2 * ff_half // width), fixed(2 * ff_half // width + 1),
        ],
        out_specs=[
            pl.BlockSpec((tile, width), lambda i: (i, 0)),
            pl.BlockSpec((width, tile), lambda i: (0, i)),
        ],
        out_shape=shape_of(((ff_half, width), F32), ((width, ff_half), F32)),
        compiler_params=params(20),
        cost_estimate=cost(5e9, 14e6),
        name="expert_grads",
    )(in_hbm(act), in_hbm(pre), stacked, in_hbm(gp), *[in_hbm(peer)] * 4)

    grad_low, moe_gain_grad, grad_res, scaled_late = pl.pallas_call(
        moe_back_body,
        out_shape=shape_of(((rows, width), BF), ((1, width), F32))
        + (hbm((rows, width), F32), hbm((count, width), BF)),
        in_specs=[ANY] + vmem_specs(1) + [ANY] + vmem_specs(1) + [ANY] * 3,
        out_specs=vmem_specs(2) + [ANY, ANY],
        input_output_aliases={5: 3},
        scratch_shapes=[
            pltpu.VMEM((slots, rows), BF),
            pltpu.VMEM((rows, width), F32),
            pltpu.VMEM((rows, width), BF),
            pltpu.VMEM((rows, width), F32),
            pltpu.SemaphoreType.DMA((4,)),
        ],
        compiler_params=params(12),
        cost_estimate=cost(1e9, 2e6),
        name="norm_back",
    )(in_hbm(place), back_rows, in_hbm(residual), gain_b, in_hbm(cotangent), scaled, in_hbm(grad_down))
    grad_other = swap(grad_low)
    scaled_rows = exchange(scaled_late)

    position = jnp.stack([expert & 3, (expert >> 2) & 3])
    shard = width // 16
    lead = 2 * experts + 16
    big, slab, token_grad = (4 * shard, 3 * local), (4 * shard, local), (rows, width)
    parts = pl.pallas_call(
        attend_back_body,
        out_shape=(
            *[hbm(big, BF)] * 4, *[hbm(slab, BF)] * 4, hbm((lead, local), BF), *[hbm(token_grad, F32)] * 2
        ),
        in_specs=[SMEM, SMEM] + vmem_specs(2) + [ANY] * 8 + vmem_specs(2),
        out_specs=[ANY] * 11,
        scratch_shapes=[pltpu.VMEM(big, BF)] * 4
        + [pltpu.VMEM(slab, BF)] * 4
        + [pltpu.VMEM((lead, local), BF)]
        + [pltpu.VMEM(token_grad, F32)] * 2
        + [
            pltpu.VMEM((group, 3 * local), BF),
            pltpu.VMEM((group, width), F32),
            pltpu.VMEM((group, local), BF),
            pltpu.VMEM((group, width), BF),
            pltpu.VMEM((local, width), BF),
            pltpu.VMEM((group, 3 * local), BF),
            pltpu.VMEM((heads, group, group), BF),
            pltpu.VMEM((group, local), BF),
            pltpu.VMEM((group, width), BF),
            pltpu.VMEM((3, width, local), BF),
            pltpu.VMEM((rows, width), BF),
            pltpu.VMEM((rows, width), BF),
            pltpu.SemaphoreType.DMA((7 + heads,)),
            pltpu.SemaphoreType.DMA((11,)),
        ],
        compiler_params=params(32),
        cost_estimate=cost(10e9, 10e6),
        name="attention_back",
    )(
        half_one, position, grad_low, grad_other, in_hbm(w_out), in_hbm(qkv), in_hbm(probs), in_hbm(context), in_hbm(normed), in_hbm(w_qkv),
        in_hbm(tokens), in_hbm(x_other), router_grad, moe_gain_grad,
    )
    a0, a1, a2, a3, c0, c1, c2, c3, small, own_gn, other_gn = parts
    a1 = pl.pallas_call(
        order_body,
        out_shape=hbm(a1.shape, BF),
        in_specs=[ANY, ANY],
        out_specs=ANY,
        input_output_aliases={0: 0},
        name="order",
    )(a1, in_hbm(scaled_rows))

    def moves(flip):
        pairs = [(2 * e + t, 2 * (e ^ flip) + t) for e in range(sources) for t in range(2)]
        return lambda value: lax.ppermute(value, ("expert", "tensor"), pairs)

    flat = [moves(d) for d in range(1, 4)]
    along = [moves(4 * d) for d in range(1, 4)]

    def add(*values):
        return functools.reduce(jnp.add, [v.astype(F32) for v in values]).astype(BF)

    def fused(name, body, shapes, values, before=(), mib=8):
        return pl.pallas_call(
            body,
            out_shape=[jax.ShapeDtypeStruct(shape, dtype) for shape, dtype in shapes],
            in_specs=vmem_specs(len(values)) + [ANY] * len(before),
            out_specs=vmem_specs(len(shapes)),
            compiler_params=params(mib),
            cost_estimate=cost(1e3, 1e3),
            name=name,
        )(*values, *[in_hbm(value) for value in before])

    quarter = 4 * shard
    wide = 3 * local
    got_a = [flat[d](a) for d, a in enumerate((a1, a2, a3))]
    got_c = [along[d](c) for d, c in enumerate((c1, c2, c3))]
    got_gn = swap(other_gn)
    folded = pl.pallas_call(
        fold_first_body,
        out_shape=shape_of(*[((shard, wide), BF)] * 4, *[((lead + shard, local), BF)] * 4),
        in_specs=vmem_specs(6) + [ANY] * 3,
        out_specs=vmem_specs(8),
        scratch_shapes=[
            pltpu.VMEM(big, BF),
            pltpu.VMEM(slab, BF),
            pltpu.VMEM((lead, local), BF),
            pltpu.SemaphoreType.DMA((3,)),
        ],
        compiler_params=params(8),
        cost_estimate=cost(1e3, 1e3),
        name="fold_first",
    )(*got_a, *got_c, in_hbm(a0), in_hbm(c0), in_hbm(small))
    parts_z, parts_c = folded[:4], folded[4:]
    got_z = [along[d](parts_z[d + 1]) for d in range(3)]
    got_e = [flat[d](parts_c[d + 1]) for d in range(3)]
    output, grad_tokens = pl.pallas_call(
        tokens_body,
        out_shape=shape_of(((rows, width), BF), ((rows, width), F32)),
        in_specs=vmem_specs(8) + [ANY],
        out_specs=vmem_specs(2),
        compiler_params=params(12),
        cost_estimate=cost(1e3, 1e3),
        name="token_outputs",
    )(place, scaled_rows, residual, own_gn, got_gn, tokens, gain_a, grad_res, in_hbm(parts_z[0]))

    total, c_shard, small = fused(
        "fold_last",
        fold_last_body,
        [((shard, wide), BF), ((shard, local), BF), ((lead, local), BF)],
        (parts_z[0], *got_z, parts_c[0], *got_e),
        (grad_tokens,),
    )
    for b in range(4, sources.bit_length() - 1):
        further = moves(1 << b)
        total = add(total, further(total))
        c_shard = add(c_shard, further(c_shard))
        small = add(small, further(small))

    others = [along[d](total) for d in range(3)]
    c_beside = [flat[d](c_shard) for d in range(3)]
    mine, c_mine = fused(
        "join",
        functools.partial(join_body, 2 * experts + 8),
        [((quarter, wide), BF), ((quarter + lead, local), BF)],
        (total, *others, c_shard, *c_beside, small, swap(small)),
    )
    all_mine = [mine] + [flat[d](mine) for d in range(3)]
    c_others = [along[d](c_mine) for d in range(3)]
    grad_router, grad_norm_gain, grad_moe_gain, grad_rel, grad_qkv, grad_out = pl.pallas_call(
        unpack_body,
        out_shape=shape_of(
            ((experts, width), F32), ((1, width), F32), ((1, width), F32), ((heads, buckets), F32)
        )
        + (hbm((3, width, local), F32), hbm((local, width), F32)),
        in_specs=[SMEM] + vmem_specs(8),
        out_specs=vmem_specs(4) + [ANY] * 2,
        scratch_shapes=[
            pltpu.VMEM((4, quarter, wide), F32),
            pltpu.VMEM((4, quarter, local), F32),
            pltpu.SemaphoreType.DMA((4, 4, 3)),
            pltpu.SemaphoreType.DMA((4, 4)),
        ],
        compiler_params=params(12),
        cost_estimate=cost(1e3, 1e3),
        name="unpack",
    )(position, *all_mine, c_mine, *c_others)

    return (
        output,
        grad_tokens,
        grad_norm_gain[0],
        grad_qkv,
        grad_rel.T,
        grad_out,
        grad_moe_gain[0],
        grad_router.T,
        grad_up[None],
        grad_down[None],
    )


def solution(mesh):
    return jax.shard_map(
        per_device,
        mesh=mesh,
        in_specs=(
            P(("expert", "tensor"), None),
            P("expert", None),
            P(("expert", "tensor"), None),
            P(),
            P(None, None, "tensor"),
            P(None, "tensor"),
            P("tensor", None),
            P(),
            P(),
            P("expert", None, None),
            P("expert", None, None),
            P(("expert", "tensor"), None),
        ),
        out_specs=(
            P(("expert", "tensor"), None),
            P(("expert", "tensor"), None),
            P(),
            P(None, None, "tensor"),
            P(None, "tensor"),
            P("tensor", None),
            P(),
            P(),
            P("expert", None, "tensor"),
            P("expert", "tensor", None),
        ),
        check_vma=False,
    )
```

time: 222 us -> 179 us (0.81)
  waiting for transfers between devices: 106 us -> 50.7 us
  starting transfers between devices: 30.9 us -> 63.5 us
  local copies, waits for them, and re-layouts: 22.4 us -> 4.47 us
  Pallas kernels: 47 us -> 57.4 us
  other arithmetic: 9.35 us -> 1.29 us
  blocking collectives: 4.74 us -> 0 us
    ppermute x8 -> x24, waiting for transfers between devices: 79.6 us -> 30.8 us  [moves(): return lambda value: lax.ppermute(value, ('expert', 'tensor'), pairs)]
    ppermute x8 -> x24, starting transfers between devices: 7.6 us -> 39.4 us  [moves(): return lambda value: lax.ppermute(value, ('expert', 'tensor'), pairs)]
    unnamed x85 -> x35, local copies, waits for them, and re-layouts: 21.2 us -> 4.45 us
    pallas_call x5 -> x9, Pallas kernels: 28.6 us -> 35.8 us  [the longest x1 14.4 us: per_device(): pl.pallas_call(attend_back_body, out_shape=(*[hbm(big, BF)] * 4, *[hbm(sl...]
    all_to_all x4, waiting for transfers between devices: 24.9 us -> 17.7 us  [exchange(): lax.all_to_all(value.reshape(experts, capacity, width), 'expert', split_a...]
    all_gather x2 -> x0, blocking collectives: 4.74 us -> none  [the longest x1 2.4 us: per_device(): grad_att = lax.all_gather(grad_low, 'tensor', axis=0, tiled=True)]
    select_n x5 -> x0, other arithmetic: 3.47 us -> none  [the longest x3 1.56 us: per_device(): jnp.where(bit == 0, total, received)]
    convert_element_type x5 -> x0, other arithmetic: 2.68 us -> none  [the longest x4 1.95 us: add(): return (a.astype(F32) + b.astype(F32)).astype(BF)]
  transfers between devices with their start and end apart: 17 -> 35, of which waited for: 11 -> 16; matrix products, arithmetic and copies ran while one was open for 2% -> 0% of each run, Pallas kernels for 9% -> 23%
where the time goes in v1:
time: 179 us; the launch traced here: 178 us
  starting transfers between devices  63.5 us (35%)
  Pallas kernels  57.4 us (32%)
  waiting for transfers between devices  50.7 us (28%)
  local copies, waits for them, and re-layouts  4.47 us (2%)
    ppermute x24, starting transfers between devices, moves(): return lambda value: lax.ppermute(value, ('expert', 'tensor'), pairs)  39.4 us
    ppermute x24, waiting for transfers between devices, moves(): return lambda value: lax.ppermute(value, ('expert', 'tensor'), pairs)  30.8 us
    all_to_all x4, starting transfers between devices, exchange(): lax.all_to_all(value.reshape(experts, capacity, width), 'expert', split_a...  22.3 us
    all_to_all x4, waiting for transfers between devices, exchange(): lax.all_to_all(value.reshape(experts, capacity, width), 'expert', split_a...  17.7 us
    pallas_call x1, Pallas kernels, per_device(): pl.pallas_call(attend_back_body, out_shape=(*[hbm(big, BF)] * 4, *[hbm(sl...  14.4 us
    pallas_call x1, Pallas kernels, per_device(): pl.pallas_call(attend_body, out_shape=shape_of(((rows, local), BF), ((row...  10.4 us
    pallas_call x1, Pallas kernels, per_device(): pl.pallas_call(expert_body, out_shape=shape_of(((count, width), BF), ((ex...  9.23 us
    pallas_call x1, Pallas kernels, per_device(): pl.pallas_call(expert_grads_body, grid=(half_steps,), in_specs=[col(0), c...  7.18 us
  transfers between devices with their start and end apart: 35, of which 16 were waited for; matrix products, arithmetic and copies ran while one was open for 0% of the time, Pallas kernels for 23%

profile of v1, /device:TPU:0, one launch (start us, length us, event | category | flops | bytes accessed | tf_op | source)
XLA Modules:
  0.0 178.3 jit_solution(5964170301460784530)
XLA Ops:
  1.2 2.7 %place_cotangent.1 = (bf16[256,192]{1,0:T(8,128)(2,1)}, bf16[256,768]{1,0:T(8,128)(2,1)}) custom-call(s32[1,192]{1,0:T(1,128)} %bitcast.34, bf16[192,768]{1,0:T(8,128)(2,1)} %cot_hbm.1), custom_call_target="tpu_custom_call" | custom-call | flops 2000000000 | bytes 1000000 | tf_op jit(solution)/shard_map/place_cotangent/pallas_call | solution.py:624
  3.9 7.9 %all-to-all-start.1 = ((bf16[16,16,768]{2,1,0:T(8,128)(2,1)}), bf16[16,16,768]{2,1,0:T(8,128)(2,1)S(1)}, u32[]{:S(2)}, u32[]{:S(2)}) async-start(bf16[16,16,768]{2,1,0:T(8,128)(2,1)} %bitcast.28), calls=%async_computation.1 | async-start | bytes 786432 | tf_op jit(solution)/shard_map/all_to_all | solution.py:618
  12.1 10.4 %attention.1 = (bf16[192,384]{1,0:T(8,128)(2,1)S(1)}, bf16[192,384]{1,0:T(8,128)(2,1)S(1)}, bf16[384,384]{1,0:T(8,128)(2,1)}, bf16[384,1152]{1,0:T(8,128)(2,1)},...) custom-call(s32[1]{0:T(128)} %bitcast.1.half_ref, s32[1,3]{1,0:T(1,128)S(1)} %copy-done.11, ...), custom_call_target="tpu_custom_call" | custom-call | flops 8000000000 | bytes 4000000 | tf_op jit(solution)/shard_map/attention/pallas_call | solution.py:636
  24.0 3.3 %projection.1 = (bf16[256,768]{1,0:T(8,128)(2,1)}, f32[192,768]{1,0:T(8,128)}) custom-call(bf16[192,384]{1,0:T(8,128)(2,1)S(1)} %get-tuple-element.66.own_ref, bf16[192,384]{1,0:T(8,128)(2,1)S(1)} %collective-permute-done.1.other_ref, bf16[384,768]{1,0:T(8,128)(2,1)S(1)} %collective-permute-done.2.w_other_ref, bf16[384,768]{1,0:T(8,128)(2,1)} %w_out_hbm.1, ...), custom_call_target="tpu_custom_call" | custom-call | flops 2000000000 | bytes 2000000 | tf_op jit(solution)/shard_map/projection/pallas_call | solution.py:662
  27.3 6.9 %all-to-all-start = ((bf16[16,16,768]{2,1,0:T(8,128)(2,1)}), bf16[16,16,768]{2,1,0:T(8,128)(2,1)S(1)}, u32[]{:S(2)}, u32[]{:S(2)}) async-start(bf16[16,16,768]{2,1,0:T(8,128)(2,1)} %bitcast.4), calls=%async_computation | async-start | bytes 786432 | tf_op jit(solution)/shard_map/all_to_all | solution.py:618
  34.4 12.9 %all-to-all-done = bf16[16,16,768]{2,1,0:T(8,128)(2,1)S(1)} async-done(((bf16[16,16,768]{2,1,0:T(8,128)(2,1)}), bf16[16,16,768]{2,1,0:T(8,128)(2,1)S(1)}, u32[]{:S(2)}, u32[]{:S(2)}) %all-to-all-start) | async-done | bytes 393248 | tf_op jit(solution)/shard_map/all_to_all | solution.py:618
  47.3 9.2 %expert.1 = (bf16[256,768]{1,0:T(8,128)(2,1)}, f32[16,768]{1,0:T(8,128)S(1)}, bf16[256,768]{1,0:T(8,128)(2,1)}, bf16[256,768]{1,0:T(8,128)(2,1)}, bf16[256,4608]...) custom-call(s32[1]{0:T(128)} %bitcast.1.half_ref, s32[1]{0:T(128)} %bitcast.2.expert_ref, ...), custom_call_target="tpu_custom_call" | custom-call | flops 10000000000 | bytes 14000000 | tf_op jit(solution)/shard_map/expert/pallas_call | solution.py:685
  56.6 3.6 %all-to-all-start.2 = ((bf16[16,16,768]{2,1,0:T(8,128)(2,1)}), bf16[16,16,768]{2,1,0:T(8,128)(2,1)S(1)}, u32[]{:S(2)}, u32[]{:S(2)}) async-start(bf16[16,16,768]{2,1,0:T(8,128)(2,1)} %bitcast.10), calls=%async_computation.2 | async-start | bytes 786432 | tf_op jit(solution)/shard_map/all_to_all | solution.py:618
  61.5 7.2 %expert_grads.1 = (f32[1536,768]{1,0:T(8,128)}, f32[768,1536]{1,0:T(8,128)}) custom-call(bf16[256,1536]{1,0:T(8,128)(2,1)} %get-tuple-element.73.act_ref, bf16[256,1536]{1,0:T(8,128)(2,1)} %get-tuple-element.74.pre_ref, bf16[256,768]{1,0:T(8,128)(2,1)S(1)} %bitcast.25, bf16[256,768]{1,0:T(8,128)(2,1)} %get-tuple-element.75.gp_ref, ...), custom_call_target="tpu_custom_call" | custom-call | flops 5000000000 | bytes 14000000 | tf_op jit(solution)/shard_map/expert_grads/pallas_call | solution.py:719
  68.7 4.8 %all-to-all-done.2 = bf16[16,16,768]{2,1,0:T(8,128)(2,1)S(1)} async-done(((bf16[16,16,768]{2,1,0:T(8,128)(2,1)}), bf16[16,16,768]{2,1,0:T(8,128)(2,1)S(1)}, u32[]{:S(2)}, u32[]{:S(2)}) %all-to-all-start.2) | async-done | bytes 393248 | tf_op jit(solution)/shard_map/all_to_all | solution.py:618
  76.0 3.8 %all-to-all-start.3 = ((bf16[16,16,768]{2,1,0:T(8,128)(2,1)}), bf16[16,16,768]{2,1,0:T(8,128)(2,1)S(1)}, u32[]{:S(2)}, u32[]{:S(2)}) async-start(bf16[16,16,768]{2,1,0:T(8,128)(2,1)} %bitcast.27), calls=%async_computation.3 | async-start | bytes 786432 | tf_op jit(solution)/shard_map/all_to_all | solution.py:618
  79.8 14.4 %attention_back.1 = (bf16[192,1152]{1,0:T(8,128)(2,1)}, bf16[192,1152]{1,0:T(8,128)(2,1)}, bf16[192,1152]{1,0:T(8,128)(2,1)}, bf16[192,1152]{1,0:T(8,128)(2,1)},...) custom-call(s32[1]{0:T(128)} %bitcast.1.half_ref, ...), custom_call_target="tpu_custom_call" | custom-call | flops 10000000000 | bytes 10000000 | tf_op jit(solution)/shard_map/attention_back/pallas_call | solution.py:761
  101.0 2.7 %collective-permute-start.10 = (bf16[192,384]{1,0:T(8,128)(2,1)}, bf16[192,384]{1,0:T(8,128)(2,1)S(1)}, u32[]{:S(2)}, u32[]{:S(2)}) collective-permute-start(bf16[192,384]{1,0:T(8,128)(2,1)} %get-tuple-element.93), channel_id=1, source_target_pairs={{0,16},{1,17},{2,18},{3,19},{4,20},{5,21},{6,22},{7,23},{8,24},{9,... | collective-permute-start | bytes 442376 | tf_op jit(solution)/shard_map/ppermute | solution.py:807
  103.7 7.0 %collective-permute-done.10.c2_ref = bf16[192,384]{1,0:T(8,128)(2,1)S(1)} collective-permute-done((bf16[192,384]{1,0:T(8,128)(2,1)}, bf16[192,384]{1,0:T(8,128)(2,1)S(1)}, u32[]{:S(2)}, u32[]{:S(2)}) %collective-permute-start.10) | collective-permute-done | bytes 147488 | tf_op jit(solution)/shard_map/ppermute | solution.py:807
  110.7 3.5 %collective-permute-start.11 = (bf16[192,384]{1,0:T(8,128)(2,1)}, bf16[192,384]{1,0:T(8,128)(2,1)S(1)}, u32[]{:S(2)}, u32[]{:S(2)}) collective-permute-start(bf16[192,384]{1,0:T(8,128)(2,1)} %get-tuple-element.94), channel_id=1, source_target_pairs={{0,24},{1,25},{2,26},{3,27},{4,28},{5,29},{6,30},{7,31},{8,16},{9,... | collective-permute-start | bytes 442376 | tf_op jit(solution)/shard_map/ppermute | solution.py:807
  114.2 4.4 %collective-permute-done.11.c3_ref = bf16[192,384]{1,0:T(8,128)(2,1)S(1)} collective-permute-done((bf16[192,384]{1,0:T(8,128)(2,1)}, bf16[192,384]{1,0:T(8,128)(2,1)S(1)}, u32[]{:S(2)}, u32[]{:S(2)}) %collective-permute-start.11) | collective-permute-done | bytes 147488 | tf_op jit(solution)/shard_map/ppermute | solution.py:807
  119.5 2.4 %fold_first.1 = (bf16[48,1152]{1,0:T(8,128)(2,1)S(1)}, bf16[48,1152]{1,0:T(8,128)(2,1)S(1)}, bf16[48,1152]{1,0:T(8,128)(2,1)S(1)}, bf16[48,1152]{1,0:T(8,128)(2,...) custom-call(bf16[192,1152]{1,0:T(8,128)(2,1)S(1)} %collective-permut, ...), custom_call_target="tpu_custom_call" | custom-call | flops 1000 | bytes 1000 | tf_op jit(solution)/shard_map/fold_first/pallas_call | solution.py:831
  136.6 2.6 %collective-permute-start.20 = (bf16[48,1152]{1,0:T(8,128)(2,1)S(1)}, bf16[48,1152]{1,0:T(8,128)(2,1)S(1)}, u32[]{:S(2)}, u32[]{:S(2)}) collective-permute-start(bf16[48,1152]{1,0:T(8,128)(2,1)S(1)} %get-tuple-element.108.refs_0_), channel_id=1, source_target_pairs={{0,24},{1,25},{2,26},{3,27},{4,28},{5,29},{6,30},{7,31},{8,16},{9,... | collective-permute-start | bytes 331784 | tf_op jit(solution)/shard_map/ppermute | solution.py:807
  146.6 3.3 %collective-permute-done.21.refs_5_ = bf16[48,384]{1,0:T(8,128)(2,1)S(1)} collective-permute-done((bf16[48,384]{1,0:T(8,128)(2,1)S(1)}, bf16[48,384]{1,0:T(8,128)(2,1)S(1)}, u32[]{:S(2)}, u32[]{:S(2)}) %collective-permute-start.21) | collective-permute-done | bytes 36896 | tf_op jit(solution)/shard_map/ppermute | solution.py:807
  153.5 2.5 %collective-permute-start.30 = (bf16[240,384]{1,0:T(8,128)(2,1)S(1)}, bf16[240,384]{1,0:T(8,128)(2,1)S(1)}, u32[]{:S(2)}, u32[]{:S(2)}) collective-permute-start(bf16[240,384]{1,0:T(8,128)(2,1)S(1)} %get-tuple-element.112.c0_ref), channel_id=1, source_target_pairs={{0,24},{1,25},{2,26},{3,27},{4,28},{5,29},{6,30},{7,31},{8,16},{9,... | collective-permute-start | bytes 552968 | tf_op jit(solution)/shard_map/ppermute | solution.py:807
  156.1 5.2 %collective-permute-done.30.c3_ref = bf16[240,384]{1,0:T(8,128)(2,1)S(1)} collective-permute-done((bf16[240,384]{1,0:T(8,128)(2,1)S(1)}, bf16[240,384]{1,0:T(8,128)(2,1)S(1)}, u32[]{:S(2)}, u32[]{:S(2)}) %collective-permute-start.30) | collective-permute-done | bytes 184352 | tf_op jit(solution)/shard_map/ppermute | solution.py:807
  161.3 6.5 %collective-permute-start.28 = (bf16[240,384]{1,0:T(8,128)(2,1)S(1)}, bf16[240,384]{1,0:T(8,128)(2,1)S(1)}, u32[]{:S(2)}, u32[]{:S(2)}) collective-permute-start(bf16[240,384]{1,0:T(8,128)(2,1)S(1)} %get-tuple-element.112.c0_ref), channel_id=1, source_target_pairs={{0,8},{1,9},{2,10},{3,11},{4,12},{5,13},{6,14},{7,15},{8,0},{9,1},... | collective-permute-start | bytes 552968 | tf_op jit(solution)/shard_map/ppermute | solution.py:807
  169.9 3.2 %collective-permute-done.28.c1_ref = bf16[240,384]{1,0:T(8,128)(2,1)S(1)} collective-permute-done((bf16[240,384]{1,0:T(8,128)(2,1)S(1)}, bf16[240,384]{1,0:T(8,128)(2,1)S(1)}, u32[]{:S(2)}, u32[]{:S(2)}) %collective-permute-start.28) | collective-permute-done | bytes 184352 | tf_op jit(solution)/shard_map/ppermute | solution.py:807
  173.2 3.9 %unpack.1 = (f32[16,768]{1,0:T(8,128)}, f32[1,768]{1,0:T(1,128)S(1)}, f32[1,768]{1,0:T(1,128)S(1)}, f32[6,32]{1,0:T(8,128)}, f32[3,768,384]{2,1,0:T(8,128)}, /*index=5*/f32[384,768]{1,0:T(8,128)}) custom-call(s32[2]{0:T(128)S(1)} %pad_add_fusion.bits_ref, bf16[192,1152]{1,0:T(8,128)(2,1)S(1)} %get-tuple-element.111.a0_ref, ...), custom_call_target="tpu_custom_call" | custom-call | flops 1000 | bytes 1000 | tf_op jit(solution)/shard_map/unpack/pallas_call | solution.py:882
  (100 shorter events, 42.8 us)
Async XLA Ops:
  0.6 11.4 %collective-permute-start = (bf16[192,768]{1,0:T(8,128)(2,1)}, bf16[192,768]{1,0:T(8,128)(2,1)S(1)}, u32[]{:S(2)}, u32[]{:S(2)}) collective-permute-start(bf16[192,768]{1,0:T(8,128)(2,1)} %x_ref.3), channel_id=1, source_target_pairs={{0,1},{1,0},{2,3},{3,2},{4,5},{5,4},{6,7},{7,6},{8,9},{9,8},{10,11... | collective-permute-start | bytes 884744 | tf_op jit(solution)/shard_map/ppermute | solution.py:615
  3.9 23.5 %all-to-all-start.1 = ((bf16[16,16,768]{2,1,0:T(8,128)(2,1)}), bf16[16,16,768]{2,1,0:T(8,128)(2,1)S(1)}, u32[]{:S(2)}, u32[]{:S(2)}) async-start(bf16[16,16,768]{2,1,0:T(8,128)(2,1)} %bitcast.28), calls=%async_computation.1 | async-start | bytes 786432 | tf_op jit(solution)/shard_map/all_to_all | solution.py:618
  11.8 12.2 %collective-permute-start.2 = (bf16[384,768]{1,0:T(8,128)(2,1)S(1)}, bf16[384,768]{1,0:T(8,128)(2,1)S(1)}, u32[]{:S(2)}, u32[]{:S(2)}) collective-permute-start(bf16[384,768]{1,0:T(8,128)(2,1)S(1)} %copy-done.16), channel_id=1, source_target_pairs={{0,1},{1,0},{2,3},{3,2},{4,5},{5,4},{6,7},{7,6},{8,9},{9,8},{10,11... | collective-permute-start | bytes 1769480 | tf_op jit(solution)/shard_map/ppermute | solution.py:615
  27.3 20.0 %all-to-all-start = ((bf16[16,16,768]{2,1,0:T(8,128)(2,1)}), bf16[16,16,768]{2,1,0:T(8,128)(2,1)S(1)}, u32[]{:S(2)}, u32[]{:S(2)}) async-start(bf16[16,16,768]{2,1,0:T(8,128)(2,1)} %bitcast.4), calls=%async_computation | async-start | bytes 786432 | tf_op jit(solution)/shard_map/all_to_all | solution.py:618
  56.6 16.8 %all-to-all-start.2 = ((bf16[16,16,768]{2,1,0:T(8,128)(2,1)}), bf16[16,16,768]{2,1,0:T(8,128)(2,1)S(1)}, u32[]{:S(2)}, u32[]{:S(2)}) async-start(bf16[16,16,768]{2,1,0:T(8,128)(2,1)} %bitcast.10), calls=%async_computation.2 | async-start | bytes 786432 | tf_op jit(solution)/shard_map/all_to_all | solution.py:618
  76.0 23.3 %all-to-all-start.3 = ((bf16[16,16,768]{2,1,0:T(8,128)(2,1)}), bf16[16,16,768]{2,1,0:T(8,128)(2,1)S(1)}, u32[]{:S(2)}, u32[]{:S(2)}) async-start(bf16[16,16,768]{2,1,0:T(8,128)(2,1)} %bitcast.27), calls=%async_computation.3 | async-start | bytes 786432 | tf_op jit(solution)/shard_map/all_to_all | solution.py:618
  94.3 34.1 %collective-permute-start.5 = (f32[192,768]{1,0:T(8,128)}, f32[192,768]{1,0:T(8,128)S(1)}, u32[]{:S(2)}, u32[]{:S(2)}) collective-permute-start(f32[192,768]{1,0:T(8,128)} %get-tuple-element.87), channel_id=1, source_target_pairs={{0,1},{1,0},{2,3},{3,2},{4,5},{5,4},{6,7},{7,6},{8,9},{9,8},{10,11... | collective-permute-start | bytes 1769480 | tf_op jit(solution)/shard_map/ppermute | solution.py:615
  96.4 22.3 %collective-permute-start.7 = (bf16[192,1152]{1,0:T(8,128)(2,1)}, bf16[192,1152]{1,0:T(8,128)(2,1)S(1)}, u32[]{:S(2)}, u32[]{:S(2)}) collective-permute-start(bf16[192,1152]{1,0:T(8,128)(2,1)} %get-tuple-element.90), channel_id=1, source_target_pairs={{0,4},{1,5},{2,6},{3,7},{4,0},{5,1},{6,2},{7,3},{8,12},{9,13},{10,... | collective-permute-start | bytes 1327112 | tf_op jit(solution)/shard_map/ppermute | solution.py:807
  97.8 20.9 %collective-permute-start.8 = (bf16[192,1152]{1,0:T(8,128)(2,1)}, bf16[192,1152]{1,0:T(8,128)(2,1)}, u32[]{:S(2)}, u32[]{:S(2)}) collective-permute-start(bf16[192,1152]{1,0:T(8,128)(2,1)} %get-tuple-element.91), channel_id=1, source_target_pairs={{0,6},{1,7},{2,4},{3,5},{4,2},{5,3},{6,0},{7,1},{8,14},{9,15},{10,... | collective-permute-start | bytes 1327112 | tf_op jit(solution)/shard_map/ppermute | solution.py:807
  100.0 19.5 %collective-permute-start.6 = (bf16[192,1152]{1,0:T(8,128)(2,1)}, bf16[192,1152]{1,0:T(8,128)(2,1)S(1)}, u32[]{:S(2)}, u32[]{:S(2)}) collective-permute-start(bf16[192,1152]{1,0:T(8,128)(2,1)} %order.1), channel_id=1, source_target_pairs={{0,2},{1,3},{2,0},{3,1},{4,6},{5,7},{6,4},{7,5},{8,10},{9,11},{10,... | collective-permute-start | bytes 1327112 | tf_op jit(solution)/shard_map/ppermute | solution.py:807
  101.0 9.7 %collective-permute-start.10 = (bf16[192,384]{1,0:T(8,128)(2,1)}, bf16[192,384]{1,0:T(8,128)(2,1)S(1)}, u32[]{:S(2)}, u32[]{:S(2)}) collective-permute-start(bf16[192,384]{1,0:T(8,128)(2,1)} %get-tuple-element.93), channel_id=1, source_target_pairs={{0,16},{1,17},{2,18},{3,19},{4,20},{5,21},{6,22},{7,23},{8,24},{9,... | collective-permute-start | bytes 442376 | tf_op jit(solution)/shard_map/ppermute | solution.py:807
  110.7 8.0 %collective-permute-start.11 = (bf16[192,384]{1,0:T(8,128)(2,1)}, bf16[192,384]{1,0:T(8,128)(2,1)S(1)}, u32[]{:S(2)}, u32[]{:S(2)}) collective-permute-start(bf16[192,384]{1,0:T(8,128)(2,1)} %get-tuple-element.94), channel_id=1, source_target_pairs={{0,24},{1,25},{2,26},{3,27},{4,28},{5,29},{6,30},{7,31},{8,16},{9,... | collective-permute-start | bytes 442376 | tf_op jit(solution)/shard_map/ppermute | solution.py:807
  124.0 11.1 %collective-permute-start.12 = (bf16[48,1152]{1,0:T(8,128)(2,1)S(1)}, bf16[48,1152]{1,0:T(8,128)(2,1)S(1)}, u32[]{:S(2)}, u32[]{:S(2)}) collective-permute-start(bf16[48,1152]{1,0:T(8,128)(2,1)S(1)} %get-tuple-element.101), channel_id=1, source_target_pairs={{0,8},{1,9},{2,10},{3,11},{4,12},{5,13},{6,14},{7,15},{8,0},{9,1},... | collective-permute-start | bytes 331784 | tf_op jit(solution)/shard_map/ppermute | solution.py:807
  125.2 10.4 %collective-permute-start.13 = (bf16[48,1152]{1,0:T(8,128)(2,1)S(1)}, bf16[48,1152]{1,0:T(8,128)(2,1)S(1)}, u32[]{:S(2)}, u32[]{:S(2)}) collective-permute-start(bf16[48,1152]{1,0:T(8,128)(2,1)S(1)} %get-tuple-element.102), channel_id=1, source_target_pairs={{0,16},{1,17},{2,18},{3,19},{4,20},{5,21},{6,22},{7,23},{8,24},{9,... | collective-permute-start | bytes 331784 | tf_op jit(solution)/shard_map/ppermute | solution.py:807
  127.2 8.4 %collective-permute-start.14 = (bf16[48,1152]{1,0:T(8,128)(2,1)S(1)}, bf16[48,1152]{1,0:T(8,128)(2,1)S(1)}, u32[]{:S(2)}, u32[]{:S(2)}) collective-permute-start(bf16[48,1152]{1,0:T(8,128)(2,1)S(1)} %get-tuple-element.103), channel_id=1, source_target_pairs={{0,24},{1,25},{2,26},{3,27},{4,28},{5,29},{6,30},{7,31},{8,16},{9,... | collective-permute-start | bytes 331784 | tf_op jit(solution)/shard_map/ppermute | solution.py:807
  136.6 13.3 %collective-permute-start.20 = (bf16[48,1152]{1,0:T(8,128)(2,1)S(1)}, bf16[48,1152]{1,0:T(8,128)(2,1)S(1)}, u32[]{:S(2)}, u32[]{:S(2)}) collective-permute-start(bf16[48,1152]{1,0:T(8,128)(2,1)S(1)} %get-tuple-element.108.refs_0_), channel_id=1, source_target_pairs={{0,24},{1,25},{2,26},{3,27},{4,28},{5,29},{6,30},{7,31},{8,16},{9,... | collective-permute-start | bytes 331784 | tf_op jit(solution)/shard_map/ppermute | solution.py:807
  139.2 10.7 %collective-permute-start.19 = (bf16[48,1152]{1,0:T(8,128)(2,1)S(1)}, bf16[48,1152]{1,0:T(8,128)(2,1)S(1)}, u32[]{:S(2)}, u32[]{:S(2)}) collective-permute-start(bf16[48,1152]{1,0:T(8,128)(2,1)S(1)} %get-tuple-element.108.refs_0_), channel_id=1, source_target_pairs={{0,16},{1,17},{2,18},{3,19},{4,20},{5,21},{6,22},{7,23},{8,24},{9,... | collective-permute-start | bytes 331784 | tf_op jit(solution)/shard_map/ppermute | solution.py:807
  139.9 10.1 %collective-permute-start.18 = (bf16[48,1152]{1,0:T(8,128)(2,1)S(1)}, bf16[48,1152]{1,0:T(8,128)(2,1)S(1)}, u32[]{:S(2)}, u32[]{:S(2)}) collective-permute-start(bf16[48,1152]{1,0:T(8,128)(2,1)S(1)} %get-tuple-element.108.refs_0_), channel_id=1, source_target_pairs={{0,8},{1,9},{2,10},{3,11},{4,12},{5,13},{6,14},{7,15},{8,0},{9,1},... | collective-permute-start | bytes 331784 | tf_op jit(solution)/shard_map/ppermute | solution.py:807
  150.0 23.2 %collective-permute-start.27 = (bf16[192,1152]{1,0:T(8,128)(2,1)S(1)}, bf16[192,1152]{1,0:T(8,128)(2,1)S(1)}, u32[]{:S(2)}, u32[]{:S(2)}) collective-permute-start(bf16[192,1152]{1,0:T(8,128)(2,1)S(1)} %get-tuple-element.111.a0_ref), channel_id=1, source_target_pairs={{0,6},{1,7},{2,4},{3,5},{4,2},{5,3},{6,0},{7,1},{8,14},{9,15},{10,... | collective-permute-start | bytes 1327112 | tf_op jit(solution)/shard_map/ppermute | solution.py:807
  151.5 21.6 %collective-permute-start.26 = (bf16[192,1152]{1,0:T(8,128)(2,1)S(1)}, bf16[192,1152]{1,0:T(8,128)(2,1)S(1)}, u32[]{:S(2)}, u32[]{:S(2)}) collective-permute-start(bf16[192,1152]{1,0:T(8,128)(2,1)S(1)} %get-tuple-element.111.a0_ref), channel_id=1, source_target_pairs={{0,4},{1,5},{2,6},{3,7},{4,0},{5,1},{6,2},{7,3},{8,12},{9,13},{10,... | collective-permute-start | bytes 1327112 | tf_op jit(solution)/shard_map/ppermute | solution.py:807
  152.0 21.1 %collective-permute-start.25 = (bf16[192,1152]{1,0:T(8,128)(2,1)S(1)}, bf16[192,1152]{1,0:T(8,128)(2,1)S(1)}, u32[]{:S(2)}, u32[]{:S(2)}) collective-permute-start(bf16[192,1152]{1,0:T(8,128)(2,1)S(1)} %get-tuple-element.111.a0_ref), channel_id=1, source_target_pairs={{0,2},{1,3},{2,0},{3,1},{4,6},{5,7},{6,4},{7,5},{8,10},{9,11},{10,... | collective-permute-start | bytes 1327112 | tf_op jit(solution)/shard_map/ppermute | solution.py:807
  153.5 7.7 %collective-permute-start.30 = (bf16[240,384]{1,0:T(8,128)(2,1)S(1)}, bf16[240,384]{1,0:T(8,128)(2,1)S(1)}, u32[]{:S(2)}, u32[]{:S(2)}) collective-permute-start(bf16[240,384]{1,0:T(8,128)(2,1)S(1)} %get-tuple-element.112.c0_ref), channel_id=1, source_target_pairs={{0,24},{1,25},{2,26},{3,27},{4,28},{5,29},{6,30},{7,31},{8,16},{9,... | collective-permute-start | bytes 552968 | tf_op jit(solution)/shard_map/ppermute | solution.py:807
  156.1 13.9 %collective-permute-start.29 = (bf16[240,384]{1,0:T(8,128)(2,1)S(1)}, bf16[240,384]{1,0:T(8,128)(2,1)S(1)}, u32[]{:S(2)}, u32[]{:S(2)}) collective-permute-start(bf16[240,384]{1,0:T(8,128)(2,1)S(1)} %get-tuple-element.112.c0_ref), channel_id=1, source_target_pairs={{0,16},{1,17},{2,18},{3,19},{4,20},{5,21},{6,22},{7,23},{8,24},{9,... | collective-permute-start | bytes 552968 | tf_op jit(solution)/shard_map/ppermute | solution.py:807
  161.3 11.9 %collective-permute-start.28 = (bf16[240,384]{1,0:T(8,128)(2,1)S(1)}, bf16[240,384]{1,0:T(8,128)(2,1)S(1)}, u32[]{:S(2)}, u32[]{:S(2)}) collective-permute-start(bf16[240,384]{1,0:T(8,128)(2,1)S(1)} %get-tuple-element.112.c0_ref), channel_id=1, source_target_pairs={{0,8},{1,9},{2,10},{3,11},{4,12},{5,13},{6,14},{7,15},{8,0},{9,1},... | collective-permute-start | bytes 552968 | tf_op jit(solution)/shard_map/ppermute | solution.py:807
  (28 other events, 283.5 us)

commit v2 on v1

--- a/solution.py
+++ b/solution.py
@@ -104,11 +104,15 @@
 
 
 def attend_body(
-    half_ref, lengths_ref, x_ref, x_other_ref, gain_ref, w_ref, bias_ref,
+    half_ref, lengths_ref, x_ref, x_other_ref, gain_ref, w_ref, bias_ref, w_out_ref,
     own_ref, other_ref, context_out, qkv_out, probs_out, normed_out,
-    w_vmem, context_ref, qkv_ref, probs_ref, normed_ref, load_sems, store_sems,
-):
-    loads = fetch([w_ref.at[c] for c in range(3)], [w_vmem.at[c] for c in range(3)], load_sems)
+    w_vmem, w_out_vmem, context_ref, qkv_ref, probs_ref, normed_ref, mask_ref, load_sems, store_sems,
+):
+    loads = fetch(
+        [w_ref.at[c] for c in range(3)] + [w_out_ref],
+        [w_vmem.at[c] for c in range(3)] + [w_out_vmem],
+        load_sems,
+    )
     stores = []
 
     def store(source, target):
@@ -133,10 +137,12 @@
         qkv_ref[:, c * local : (c + 1) * local] = mm(normed, w_vmem[c]).astype(BF)
     store(qkv_ref, qkv_out)
     buckets = bias_ref.shape[1]
-    tables = [
-        mm(bias_ref[...], distance_hot(buckets, delta).astype(F32).astype(BF))
-        for delta in range(1 - blocks, blocks)
-    ]
+    tables = {
+        delta: mm(bias_ref[...], distance_hot(buckets, delta).astype(F32).astype(BF))
+        for delta in (-1, 0, 1)
+    }
+    bias = bias_ref[...].astype(F32)
+    far = {-1: bias[:, halfway - 1 : halfway], 1: bias[:, 2 * halfway - 1 : 2 * halfway]}
     segment_rows = jnp.zeros((group, 1), jnp.int32)
     segment_lanes = jnp.zeros((1, group), jnp.int32)
     border = jnp.int32(0)
@@ -144,56 +150,57 @@
         border = border + lengths_ref[0, s]
         segment_rows = segment_rows + (iota((group, 1), 0) >= border).astype(jnp.int32)
         segment_lanes = segment_lanes + (iota((1, group), 1) >= border).astype(jnp.int32)
+    mask_ref[...] = jnp.where(segment_rows == segment_lanes, 0.0, -1e30)
     for h in range(heads):
         lo = h * HEAD
         keys = qkv_ref[:, local + lo : local + lo + HEAD]
         values = qkv_ref[:, 2 * local + lo : 2 * local + lo + HEAD]
         bands = []
-        for number, delta in enumerate(range(1 - blocks, blocks)):
-            row = tables[number][h : h + 1, :]
+        for delta in range(1 - blocks, blocks):
             if abs(delta) > 1:
-                bands.append(jnp.broadcast_to(row[:, :1], (TILE, TILE)))
+                value = far[1 if delta > 0 else -1][h : h + 1]
+                bands.append(jnp.broadcast_to(value, (TILE, TILE)))
             else:
-                wide = jnp.broadcast_to(row, (TILE, 2 * TILE))
+                wide = jnp.broadcast_to(tables[delta][h : h + 1, :], (TILE, 2 * TILE))
                 band = pltpu.roll(wide, TILE + 1, 1, stride=1, stride_axis=0)
                 bands.append(band[:, :TILE])
-        for b in range(blocks):
-            at = slice(b * TILE, (b + 1) * TILE)
-            queries = qkv_ref[at, lo : lo + HEAD]
-            scores = mm_nt(queries, keys) * (HEAD**-0.5)
-            scores = scores + jnp.concatenate(
-                [bands[k - b + blocks - 1] for k in range(blocks)], axis=1
-            )
-            scores = jnp.where(segment_rows[at] == segment_lanes, scores, -1e30)
-            exponent = jnp.exp(scores - jnp.max(scores, axis=-1, keepdims=True))
-            probs = exponent * (1.0 / jnp.sum(exponent, axis=-1, keepdims=True))
-            low = probs.astype(BF)
-            probs_ref[h, at, :] = low
-            context_ref[at, lo : lo + HEAD] = mm(low, values).astype(BF)
+        bias = jnp.concatenate(
+            [
+                jnp.concatenate([bands[k - b + blocks - 1] for k in range(blocks)], axis=1)
+                for b in range(blocks)
+            ],
+            axis=0,
+        )
+        queries = qkv_ref[:, lo : lo + HEAD] * (HEAD**-0.5)
+        scores = mm_nt(queries, keys) + (bias + mask_ref[...])
+        exponent = jnp.exp(scores - jnp.max(scores, axis=-1, keepdims=True))
+        probs = exponent * (1.0 / jnp.sum(exponent, axis=-1, keepdims=True))
+        low = probs.astype(BF)
+        probs_ref[h] = low
+        context_ref[:, lo : lo + HEAD] = mm(low, values).astype(BF)
         store(probs_ref.at[h], probs_out.at[h])
     store(context_ref, context_out)
-    own_ref[...] = context_ref[pl.ds(own_at, rows), :]
-    other_ref[...] = context_ref[pl.ds(other_at, rows), :]
+    loads[3].wait()
+    other_ref[...] = mm(context_ref[pl.ds(other_at, rows), :], w_out_vmem[...])
+    own_ref[...] = mm(context_ref[pl.ds(own_at, rows), :], w_out_vmem[...])
     for copy in stores:
         copy.wait()
 
 
 def project_body(
-    own_ref, other_ref, w_other_ref, w_own_hbm, x_hbm, gain_ref, place_hbm, out_ref, residual_out,
-    w_own_ref, x_ref, place_ref, residual_ref, sems,
-):
-    loads = fetch([w_own_hbm, x_hbm, place_hbm], [w_own_ref, x_ref, place_ref], sems)
-    attended = mm(other_ref[...], w_other_ref[...])
-    loads[0].wait()
-    attended = attended + mm(own_ref[...], w_own_ref[...])
-    loads[1].wait()
-    residual = x_ref[...].astype(F32) + attended
+    _expert, own_ref, other_ref, x_ref, gain_ref, router_ref, place_hbm, _after,
+    out_ref, router_out, residual_out,
+    place_ref, residual_ref, sems,
+):
+    loads = fetch([place_hbm], [place_ref], sems)
+    router_out[...] = router_ref[...]
+    residual = x_ref[...].astype(F32) + (own_ref[...] + other_ref[...])
     residual_ref[...] = residual
-    store = pltpu.make_async_copy(residual_ref, residual_out, sems.at[3])
+    store = pltpu.make_async_copy(residual_ref, residual_out, sems.at[1])
     store.start()
     factor = lax.rsqrt(jnp.mean(residual * residual, axis=-1, keepdims=True) + epsilon)
     moe_rows = (residual * factor * gain_ref[...].astype(F32)).astype(BF)
-    loads[2].wait()
+    loads[0].wait()
     out_ref[...] = mm(place_ref[...], moe_rows).astype(BF)
     store.wait()
 
@@ -309,25 +316,21 @@
     store.wait()
 
 
-def fold_diagonals(square):
-    wide = jnp.concatenate([square, jnp.zeros_like(square)], axis=1)
+def fold_diagonals(squares):
+    wide = jnp.concatenate([squares, jnp.zeros_like(squares)], axis=2)
     count = TILE
     while count > 8:
         count //= 2
-        wide = wide[:count] + pltpu.roll(wide[count:], 2 * TILE - count, 1)
-    total = wide[:1]
-    for i in range(1, 8):
-        total = total + pltpu.roll(wide[i : i + 1], 2 * TILE - i, 1)
-    return total
+        wide = wide[:, :count] + pltpu.roll(wide[:, count:], 2 * TILE - count, 2)
+    return wide
 
 
 def attend_back_body(
-    half_ref, bits_ref, grad_own_ref, grad_other_ref, w_out_hbm, qkv_hbm, probs_hbm, context_hbm, normed_hbm, w_hbm,
-    x_hbm, x_other_hbm, router_grad_ref, moe_gain_grad_ref,
-    a0_out, a1_out, a2_out, a3_out, c0_out, c1_out, c2_out, c3_out, small_out, own_out, other_out,
-    a0_ref, a1_ref, a2_ref, a3_ref, c0_ref, c1_ref, c2_ref, c3_ref, small_ref, own_ref, other_ref,
-    gqkv_ref, all_ref, gctx_ref, grad_ref,
-    w_out_ref, qkv_ref, probs_ref, context_ref, normed_ref, w_ref, x_ref, x_other_ref, sems, store_sems,
+    half_ref, bits_ref, grad_own_ref, grad_other_ref, w_out_hbm, qkv_hbm, probs_hbm, context_hbm, normed_hbm,
+    folded_ref, edge_ref, a0_out, a1_out, a2_out, a3_out, c0_out, c2_out, near_out, gqkv_out,
+    a0_ref, a1_ref, a2_ref, a3_ref, c0_ref, c1_ref, c2_ref, c3_ref,
+    gqkv_ref, gctx_ref, grad_ref, kv_ref, band_ref,
+    w_out_ref, qkv_ref, probs_ref, context_ref, normed_ref, sems, store_sems,
 ):
     heads = probs_ref.shape[0]
     w_out_in, qkv_in, *probs_in = fetch(
@@ -335,10 +338,8 @@
         [w_out_ref, qkv_ref] + [probs_ref.at[h] for h in range(heads)],
         sems,
     )
-    context_in, *rest = fetch(
-        [context_hbm, w_hbm, x_hbm, x_other_hbm, normed_hbm],
-        [context_ref, w_ref, x_ref, x_other_ref, normed_ref],
-        sems.at[pl.ds(2 + heads, 5)],
+    context_in, normed_in = fetch(
+        [context_hbm, normed_hbm], [context_ref, normed_ref], sems.at[pl.ds(2 + heads, 2)]
     )
     stores = []
 
@@ -347,9 +348,8 @@
         stores[-1].start()
 
     group, width = normed_ref.shape
-    rows = own_ref.shape[0]
-    local = w_ref.shape[2]
-    heads = local // HEAD
+    rows = grad_own_ref.shape[0]
+    local = context_ref.shape[1]
     blocks = group // TILE
     own_at = pl.multiple_of(half_ref[0] * rows, rows)
     other_at = pl.multiple_of((1 - half_ref[0]) * rows, rows)
@@ -359,11 +359,8 @@
     w_out_in.wait()
     gctx_ref[...] = mm_nt(grad, w_out_ref[...]).astype(BF)
     qkv_in.wait()
-    heads_distance = []
     scale = HEAD**-0.5
     buckets = 2 * halfway
-    table = jnp.zeros((8, buckets), F32)
-    per_distance = [[] for _ in range(3)]
     edges = [[], []]
     for h in range(heads):
         lo = h * HEAD
@@ -371,16 +368,18 @@
         keys = qkv_ref[:, local + lo : local + lo + HEAD]
         values = qkv_ref[:, 2 * local + lo : 2 * local + lo + HEAD]
         gctx = gctx_ref[:, lo : lo + HEAD]
+        if h == 0:
+            context_in.wait()
+        terms = gctx.astype(F32) * context_ref[:, lo : lo + HEAD].astype(F32)
+        inner = jnp.sum(terms, axis=-1, keepdims=True)
+        grad_probs = mm_nt(gctx, values)
         probs_in[h].wait()
         low_probs = probs_ref[h]
-        grad_probs = mm_nt(gctx, values)
-        probs = low_probs.astype(F32)
-        inner = jnp.sum(probs * grad_probs, axis=-1, keepdims=True)
-        grad_scores = probs * (grad_probs - inner)
+        grad_scores = low_probs.astype(F32) * (grad_probs - inner)
         low = grad_scores.astype(BF)
         gqkv_ref[:, lo : lo + HEAD] = (mm(low, keys) * scale).astype(BF)
-        gqkv_ref[:, local + lo : local + lo + HEAD] = (mm_tn(low, queries) * scale).astype(BF)
-        gqkv_ref[:, 2 * local + lo : 2 * local + lo + HEAD] = mm_tn(low_probs, gctx).astype(BF)
+        kv_ref[lo : lo + HEAD, :] = mm_tn(queries, low) * scale
+        kv_ref[local + lo : local + lo + HEAD, :] = mm_tn(gctx, low_probs)
         for number, delta in enumerate((-1, 0, 1)):
             band = None
             for b in range(blocks):
@@ -390,7 +389,7 @@
                         b * TILE : (b + 1) * TILE, k * TILE : (k + 1) * TILE
                     ]
                     band = piece if band is None else band + piece
-            per_distance[number].append(fold_diagonals(band))
+            band_ref[number * heads + h] = band
         for number, sign in enumerate((-1, 1)):
             total = jnp.zeros((1, 1), F32)
             for b in range(blocks):
@@ -403,37 +402,91 @@
                             jnp.sum(piece, axis=0, keepdims=True), axis=1, keepdims=True
                         )
             edges[number].append(total)
+    gqkv_ref[:, local : 2 * local] = kv_ref[:local].T.astype(BF)
+    gqkv_ref[:, 2 * local :] = kv_ref[local:].T.astype(BF)
     plane, depth = bits_ref[0], bits_ref[1]
     shard = width // 16
     half = width // 2
     targets = (c0_ref, c1_ref, c2_ref, c3_ref)
-    context_in.wait()
+    dense = mm_tn(context_ref[...], grad).astype(BF)
     for a in range(2):
-        block = mm_tn(context_ref[...], grad_ref[:, a * half : (a + 1) * half]).astype(BF)
         for z in range(2):
             for number, target in enumerate(targets):
 
                 @pl.when((depth ^ (2 * a + z)) == number)
-                def _(target=target, block=block, z=z):
-                    for p in range(4):
-                        piece = block[(z * 4 + p) * shard : (z * 4 + p + 1) * shard]
-                        at = pl.multiple_of((plane ^ p) * shard, shard)
-                        target[pl.ds(at, shard), :] = piece
-    for target, out in zip(targets, (c0_out, c1_out, c2_out, c3_out)):
+                def _(target=target, dense=dense, a=a, z=z):
+                    rows_of = slice(z * 4 * shard, (z + 1) * 4 * shard)
+                    target[...] = dense[rows_of, a * half : (a + 1) * half]
+    size = 4 * shard
+    outs = (c0_out, near_out.at[pl.ds(0, size), :], c2_out, near_out.at[pl.ds(size, size), :])
+    for target, out in zip(targets, outs):
         store(target, out)
-    pad = [jnp.zeros((8 - heads, 2 * TILE), F32)]
+    normed_in.wait()
+    targets = (a0_ref, a1_ref, a2_ref, a3_ref)
+    dense = mm_tn(normed_ref[...], gqkv_ref[...]).astype(BF)
+    for p in range(4):
+        for number, target in enumerate(targets):
+
+            @pl.when((plane ^ p) == number)
+            def _(target=target, p=p):
+                for z in range(4):
+                    piece = dense[(p * 4 + z) * shard : (p * 4 + z + 1) * shard]
+                    at = pl.multiple_of((depth ^ z) * shard, shard)
+                    target[pl.ds(at, shard), :] = piece
+    for target, out in zip(targets, (a0_out, a1_out, a2_out, a3_out)):
+        store(target, out)
+    store(gqkv_ref, gqkv_out)
+    folded_ref[...] = fold_diagonals(band_ref[...])
+    for number in range(2):
+        for h in range(heads):
+            edge_ref[h : h + 1, number * TILE : (number + 1) * TILE] = jnp.broadcast_to(
+                edges[number][h], (1, TILE)
+            )
+    for copy in stores:
+        copy.wait()
+
+
+def small_grads_body(
+    half_ref, folded_ref, edge_ref, router_grad_ref, moe_gain_grad_ref, gqkv_hbm, w_hbm, x_hbm, x_other_hbm,
+    _after, small_ref, own_ref, other_ref,
+    gqkv_ref, w_ref, x_ref, x_other_ref, all_ref, sems,
+):
+    loads = fetch([gqkv_hbm, w_hbm, x_hbm, x_other_hbm], [gqkv_ref, w_ref, x_ref, x_other_ref], sems)
+    rows, width = own_ref.shape
+    local = w_ref.shape[2]
+    heads = local // HEAD
+    buckets = 2 * halfway
+    own_at = pl.multiple_of(half_ref[0] * rows, rows)
+    other_at = pl.multiple_of((1 - half_ref[0]) * rows, rows)
+    folded = folded_ref[...]
+    spread = jnp.zeros((heads * 8, 8 * buckets), F32)
     for number, delta in enumerate((-1, 0, 1)):
-        sums = jnp.concatenate(per_distance[number] + pad, axis=0)
-        distance = iota((buckets, 2 * TILE), 1)
+        distance = iota((8, 2 * TILE), 1) - iota((8, 2 * TILE), 0)
         distance = jnp.where(distance >= TILE, distance - 2 * TILE, distance) + TILE * delta
-        hot = (bucket_of(distance) == iota((buckets, 2 * TILE), 0)).astype(F32)
-        table = table + lax.dot_general(
-            sums, hot, (((1,), (1,)), ((), ())), precision=HIGH, preferred_element_type=F32
+        bucket = bucket_of(distance)
+        hot = jnp.concatenate(
+            [bucket[r : r + 1] == iota((buckets, 2 * TILE), 0) for r in range(8)], axis=0
         )
+        hot = hot.astype(F32).astype(BF)
+        sums = folded[number * heads : (number + 1) * heads].reshape(heads * 8, 2 * TILE)
+        for _ in range(3):
+            low = sums.astype(BF)
+            spread = spread + mm_nt(low, hot)
+            sums = sums - low.astype(F32)
+    same = iota(spread.shape, 0) % 8 == iota(spread.shape, 1) // buckets
+    table = jnp.sum(jnp.where(same, spread, 0.0).reshape(heads, 8, 8 * buckets), axis=1)
+    step = 4 * buckets
+    while step >= buckets:
+        table = table + pltpu.roll(table, step, 1)
+        step //= 2
+    table = table[:, :buckets]
+    table = jnp.concatenate([table, jnp.zeros((8 - heads, buckets), F32)], axis=0)
     for number, bucket in enumerate((halfway - 1, 2 * halfway - 1)):
-        column = jnp.concatenate(edges[number] + [jnp.zeros((8 - heads, 1), F32)], axis=0)
+        column = jnp.concatenate(
+            [edge_ref[:heads, number * TILE : number * TILE + 1], jnp.zeros((8 - heads, 1), F32)], axis=0
+        )
         table = table + jnp.where(iota((8, buckets), 1) == bucket, column, 0.0)
-    for copy in rest:
+    for copy in loads:
         copy.wait()
     total = None
     for c in range(3):
@@ -442,27 +495,11 @@
     all_ref[...] = total
     own_ref[...] = all_ref[pl.ds(own_at, rows), :]
     other_ref[...] = all_ref[pl.ds(other_at, rows), :]
-    store(own_ref, own_out)
-    store(other_ref, other_out)
     gain_grad = jnp.zeros((1, width), F32)
     for ref, part in ((x_ref, own_ref), (x_other_ref, other_ref)):
         x = ref[...].astype(F32)
         factor = lax.rsqrt(jnp.mean(x * x, axis=-1, keepdims=True) + epsilon)
         gain_grad = gain_grad + jnp.sum(part[...] * (x * factor), axis=0, keepdims=True)
-    targets = (a0_ref, a1_ref, a2_ref, a3_ref)
-    for a in range(2):
-        block = mm_tn(normed_ref[:, a * half : (a + 1) * half], gqkv_ref[...]).astype(BF)
-        for p in range(2):
-            for number, target in enumerate(targets):
-
-                @pl.when((plane ^ (2 * a + p)) == number)
-                def _(target=target, block=block, p=p):
-                    for z in range(4):
-                        piece = block[(p * 4 + z) * shard : (p * 4 + z + 1) * shard]
-                        at = pl.multiple_of((depth ^ z) * shard, shard)
-                        target[pl.ds(at, shard), :] = piece
-    for target, out in zip(targets, (a0_out, a1_out, a2_out, a3_out)):
-        store(target, out)
     moe_gain_grad = moe_gain_grad_ref[...]
     row = iota((16, local), 0)
     extra = jnp.concatenate([table, jnp.zeros((8, local - buckets), F32)], axis=1)
@@ -475,9 +512,6 @@
         [router_grad_ref[:, :local], router_grad_ref[:, local:], extra], axis=0
     ).astype(BF)
     small_ref[...] = small
-    store(small_ref, small_out)
-    for copy in stores:
-        copy.wait()
 
 
 def order_body(_value, _after, _out):
@@ -492,25 +526,32 @@
     return ((a.astype(F32) + b.astype(F32)) + (c.astype(F32) + d.astype(F32))).astype(BF)
 
 
+def fold_near_body(got_ref, c0_hbm, c2_hbm, c0_out, c2_out, c0_ref, c2_ref, sems):
+    for copy in fetch([c0_hbm, c2_hbm], [c0_ref, c2_ref], sems):
+        copy.wait()
+    size = c0_ref.shape[0]
+    c0_out[...] = total_of(c0_ref[...], got_ref[:size])
+    c2_out[...] = total_of(c2_ref[...], got_ref[size:])
+
+
 def fold_first_body(
-    a1_ref, a2_ref, a3_ref, c1_ref, c2_ref, c3_ref, a0_hbm, c0_hbm, small_hbm,
-    s0_ref, s1_ref, s2_ref, s3_ref, e0_ref, e1_ref, e2_ref, e3_ref,
-    a0_ref, c0_ref, small_ref, sems,
-):
-    for copy in fetch([a0_hbm, c0_hbm, small_hbm], [a0_ref, c0_ref, small_ref], sems):
-        copy.wait()
+    a1_ref, a2_ref, a3_ref, c0_ref, got_ref, a0_hbm, small_ref,
+    s0_ref, s1_ref, s2_ref, s3_ref, e_ref,
+    a0_ref, sem,
+):
+    load = pltpu.make_async_copy(a0_hbm, a0_ref, sem)
+    load.start()
+    load.wait()
     shard, lead = s0_ref.shape[0], small_ref.shape[0]
     for d, target in enumerate((s0_ref, s1_ref, s2_ref, s3_ref)):
         at = slice(d * shard, (d + 1) * shard)
         target[...] = pairs_of(a0_ref[at], a1_ref[at], a2_ref[at], a3_ref[at])
-    for d, target in enumerate((e0_ref, e1_ref, e2_ref, e3_ref)):
-        at = slice(d * shard, (d + 1) * shard)
-        target[:lead] = small_ref[...]
-        target[lead:] = pairs_of(c0_ref[at], c1_ref[at], c2_ref[at], c3_ref[at])
+    e_ref[:lead] = small_ref[...]
+    e_ref[lead:] = total_of(c0_ref[...], got_ref[...])
 
 
 def fold_last_body(
-    s0_ref, s1_ref, s2_ref, s3_ref, e0_ref, e1_ref, e2_ref, e3_ref, _after, total_ref, c_ref, small_ref
+    s0_ref, s1_ref, s2_ref, s3_ref, e0_ref, e1_ref, e2_ref, e3_ref, total_ref, c_ref, small_ref
 ):
     lead = small_ref.shape[0]
     total_ref[...] = pairs_of(s0_ref[...], s1_ref[...], s2_ref[...], s3_ref[...])
@@ -518,16 +559,20 @@
     c_ref[...] = pairs_of(e0_ref[lead:], e1_ref[lead:], e2_ref[lead:], e3_ref[lead:])
 
 
-def join_body(shared, *refs):
-    total_refs, c_refs = refs[:4], refs[4:8]
-    small_ref, other_ref, mine_ref, c_mine_ref = refs[8:]
-    shard = c_refs[0].shape[0]
-    for d in range(4):
-        mine_ref[d * shard : (d + 1) * shard] = total_refs[d][...]
-        c_mine_ref[d * shard : (d + 1) * shard] = c_refs[d][...]
+def join_body(shared, t0_ref, t1_ref, t2_ref, t3_ref, c_ref, small_ref, other_ref, _after, mine_ref, c_mine_ref):
+    shard, size = t0_ref.shape[0], c_ref.shape[0]
+    for d, ref in enumerate((t0_ref, t1_ref, t2_ref, t3_ref)):
+        mine_ref[d * shard : (d + 1) * shard] = ref[...]
+    c_mine_ref[:size] = c_ref[...]
     own = small_ref[...].astype(F32)
     both = own + other_ref[...].astype(F32)
-    c_mine_ref[4 * shard :] = jnp.where(iota(own.shape, 0) < shared, both, own).astype(BF)
+    c_mine_ref[size:] = jnp.where(iota(own.shape, 0) < shared, both, own).astype(BF)
+
+
+def stack_body(a_ref, b_ref, out_ref):
+    size = a_ref.shape[0]
+    out_ref[:size] = a_ref[...]
+    out_ref[size:] = b_ref[...]
 
 
 def tokens_body(
@@ -541,7 +586,7 @@
 
 
 def unpack_body(
-    bits_ref, a0_ref, a1_ref, a2_ref, a3_ref, c0_ref, c1_ref, c2_ref, c3_ref,
+    bits_ref, a0_ref, a1_ref, a2_ref, a3_ref, c0_ref, c2_ref, near_ref,
     router_ref, norm_gain_ref, moe_gain_ref, bias_ref, qkv_out, w_out_out,
     wide_ref, w_out_ref, qkv_sems, out_sems,
 ):
@@ -562,21 +607,18 @@
                 )
                 copy.start()
                 copies.append(copy)
-    others = (c0_ref, c1_ref, c2_ref, c3_ref)
+    size = c0_ref.shape[0]
+    others = (c0_ref, near_ref.at[:size], c2_ref, near_ref.at[size:])
     for number, ref in enumerate(others):
         w_out_ref[number] = ref[: 4 * shard].astype(F32)
         slab = depth ^ number
         lane = pl.multiple_of((slab // 2) * local, local)
-        for b in range(4):
-            place = (slab % 2) * 4 + (plane ^ b)
-            at = pl.multiple_of(place * shard, shard)
-            copy = pltpu.make_async_copy(
-                w_out_ref.at[number, pl.ds(b * shard, shard), :],
-                w_out_out.at[pl.ds(at, shard), pl.ds(lane, local)],
-                out_sems.at[number, b],
-            )
-            copy.start()
-            copies.append(copy)
+        at = pl.multiple_of((slab % 2) * 4 * shard, 4 * shard)
+        copy = pltpu.make_async_copy(
+            w_out_ref.at[number], w_out_out.at[pl.ds(at, 4 * shard), pl.ds(lane, local)], out_sems.at[number]
+        )
+        copy.start()
+        copies.append(copy)
     parts = [ref[4 * shard :].astype(F32) for ref in others]
     small = (parts[0] + parts[1]) + (parts[2] + parts[3])
     experts = router_ref.shape[0]
@@ -584,8 +626,8 @@
     router_ref[:, local:] = small[experts : 2 * experts]
     rest = small[2 * experts :]
     for number, ref in enumerate((moe_gain_ref, norm_gain_ref)):
-        ref[:, :local] = rest[2 * number : 2 * number + 1]
-        ref[:, local:] = rest[2 * number + 1 : 2 * number + 2]
+        ref[:local] = rest[2 * number]
+        ref[local:] = rest[2 * number + 1]
     bias_ref[...] = rest[8 : 8 + bias_ref.shape[0], : bias_ref.shape[1]]
     for copy in copies:
         copy.wait()
@@ -620,7 +662,6 @@
         ).reshape(slots, width)
 
     x_other = swap(tokens)
-    w_out_other = swap(w_out)
     place, cot_slots = pl.pallas_call(
         functools.partial(prep_body, capacity, experts),
         out_shape=(hbm((slots, rows), BF),) + shape_of(((slots, width), BF)),
@@ -633,48 +674,49 @@
     cot_rows = exchange(cot_slots)
 
     bias_rows = jnp.pad(rel_bias.T, ((0, 8 - heads), (0, 0)))
-    own_ctx, other_ctx, context, qkv, probs, normed = pl.pallas_call(
+    own_sum, other_sum, context, qkv, probs, normed = pl.pallas_call(
         attend_body,
-        out_shape=shape_of(((rows, local), BF), ((rows, local), BF))
+        out_shape=shape_of(((rows, width), F32), ((rows, width), F32))
         + (
             hbm((group, local), BF),
             hbm((group, 3 * local), BF),
             hbm((heads, group, group), BF),
             hbm((group, width), BF),
         ),
-        in_specs=[SMEM, SMEM] + vmem_specs(3) + [ANY] + vmem_specs(1),
+        in_specs=[SMEM, SMEM] + vmem_specs(3) + [ANY] + vmem_specs(1) + [ANY],
         out_specs=vmem_specs(2) + [ANY] * 4,
         scratch_shapes=[
             pltpu.VMEM((3, width, local), BF),
+            pltpu.VMEM((local, width), BF),
             pltpu.VMEM((group, local), BF),
             pltpu.VMEM((group, 3 * local), BF),
             pltpu.VMEM((heads, group, group), BF),
             pltpu.VMEM((group, width), BF),
-            pltpu.SemaphoreType.DMA((3,)),
+            pltpu.VMEM((group, group), F32),
+            pltpu.SemaphoreType.DMA((4,)),
             pltpu.SemaphoreType.DMA((heads + 3,)),
         ],
         compiler_params=params(20),
         cost_estimate=cost(8e9, 4e6),
         name="attention",
-    )(half_one, lengths, tokens, x_other, gain_a, in_hbm(w_qkv), bias_rows)
-    got_ctx = swap(other_ctx)
-
-    moe_slots, residual = pl.pallas_call(
+    )(half_one, lengths, tokens, x_other, gain_a, in_hbm(w_qkv), bias_rows, in_hbm(w_out))
+    got_sum = swap(other_sum)
+
+    expert_one = expert.reshape(1)
+    moe_slots, router, residual = pl.pallas_call(
         project_body,
-        out_shape=shape_of(((slots, width), BF)) + (hbm((rows, width), F32),),
-        in_specs=vmem_specs(3) + [ANY] * 2 + vmem_specs(1) + [ANY],
-        out_specs=vmem_specs(1) + [ANY],
+        out_shape=shape_of(((slots, width), BF), ((width, experts), BF)) + (hbm((rows, width), F32),),
+        in_specs=[SMEM] + vmem_specs(5) + [ANY, ANY],
+        out_specs=vmem_specs(2) + [ANY],
         scratch_shapes=[
-            pltpu.VMEM((local, width), BF),
-            pltpu.VMEM((rows, width), BF),
             pltpu.VMEM((slots, rows), BF),
             pltpu.VMEM((rows, width), F32),
-            pltpu.SemaphoreType.DMA((4,)),
+            pltpu.SemaphoreType.DMA((2,)),
         ],
         compiler_params=params(12),
         cost_estimate=cost(2e9, 2e6),
         name="projection",
-    )(own_ctx, got_ctx, w_out_other, in_hbm(w_out), in_hbm(tokens), gain_b, in_hbm(place))
+    )(expert_one, own_sum, got_sum, tokens, gain_b, w_router, in_hbm(place), cot_rows)
     stacked = exchange(moe_slots)
 
     count = sources * capacity
@@ -710,7 +752,7 @@
         compiler_params=params(32),
         cost_estimate=cost(10e9, 14e6),
         name="expert",
-    )(half_one, expert.reshape(1), stacked, cot_rows, w_router, in_hbm(w_in[0]), in_hbm(w_down[0]))
+    )(half_one, expert_one, stacked, cot_rows, router, in_hbm(w_in[0]), in_hbm(w_down[0]))
     back_rows = exchange(back)
     peer = swap(send)
 
@@ -757,42 +799,38 @@
     position = jnp.stack([expert & 3, (expert >> 2) & 3])
     shard = width // 16
     lead = 2 * experts + 16
-    big, slab, token_grad = (4 * shard, 3 * local), (4 * shard, local), (rows, width)
-    parts = pl.pallas_call(
+    big, slab = (4 * shard, 3 * local), (4 * shard, local)
+    folded, edges, a0, a1, a2, a3, c0, c2, c_near, grad_joined = pl.pallas_call(
         attend_back_body,
         out_shape=(
-            *[hbm(big, BF)] * 4, *[hbm(slab, BF)] * 4, hbm((lead, local), BF), *[hbm(token_grad, F32)] * 2
+            *shape_of(((3 * heads, 8, 2 * TILE), F32), ((8, 2 * TILE), F32)),
+            *[hbm(big, BF)] * 4, *[hbm(slab, BF)] * 2, hbm((8 * shard, local), BF), hbm((group, 3 * local), BF),
         ),
-        in_specs=[SMEM, SMEM] + vmem_specs(2) + [ANY] * 8 + vmem_specs(2),
-        out_specs=[ANY] * 11,
+        in_specs=[SMEM, SMEM] + vmem_specs(2) + [ANY] * 5,
+        out_specs=vmem_specs(2) + [ANY] * 8,
         scratch_shapes=[pltpu.VMEM(big, BF)] * 4
         + [pltpu.VMEM(slab, BF)] * 4
-        + [pltpu.VMEM((lead, local), BF)]
-        + [pltpu.VMEM(token_grad, F32)] * 2
         + [
             pltpu.VMEM((group, 3 * local), BF),
-            pltpu.VMEM((group, width), F32),
             pltpu.VMEM((group, local), BF),
             pltpu.VMEM((group, width), BF),
+            pltpu.VMEM((2 * local, group), F32),
+            pltpu.VMEM((3 * heads, TILE, TILE), F32),
             pltpu.VMEM((local, width), BF),
             pltpu.VMEM((group, 3 * local), BF),
             pltpu.VMEM((heads, group, group), BF),
             pltpu.VMEM((group, local), BF),
             pltpu.VMEM((group, width), BF),
-            pltpu.VMEM((3, width, local), BF),
-            pltpu.VMEM((rows, width), BF),
-            pltpu.VMEM((rows, width), BF),
-            pltpu.SemaphoreType.DMA((7 + heads,)),
-            pltpu.SemaphoreType.DMA((11,)),
+            pltpu.SemaphoreType.DMA((4 + heads,)),
+            pltpu.SemaphoreType.DMA((9,)),
         ],
         compiler_params=params(32),
         cost_estimate=cost(10e9, 10e6),
         name="attention_back",
     )(
-        half_one, position, grad_low, grad_other, in_hbm(w_out), in_hbm(qkv), in_hbm(probs), in_hbm(context), in_hbm(normed), in_hbm(w_qkv),
-        in_hbm(tokens), in_hbm(x_other), router_grad, moe_gain_grad,
+        half_one, position, grad_low, grad_other, in_hbm(w_out), in_hbm(qkv), in_hbm(probs), in_hbm(context),
+        in_hbm(normed),
     )
-    a0, a1, a2, a3, c0, c1, c2, c3, small, own_gn, other_gn = parts
     a1 = pl.pallas_call(
         order_body,
         out_shape=hbm(a1.shape, BF),
@@ -800,7 +838,7 @@
         out_specs=ANY,
         input_output_aliases={0: 0},
         name="order",
-    )(a1, in_hbm(scaled_rows))
+    )(a1, scaled_rows)
 
     def moves(flip):
         pairs = [(2 * e + t, 2 * (e ^ flip) + t) for e in range(sources) for t in range(2)]
@@ -821,31 +859,43 @@
             compiler_params=params(mib),
             cost_estimate=cost(1e3, 1e3),
             name=name,
-        )(*values, *[in_hbm(value) for value in before])
+        )(*values, *before)
 
     quarter = 4 * shard
     wide = 3 * local
     got_a = [flat[d](a) for d, a in enumerate((a1, a2, a3))]
-    got_c = [along[d](c) for d, c in enumerate((c1, c2, c3))]
-    got_gn = swap(other_gn)
-    folded = pl.pallas_call(
-        fold_first_body,
-        out_shape=shape_of(*[((shard, wide), BF)] * 4, *[((lead + shard, local), BF)] * 4),
-        in_specs=vmem_specs(6) + [ANY] * 3,
-        out_specs=vmem_specs(8),
-        scratch_shapes=[
-            pltpu.VMEM(big, BF),
-            pltpu.VMEM(slab, BF),
-            pltpu.VMEM((lead, local), BF),
-            pltpu.SemaphoreType.DMA((3,)),
-        ],
+    c0, c2 = pl.pallas_call(
+        fold_near_body,
+        out_shape=shape_of(*[(slab, BF)] * 2),
+        in_specs=vmem_specs(1) + [ANY] * 2,
+        out_specs=vmem_specs(2),
+        scratch_shapes=[pltpu.VMEM(slab, BF)] * 2 + [pltpu.SemaphoreType.DMA((2,))],
         compiler_params=params(8),
         cost_estimate=cost(1e3, 1e3),
-        name="fold_first",
-    )(*got_a, *got_c, in_hbm(a0), in_hbm(c0), in_hbm(small))
-    parts_z, parts_c = folded[:4], folded[4:]
-    got_z = [along[d](parts_z[d + 1]) for d in range(3)]
-    got_e = [flat[d](parts_c[d + 1]) for d in range(3)]
+        name="fold_near",
+    )(along[0](c_near), in_hbm(c0), in_hbm(c2))
+    got_c = along[1](c2)
+    small, own_gn, other_gn = pl.pallas_call(
+        small_grads_body,
+        out_shape=shape_of(((lead, local), BF), ((rows, width), F32), ((rows, width), F32)),
+        in_specs=[SMEM] + vmem_specs(4) + [ANY] * 5,
+        out_specs=vmem_specs(3),
+        scratch_shapes=[
+            pltpu.VMEM((group, 3 * local), BF),
+            pltpu.VMEM((3, width, local), BF),
+            pltpu.VMEM((rows, width), BF),
+            pltpu.VMEM((rows, width), BF),
+            pltpu.VMEM((group, width), F32),
+            pltpu.SemaphoreType.DMA((4,)),
+        ],
+        compiler_params=params(16),
+        cost_estimate=cost(1e3, 1e3),
+        name="small_grads",
+    )(
+        half_one, folded, edges, router_grad, moe_gain_grad, in_hbm(grad_joined), in_hbm(w_qkv), in_hbm(tokens),
+        in_hbm(x_other), c0,
+    )
+    got_gn = swap(other_gn)
     output, grad_tokens = pl.pallas_call(
         tokens_body,
         out_shape=shape_of(((rows, width), BF), ((rows, width), F32)),
@@ -854,58 +904,71 @@
         compiler_params=params(12),
         cost_estimate=cost(1e3, 1e3),
         name="token_outputs",
-    )(place, scaled_rows, residual, own_gn, got_gn, tokens, gain_a, grad_res, in_hbm(parts_z[0]))
-
-    total, c_shard, small = fused(
+    )(place, scaled_rows, residual, own_gn, got_gn, tokens, gain_a, grad_res, c0)
+
+    *parts_z, part_c = pl.pallas_call(
+        fold_first_body,
+        out_shape=shape_of(*[((shard, wide), BF)] * 4, ((lead + 4 * shard, local), BF)),
+        in_specs=vmem_specs(5) + [ANY] + vmem_specs(1),
+        out_specs=vmem_specs(5),
+        scratch_shapes=[pltpu.VMEM(big, BF), pltpu.SemaphoreType.DMA],
+        compiler_params=params(8),
+        cost_estimate=cost(1e3, 1e3),
+        name="fold_first",
+    )(*got_a, c0, got_c, in_hbm(a0), small)
+    got_z = [along[d](parts_z[d + 1]) for d in range(3)]
+    got_e = [flat[d](part_c) for d in range(3)]
+    total, c_full, small = fused(
         "fold_last",
         fold_last_body,
-        [((shard, wide), BF), ((shard, local), BF), ((lead, local), BF)],
-        (parts_z[0], *got_z, parts_c[0], *got_e),
-        (grad_tokens,),
+        [((shard, wide), BF), (slab, BF), ((lead, local), BF)],
+        (parts_z[0], *got_z, part_c, *got_e),
     )
     for b in range(4, sources.bit_length() - 1):
         further = moves(1 << b)
         total = add(total, further(total))
-        c_shard = add(c_shard, further(c_shard))
+        c_full = add(c_full, further(c_full))
         small = add(small, further(small))
 
     others = [along[d](total) for d in range(3)]
-    c_beside = [flat[d](c_shard) for d in range(3)]
     mine, c_mine = fused(
         "join",
         functools.partial(join_body, 2 * experts + 8),
         [((quarter, wide), BF), ((quarter + lead, local), BF)],
-        (total, *others, c_shard, *c_beside, small, swap(small)),
+        (total, *others, c_full, small, swap(small)),
+        (grad_tokens,),
     )
     all_mine = [mine] + [flat[d](mine) for d in range(3)]
-    c_others = [along[d](c_mine) for d in range(3)]
+    c_far = along[1](c_mine)
+    (c_two,) = fused("stack", stack_body, [((2 * (quarter + lead), local), BF)], (c_mine, c_far))
+    c_near = along[0](c_two)
     grad_router, grad_norm_gain, grad_moe_gain, grad_rel, grad_qkv, grad_out = pl.pallas_call(
         unpack_body,
         out_shape=shape_of(
-            ((experts, width), F32), ((1, width), F32), ((1, width), F32), ((heads, buckets), F32)
+            ((experts, width), F32), ((width,), F32), ((width,), F32), ((heads, buckets), F32)
         )
         + (hbm((3, width, local), F32), hbm((local, width), F32)),
-        in_specs=[SMEM] + vmem_specs(8),
+        in_specs=[SMEM] + vmem_specs(7),
         out_specs=vmem_specs(4) + [ANY] * 2,
         scratch_shapes=[
             pltpu.VMEM((4, quarter, wide), F32),
             pltpu.VMEM((4, quarter, local), F32),
             pltpu.SemaphoreType.DMA((4, 4, 3)),
-            pltpu.SemaphoreType.DMA((4, 4)),
+            pltpu.SemaphoreType.DMA((4,)),
         ],
         compiler_params=params(12),
         cost_estimate=cost(1e3, 1e3),
         name="unpack",
-    )(position, *all_mine, c_mine, *c_others)
+    )(position, *all_mine, c_mine, c_far, c_near)
 
     return (
         output,
         grad_tokens,
-        grad_norm_gain[0],
+        grad_norm_gain,
         grad_qkv,
         grad_rel.T,
         grad_out,
-        grad_moe_gain[0],
+        grad_moe_gain,
         grad_router.T,
         grad_up[None],
         grad_down[None],

time: 179 us -> 167 us (0.933)
  starting transfers between devices: 63.5 us -> 43.1 us
  blocking collectives: 0 us -> 16.9 us
  Pallas kernels: 57.4 us -> 52.2 us
  local copies, waits for them, and re-layouts: 4.47 us -> 2.05 us
    all_to_all x0 -> x1, blocking collectives: none -> 16.9 us  [exchange(): lax.all_to_all(value.reshape(experts, capacity, width), 'expert', split_a...]
    ppermute x24 -> x19, starting transfers between devices: 39.4 us -> 26.6 us  [moves(): return lambda value: lax.ppermute(value, ('expert', 'tensor'), pairs)]
    ppermute x24 -> x19, waiting for transfers between devices: 30.8 us -> 40.4 us  [moves(): return lambda value: lax.ppermute(value, ('expert', 'tensor'), pairs)]
    all_to_all x4 -> x3, waiting for transfers between devices: 17.7 us -> 9.12 us  [exchange(): lax.all_to_all(value.reshape(experts, capacity, width), 'expert', split_a...]
    all_to_all x4 -> x3, starting transfers between devices: 22.3 us -> 15.5 us  [exchange(): lax.all_to_all(value.reshape(experts, capacity, width), 'expert', split_a...]
    pallas_call x3 -> x5, Pallas kernels: 28.1 us -> 24 us  [the longest x1 9.49 us: per_device(): pl.pallas_call(attend_back_body, out_shape=(*shape_of(((3 * heads, 8, 2 *...]
    unnamed x35 -> x29, local copies, waits for them, and re-layouts: 4.45 us -> 2.03 us
  transfers between devices with their start and end apart: 35 -> 28, of which waited for: 16 -> 13; matrix products, arithmetic and copies ran while one was open for 0% -> 0% of each run, Pallas kernels for 23% -> 21%
where the time goes in v2:
time: 167 us; the launch traced here: 166 us
  Pallas kernels  52.2 us (31%)
  waiting for transfers between devices  50.6 us (30%)
  starting transfers between devices  43.1 us (26%)
  blocking collectives  16.9 us (10%)
  local copies, waits for them, and re-layouts  2.05 us (1%)
    ppermute x19, waiting for transfers between devices, moves(): return lambda value: lax.ppermute(value, ('expert', 'tensor'), pairs)  40.4 us
    ppermute x19, starting transfers between devices, moves(): return lambda value: lax.ppermute(value, ('expert', 'tensor'), pairs)  26.6 us
    all_to_all x1, blocking collectives, exchange(): lax.all_to_all(value.reshape(experts, capacity, width), 'expert', split_a...  16.9 us
    all_to_all x3, starting transfers between devices, exchange(): lax.all_to_all(value.reshape(experts, capacity, width), 'expert', split_a...  15.5 us
    pallas_call x1, Pallas kernels, per_device(): pl.pallas_call(attend_back_body, out_shape=(*shape_of(((3 * heads, 8, 2 *...  9.49 us
    pallas_call x1, Pallas kernels, per_device(): pl.pallas_call(expert_body, out_shape=shape_of(((count, width), BF), ((ex...  9.27 us
    all_to_all x3, waiting for transfers between devices, exchange(): lax.all_to_all(value.reshape(experts, capacity, width), 'expert', split_a...  9.12 us
    pallas_call x1, Pallas kernels, per_device(): pl.pallas_call(attend_body, out_shape=shape_of(((rows, width), F32), ((ro...  8.25 us
  transfers between devices with their start and end apart: 28, of which 13 were waited for; matrix products, arithmetic and copies ran while one was open for 0% of the time, Pallas kernels for 21%

profile of v2, /device:TPU:0, one launch (start us, length us, event | category | flops | bytes accessed | tf_op | source)
XLA Modules:
  0.0 166.0 jit_solution(18432991880030695859)
XLA Ops:
  1.2 2.6 %place_cotangent.1 = (bf16[256,192]{1,0:T(8,128)(2,1)}, bf16[256,768]{1,0:T(8,128)(2,1)}) custom-call(s32[1,192]{1,0:T(1,128)} %bitcast.36, bf16[192,768]{1,0:T(8,128)(2,1)} %cot_hbm.1), custom_call_target="tpu_custom_call" | custom-call | flops 2000000000 | bytes 1000000 | tf_op jit(solution)/shard_map/place_cotangent/pallas_call | solution.py:665
  3.8 7.9 %all-to-all-start = ((bf16[16,16,768]{2,1,0:T(8,128)(2,1)}), bf16[16,16,768]{2,1,0:T(8,128)(2,1)S(1)}, u32[]{:S(2)}, u32[]{:S(2)}) async-start(bf16[16,16,768]{2,1,0:T(8,128)(2,1)} %bitcast.30), calls=%async_computation | async-start | bytes 786432 | tf_op jit(solution)/shard_map/all_to_all | solution.py:660
  11.8 8.2 %attention.1 = (f32[192,768]{1,0:T(8,128)S(1)}, f32[192,768]{1,0:T(8,128)S(1)}, bf16[384,384]{1,0:T(8,128)(2,1)}, bf16[384,1152]{1,0:T(8,128)(2,1)}, bf16[6,384,...) custom-call(s32[1]{0:T(128)} %bitcast.1.half_ref, s32[1,3]{1,0:T(1,128)S(1)} %copy-done.9, bf16[192,768]{1,0:T(8,128)(2,1)S(1)} %copy-done.3, ...), custom_call_target="tpu_custom_call" | custom-call | flops 8000000000 | bytes 4000000 | tf_op jit(solution)/shard_map/attention/pallas_call | solution.py:677
  20.5 4.4 %all-to-all-done = bf16[16,16,768]{2,1,0:T(8,128)(2,1)S(1)} async-done(((bf16[16,16,768]{2,1,0:T(8,128)(2,1)}), bf16[16,16,768]{2,1,0:T(8,128)(2,1)S(1)}, u32[]{:S(2)}, u32[]{:S(2)}) %all-to-all-start) | async-done | bytes 393248 | tf_op jit(solution)/shard_map/all_to_all | solution.py:660
  26.3 16.9 %all_to_all.20 = bf16[16,16,768]{2,1,0:T(8,128)(2,1)S(1)} all-to-all(bf16[16,16,768]{2,1,0:T(8,128)(2,1)S(1)} %bitcast.27), channel_id=1, replica_groups=mesh['expert'=16,'tensor'=2] {'expert'}, dimensions={0} | all-to-all | bytes 786432 | tf_op jit(solution)/shard_map/all_to_all | solution.py:660
  43.1 9.3 %expert.1 = (bf16[256,768]{1,0:T(8,128)(2,1)}, f32[16,768]{1,0:T(8,128)S(1)}, bf16[256,768]{1,0:T(8,128)(2,1)}, bf16[256,768]{1,0:T(8,128)(2,1)}, bf16[256,4608]...) custom-call(s32[1]{0:T(128)} %bitcast.1.half_ref, s32[1]{0:T(128)} %bitcast.2._expert.expert_ref, ...), custom_call_target="tpu_custom_call" | custom-call | flops 10000000000 | bytes 14000000 | tf_op jit(solution)/shard_map/expert/pallas_call | solution.py:727
  52.5 3.8 %all-to-all-start.2 = ((bf16[16,16,768]{2,1,0:T(8,128)(2,1)}), bf16[16,16,768]{2,1,0:T(8,128)(2,1)S(1)}, u32[]{:S(2)}, u32[]{:S(2)}) async-start(bf16[16,16,768]{2,1,0:T(8,128)(2,1)} %bitcast.10), calls=%async_computation.2 | async-start | bytes 786432 | tf_op jit(solution)/shard_map/all_to_all | solution.py:660
  57.4 7.2 %expert_grads.1 = (f32[1536,768]{1,0:T(8,128)}, f32[768,1536]{1,0:T(8,128)}) custom-call(bf16[256,1536]{1,0:T(8,128)(2,1)} %get-tuple-element.76.act_ref, bf16[256,1536]{1,0:T(8,128)(2,1)} %get-tuple-element.77.pre_ref, bf16[256,768]{1,0:T(8,128)(2,1)S(1)} %bitcast.26, bf16[256,768]{1,0:T(8,128)(2,1)} %get-tuple-element.78.gp_ref, ...), custom_call_target="tpu_custom_call" | custom-call | flops 5000000000 | bytes 14000000 | tf_op jit(solution)/shard_map/expert_grads/pallas_call | solution.py:761
  64.6 4.8 %all-to-all-done.2 = bf16[16,16,768]{2,1,0:T(8,128)(2,1)S(1)} async-done(((bf16[16,16,768]{2,1,0:T(8,128)(2,1)}), bf16[16,16,768]{2,1,0:T(8,128)(2,1)S(1)}, u32[]{:S(2)}, u32[]{:S(2)}) %all-to-all-start.2) | async-done | bytes 393248 | tf_op jit(solution)/shard_map/all_to_all | solution.py:660
  71.9 3.8 %all-to-all-start.3 = ((bf16[16,16,768]{2,1,0:T(8,128)(2,1)}), bf16[16,16,768]{2,1,0:T(8,128)(2,1)S(1)}, u32[]{:S(2)}, u32[]{:S(2)}) async-start(bf16[16,16,768]{2,1,0:T(8,128)(2,1)} %bitcast.29), calls=%async_computation.3 | async-start | bytes 786432 | tf_op jit(solution)/shard_map/all_to_all | solution.py:660
  75.7 9.5 %attention_back.1 = (f32[18,8,256]{2,1,0:T(8,128)S(1)}, f32[8,256]{1,0:T(8,128)S(1)}, bf16[192,1152]{1,0:T(8,128)(2,1)}, bf16[192,1152]{1,0:T(8,128)(2,1)}, bf16...) custom-call(s32[1]{0:T(128)} %bitcast.1.half_ref, ...), custom_call_target="tpu_custom_call" | custom-call | flops 10000000000 | bytes 10000000 | tf_op jit(solution)/shard_map/attention_back/pallas_call | solution.py:803
  91.4 3.2 %collective-permute-done.4.got_ref = bf16[384,384]{1,0:T(8,128)(2,1)S(1)} collective-permute-done((bf16[384,384]{1,0:T(8,128)(2,1)}, bf16[384,384]{1,0:T(8,128)(2,1)S(1)}, u32[]{:S(2)}, u32[]{:S(2)}) %collective-permute-start.4) | collective-permute-done | bytes 294944 | tf_op jit(solution)/shard_map/ppermute | solution.py:845
  95.8 3.8 %small_grads.1 = (bf16[48,384]{1,0:T(8,128)(2,1)S(1)}, f32[192,768]{1,0:T(8,128)S(1)}, f32[192,768]{1,0:T(8,128)S(1)}) custom-call(s32[1]{0:T(128)} %bitcast.1.half_ref, f32[18,8,256]{2,1,0:T(8,128)S(1)} %get-tuple-element.87.folded_ref, f32[8,256]{1,0:T(8,128)S(1)} %get-tuple-element.88.edge_ref, f32[16,768]{1,0:T(8,128)S(1)} %get-tuple-element.89.router_grad_ref, ...), custom_call_target="tpu_custom_call" | custom-call | flops 1000 | bytes 1000 | tf_op jit(solution)/shard_map/small_grads/pallas_call | solution.py:878
  99.6 2.6 %collective-permute-start.9 = (bf16[192,384]{1,0:T(8,128)(2,1)S(1)}, bf16[192,384]{1,0:T(8,128)(2,1)S(1)}, u32[]{:S(2)}, u32[]{:S(2)}) collective-permute-start(bf16[192,384]{1,0:T(8,128)(2,1)S(1)} %get-tuple-element.104), channel_id=1, source_target_pairs={{0,16},{1,17},{2,18},{3,19},{4,20},{5,21},{6,22},{7,23},{8,24},{9,... | collective-permute-start | bytes 442376 | tf_op jit(solution)/shard_map/ppermute | solution.py:845
  102.2 7.7 %collective-permute-done.9.got_ref = bf16[192,384]{1,0:T(8,128)(2,1)S(1)} collective-permute-done((bf16[192,384]{1,0:T(8,128)(2,1)S(1)}, bf16[192,384]{1,0:T(8,128)(2,1)S(1)}, u32[]{:S(2)}, u32[]{:S(2)}) %collective-permute-start.9) | collective-permute-done | bytes 147488 | tf_op jit(solution)/shard_map/ppermute | solution.py:845
  112.0 3.4 %collective-permute-start.11 = (bf16[48,1152]{1,0:T(8,128)(2,1)S(1)}, bf16[48,1152]{1,0:T(8,128)(2,1)S(1)}, u32[]{:S(2)}, u32[]{:S(2)}) collective-permute-start(bf16[48,1152]{1,0:T(8,128)(2,1)S(1)} %get-tuple-element.109), channel_id=1, source_target_pairs={{0,16},{1,17},{2,18},{3,19},{4,20},{5,21},{6,22},{7,23},{8,24},{9,... | collective-permute-start | bytes 331784 | tf_op jit(solution)/shard_map/ppermute | solution.py:845
  120.8 2.4 %collective-permute-start.12 = (bf16[48,1152]{1,0:T(8,128)(2,1)S(1)}, bf16[48,1152]{1,0:T(8,128)(2,1)S(1)}, u32[]{:S(2)}, u32[]{:S(2)}) collective-permute-start(bf16[48,1152]{1,0:T(8,128)(2,1)S(1)} %get-tuple-element.110), channel_id=1, source_target_pairs={{0,24},{1,25},{2,26},{3,27},{4,28},{5,29},{6,30},{7,31},{8,16},{9,... | collective-permute-start | bytes 331784 | tf_op jit(solution)/shard_map/ppermute | solution.py:845
  123.2 4.1 %collective-permute-done.12.s3_ref = bf16[48,1152]{1,0:T(8,128)(2,1)S(1)} collective-permute-done((bf16[48,1152]{1,0:T(8,128)(2,1)S(1)}, bf16[48,1152]{1,0:T(8,128)(2,1)S(1)}, u32[]{:S(2)}, u32[]{:S(2)}) %collective-permute-start.12) | collective-permute-done | bytes 110624 | tf_op jit(solution)/shard_map/ppermute | solution.py:845
  127.5 2.5 %collective-permute-start.18 = (bf16[48,1152]{1,0:T(8,128)(2,1)S(1)}, bf16[48,1152]{1,0:T(8,128)(2,1)S(1)}, u32[]{:S(2)}, u32[]{:S(2)}) collective-permute-start(bf16[48,1152]{1,0:T(8,128)(2,1)S(1)} %get-tuple-element.112.t0_ref), channel_id=1, source_target_pairs={{0,24},{1,25},{2,26},{3,27},{4,28},{5,29},{6,30},{7,31},{8,16},{9,... | collective-permute-start | bytes 331784 | tf_op jit(solution)/shard_map/ppermute | solution.py:845
  135.4 2.9 %collective-permute-done.17.t2_ref = bf16[48,1152]{1,0:T(8,128)(2,1)S(1)} collective-permute-done((bf16[48,1152]{1,0:T(8,128)(2,1)S(1)}, bf16[48,1152]{1,0:T(8,128)(2,1)S(1)}, u32[]{:S(2)}, u32[]{:S(2)}) %collective-permute-start.17) | collective-permute-done | bytes 110624 | tf_op jit(solution)/shard_map/ppermute | solution.py:845
  143.1 6.0 %collective-permute-done.23.b_ref.c2_ref = bf16[240,384]{1,0:T(8,128)(2,1)S(1)} collective-permute-done((bf16[240,384]{1,0:T(8,128)(2,1)S(1)}, bf16[240,384]{1,0:T(8,128)(2,1)S(1)}, u32[]{:S(2)}, u32[]{:S(2)}) %collective-permute-start.23) | collective-permute-done | bytes 184352 | tf_op jit(solution)/shard_map/ppermute | solution.py:845
  149.2 4.4 %collective-permute-done.22.a3_ref = bf16[192,1152]{1,0:T(8,128)(2,1)S(1)} collective-permute-done((bf16[192,1152]{1,0:T(8,128)(2,1)S(1)}, bf16[192,1152]{1,0:T(8,128)(2,1)S(1)}, u32[]{:S(2)}, u32[]{:S(2)}) %collective-permute-start.22) | collective-permute-done | bytes 442400 | tf_op jit(solution)/shard_map/ppermute | solution.py:845
  153.6 8.2 %collective-permute-done.21.a2_ref = bf16[192,1152]{1,0:T(8,128)(2,1)S(1)} collective-permute-done((bf16[192,1152]{1,0:T(8,128)(2,1)S(1)}, bf16[192,1152]{1,0:T(8,128)(2,1)S(1)}, u32[]{:S(2)}, u32[]{:S(2)}) %collective-permute-start.21) | collective-permute-done | bytes 442400 | tf_op jit(solution)/shard_map/ppermute | solution.py:845
  162.0 3.9 %unpack.1 = (f32[16,768]{1,0:T(8,128)}, f32[768]{0:T(1024)}, f32[768]{0:T(1024)}, f32[6,32]{1,0:T(8,128)}, f32[3,768,384]{2,1,0:T(8,128)}, /*index=5*/f32[384,768]{1,0:T(8,128)}) custom-call(s32[2]{0:T(128)S(1)} %pad_add_fusion.bits_ref, bf16[192,1152]{1,0:T(8,128)(2,1)S(1)} %get-tuple-element.115.a0_ref, ...), custom_call_target="tpu_custom_call" | custom-call | flops 1000 | bytes 1000 | tf_op jit(solution)/shard_map/unpack/pallas_call | solution.py:945
  (82 shorter events, 31.5 us)
Async XLA Ops:
  0.6 11.1 %collective-permute-start = (bf16[192,768]{1,0:T(8,128)(2,1)}, bf16[192,768]{1,0:T(8,128)(2,1)S(1)}, u32[]{:S(2)}, u32[]{:S(2)}) collective-permute-start(bf16[192,768]{1,0:T(8,128)(2,1)} %x_ref.5), channel_id=1, source_target_pairs={{0,1},{1,0},{2,3},{3,2},{4,5},{5,4},{6,7},{7,6},{8,9},{9,8},{10,11... | collective-permute-start | bytes 884744 | tf_op jit(solution)/shard_map/ppermute | solution.py:657
  3.8 21.1 %all-to-all-start = ((bf16[16,16,768]{2,1,0:T(8,128)(2,1)}), bf16[16,16,768]{2,1,0:T(8,128)(2,1)S(1)}, u32[]{:S(2)}, u32[]{:S(2)}) async-start(bf16[16,16,768]{2,1,0:T(8,128)(2,1)} %bitcast.30), calls=%async_computation | async-start | bytes 786432 | tf_op jit(solution)/shard_map/all_to_all | solution.py:660
  52.5 16.8 %all-to-all-start.2 = ((bf16[16,16,768]{2,1,0:T(8,128)(2,1)}), bf16[16,16,768]{2,1,0:T(8,128)(2,1)S(1)}, u32[]{:S(2)}, u32[]{:S(2)}) async-start(bf16[16,16,768]{2,1,0:T(8,128)(2,1)} %bitcast.10), calls=%async_computation.2 | async-start | bytes 786432 | tf_op jit(solution)/shard_map/all_to_all | solution.py:660
  71.9 18.3 %all-to-all-start.3 = ((bf16[16,16,768]{2,1,0:T(8,128)(2,1)}), bf16[16,16,768]{2,1,0:T(8,128)(2,1)S(1)}, u32[]{:S(2)}, u32[]{:S(2)}) async-start(bf16[16,16,768]{2,1,0:T(8,128)(2,1)} %bitcast.29), calls=%async_computation.3 | async-start | bytes 786432 | tf_op jit(solution)/shard_map/all_to_all | solution.py:660
  85.2 9.4 %collective-permute-start.4 = (bf16[384,384]{1,0:T(8,128)(2,1)}, bf16[384,384]{1,0:T(8,128)(2,1)S(1)}, u32[]{:S(2)}, u32[]{:S(2)}) collective-permute-start(bf16[384,384]{1,0:T(8,128)(2,1)} %get-tuple-element.92), channel_id=1, source_target_pairs={{0,8},{1,9},{2,10},{3,11},{4,12},{5,13},{6,14},{7,15},{8,0},{9,1},... | collective-permute-start | bytes 884744 | tf_op jit(solution)/shard_map/ppermute | solution.py:845
  87.2 22.8 %collective-permute-start.7 = (bf16[192,1152]{1,0:T(8,128)(2,1)}, bf16[192,1152]{1,0:T(8,128)(2,1)S(1)}, u32[]{:S(2)}, u32[]{:S(2)}) collective-permute-start(bf16[192,1152]{1,0:T(8,128)(2,1)} %get-tuple-element.102), channel_id=1, source_target_pairs={{0,4},{1,5},{2,6},{3,7},{4,0},{5,1},{6,2},{7,3},{8,12},{9,13},{10,... | collective-permute-start | bytes 1327112 | tf_op jit(solution)/shard_map/ppermute | solution.py:845
  88.7 21.3 %collective-permute-start.8 = (bf16[192,1152]{1,0:T(8,128)(2,1)}, bf16[192,1152]{1,0:T(8,128)(2,1)S(1)}, u32[]{:S(2)}, u32[]{:S(2)}) collective-permute-start(bf16[192,1152]{1,0:T(8,128)(2,1)} %get-tuple-element.103), channel_id=1, source_target_pairs={{0,6},{1,7},{2,4},{3,5},{4,2},{5,3},{6,0},{7,1},{8,14},{9,15},{10,... | collective-permute-start | bytes 1327112 | tf_op jit(solution)/shard_map/ppermute | solution.py:845
  90.9 19.1 %collective-permute-start.6 = (bf16[192,1152]{1,0:T(8,128)(2,1)}, bf16[192,1152]{1,0:T(8,128)(2,1)S(1)}, u32[]{:S(2)}, u32[]{:S(2)}) collective-permute-start(bf16[192,1152]{1,0:T(8,128)(2,1)} %order.1), channel_id=1, source_target_pairs={{0,2},{1,3},{2,0},{3,1},{4,6},{5,7},{6,4},{7,5},{8,10},{9,11},{10,... | collective-permute-start | bytes 1327112 | tf_op jit(solution)/shard_map/ppermute | solution.py:845
  99.5 32.4 %collective-permute-start.5 = (f32[192,768]{1,0:T(8,128)S(1)}, f32[192,768]{1,0:T(8,128)S(1)}, u32[]{:S(2)}, u32[]{:S(2)}) collective-permute-start(f32[192,768]{1,0:T(8,128)S(1)} %get-tuple-element.97), channel_id=1, source_target_pairs={{0,1},{1,0},{2,3},{3,2},{4,5},{5,4},{6,7},{7,6},{8,9},{9,8},{10,11... | collective-permute-start | bytes 1769480 | tf_op jit(solution)/shard_map/ppermute | solution.py:657
  99.6 10.3 %collective-permute-start.9 = (bf16[192,384]{1,0:T(8,128)(2,1)S(1)}, bf16[192,384]{1,0:T(8,128)(2,1)S(1)}, u32[]{:S(2)}, u32[]{:S(2)}) collective-permute-start(bf16[192,384]{1,0:T(8,128)(2,1)S(1)} %get-tuple-element.104), channel_id=1, source_target_pairs={{0,16},{1,17},{2,18},{3,19},{4,20},{5,21},{6,22},{7,23},{8,24},{9,... | collective-permute-start | bytes 442376 | tf_op jit(solution)/shard_map/ppermute | solution.py:845
  111.3 7.0 %collective-permute-start.10 = (bf16[48,1152]{1,0:T(8,128)(2,1)S(1)}, bf16[48,1152]{1,0:T(8,128)(2,1)S(1)}, u32[]{:S(2)}, u32[]{:S(2)}) collective-permute-start(bf16[48,1152]{1,0:T(8,128)(2,1)S(1)} %get-tuple-element.108), channel_id=1, source_target_pairs={{0,8},{1,9},{2,10},{3,11},{4,12},{5,13},{6,14},{7,15},{8,0},{9,1},... | collective-permute-start | bytes 331784 | tf_op jit(solution)/shard_map/ppermute | solution.py:845
  112.0 8.8 %collective-permute-start.11 = (bf16[48,1152]{1,0:T(8,128)(2,1)S(1)}, bf16[48,1152]{1,0:T(8,128)(2,1)S(1)}, u32[]{:S(2)}, u32[]{:S(2)}) collective-permute-start(bf16[48,1152]{1,0:T(8,128)(2,1)S(1)} %get-tuple-element.109), channel_id=1, source_target_pairs={{0,16},{1,17},{2,18},{3,19},{4,20},{5,21},{6,22},{7,23},{8,24},{9,... | collective-permute-start | bytes 331784 | tf_op jit(solution)/shard_map/ppermute | solution.py:845
  115.3 12.0 %collective-permute-start.15 = (bf16[240,384]{1,0:T(8,128)(2,1)S(1)}, bf16[240,384]{1,0:T(8,128)(2,1)S(1)}, u32[]{:S(2)}, u32[]{:S(2)}) collective-permute-start(bf16[240,384]{1,0:T(8,128)(2,1)S(1)} %get-tuple-element.111.e0_ref), channel_id=1, source_target_pairs={{0,6},{1,7},{2,4},{3,5},{4,2},{5,3},{6,0},{7,1},{8,14},{9,15},{10,... | collective-permute-start | bytes 552968 | tf_op jit(solution)/shard_map/ppermute | solution.py:845
  117.7 9.6 %collective-permute-start.14 = (bf16[240,384]{1,0:T(8,128)(2,1)S(1)}, bf16[240,384]{1,0:T(8,128)(2,1)S(1)}, u32[]{:S(2)}, u32[]{:S(2)}) collective-permute-start(bf16[240,384]{1,0:T(8,128)(2,1)S(1)} %get-tuple-element.111.e0_ref), channel_id=1, source_target_pairs={{0,4},{1,5},{2,6},{3,7},{4,0},{5,1},{6,2},{7,3},{8,12},{9,13},{10,... | collective-permute-start | bytes 552968 | tf_op jit(solution)/shard_map/ppermute | solution.py:845
  118.3 9.0 %collective-permute-start.13 = (bf16[240,384]{1,0:T(8,128)(2,1)S(1)}, bf16[240,384]{1,0:T(8,128)(2,1)S(1)}, u32[]{:S(2)}, u32[]{:S(2)}) collective-permute-start(bf16[240,384]{1,0:T(8,128)(2,1)S(1)} %get-tuple-element.111.e0_ref), channel_id=1, source_target_pairs={{0,2},{1,3},{2,0},{3,1},{4,6},{5,7},{6,4},{7,5},{8,10},{9,11},{10,... | collective-permute-start | bytes 552968 | tf_op jit(solution)/shard_map/ppermute | solution.py:845
  120.8 6.5 %collective-permute-start.12 = (bf16[48,1152]{1,0:T(8,128)(2,1)S(1)}, bf16[48,1152]{1,0:T(8,128)(2,1)S(1)}, u32[]{:S(2)}, u32[]{:S(2)}) collective-permute-start(bf16[48,1152]{1,0:T(8,128)(2,1)S(1)} %get-tuple-element.110), channel_id=1, source_target_pairs={{0,24},{1,25},{2,26},{3,27},{4,28},{5,29},{6,30},{7,31},{8,16},{9,... | collective-permute-start | bytes 331784 | tf_op jit(solution)/shard_map/ppermute | solution.py:845
  127.5 7.9 %collective-permute-start.18 = (bf16[48,1152]{1,0:T(8,128)(2,1)S(1)}, bf16[48,1152]{1,0:T(8,128)(2,1)S(1)}, u32[]{:S(2)}, u32[]{:S(2)}) collective-permute-start(bf16[48,1152]{1,0:T(8,128)(2,1)S(1)} %get-tuple-element.112.t0_ref), channel_id=1, source_target_pairs={{0,24},{1,25},{2,26},{3,27},{4,28},{5,29},{6,30},{7,31},{8,16},{9,... | collective-permute-start | bytes 331784 | tf_op jit(solution)/shard_map/ppermute | solution.py:845
  130.0 8.3 %collective-permute-start.17 = (bf16[48,1152]{1,0:T(8,128)(2,1)S(1)}, bf16[48,1152]{1,0:T(8,128)(2,1)S(1)}, u32[]{:S(2)}, u32[]{:S(2)}) collective-permute-start(bf16[48,1152]{1,0:T(8,128)(2,1)S(1)} %get-tuple-element.112.t0_ref), channel_id=1, source_target_pairs={{0,16},{1,17},{2,18},{3,19},{4,20},{5,21},{6,22},{7,23},{8,24},{9,... | collective-permute-start | bytes 331784 | tf_op jit(solution)/shard_map/ppermute | solution.py:845
  130.0 8.3 %collective-permute-start.16 = (bf16[48,1152]{1,0:T(8,128)(2,1)S(1)}, bf16[48,1152]{1,0:T(8,128)(2,1)S(1)}, u32[]{:S(2)}, u32[]{:S(2)}) collective-permute-start(bf16[48,1152]{1,0:T(8,128)(2,1)S(1)} %get-tuple-element.112.t0_ref), channel_id=1, source_target_pairs={{0,8},{1,9},{2,10},{3,11},{4,12},{5,13},{6,14},{7,15},{8,0},{9,1},... | collective-permute-start | bytes 331784 | tf_op jit(solution)/shard_map/ppermute | solution.py:845
  139.4 9.7 %collective-permute-start.23 = (bf16[240,384]{1,0:T(8,128)(2,1)S(1)}, bf16[240,384]{1,0:T(8,128)(2,1)S(1)}, u32[]{:S(2)}, u32[]{:S(2)}) collective-permute-start(bf16[240,384]{1,0:T(8,128)(2,1)S(1)} %get-tuple-element.116.a_ref.c0_ref), channel_id=1, source_target_pairs={{0,16},{1,17},{2,18},{3,19},{4,20},{5,21},{6,22},{7,23},{8,24},{9,... | collective-permute-start | bytes 552968 | tf_op jit(solution)/shard_map/ppermute | solution.py:845
  139.6 14.0 %collective-permute-start.22 = (bf16[192,1152]{1,0:T(8,128)(2,1)S(1)}, bf16[192,1152]{1,0:T(8,128)(2,1)S(1)}, u32[]{:S(2)}, u32[]{:S(2)}) collective-permute-start(bf16[192,1152]{1,0:T(8,128)(2,1)S(1)} %get-tuple-element.115.a0_ref), channel_id=1, source_target_pairs={{0,6},{1,7},{2,4},{3,5},{4,2},{5,3},{6,0},{7,1},{8,14},{9,15},{10,... | collective-permute-start | bytes 1327112 | tf_op jit(solution)/shard_map/ppermute | solution.py:845
  141.4 20.4 %collective-permute-start.21 = (bf16[192,1152]{1,0:T(8,128)(2,1)S(1)}, bf16[192,1152]{1,0:T(8,128)(2,1)S(1)}, u32[]{:S(2)}, u32[]{:S(2)}) collective-permute-start(bf16[192,1152]{1,0:T(8,128)(2,1)S(1)} %get-tuple-element.115.a0_ref), channel_id=1, source_target_pairs={{0,4},{1,5},{2,6},{3,7},{4,0},{5,1},{6,2},{7,3},{8,12},{9,13},{10,... | collective-permute-start | bytes 1327112 | tf_op jit(solution)/shard_map/ppermute | solution.py:845
  142.7 19.2 %collective-permute-start.20 = (bf16[192,1152]{1,0:T(8,128)(2,1)S(1)}, bf16[192,1152]{1,0:T(8,128)(2,1)S(1)}, u32[]{:S(2)}, u32[]{:S(2)}) collective-permute-start(bf16[192,1152]{1,0:T(8,128)(2,1)S(1)} %get-tuple-element.115.a0_ref), channel_id=1, source_target_pairs={{0,2},{1,3},{2,0},{3,1},{4,6},{5,7},{6,4},{7,5},{8,10},{9,11},{10,... | collective-permute-start | bytes 1327112 | tf_op jit(solution)/shard_map/ppermute | solution.py:845
  149.1 12.8 %collective-permute-start.24 = (bf16[480,384]{1,0:T(8,128)(2,1)S(1)}, bf16[480,384]{1,0:T(8,128)(2,1)S(1)}, u32[]{:S(2)}, u32[]{:S(2)}) collective-permute-start(bf16[480,384]{1,0:T(8,128)(2,1)S(1)} %stack.13), channel_id=1, source_target_pairs={{0,8},{1,9},{2,10},{3,11},{4,12},{5,13},{6,14},{7,15},{8,0},{9,1},... | collective-permute-start | bytes 1105928 | tf_op jit(solution)/shard_map/ppermute | solution.py:845
  (18 other events, 265.9 us)

commit v3 on v2

--- a/solution.py
+++ b/solution.py
@@ -536,25 +536,31 @@
 
 def fold_first_body(
     a1_ref, a2_ref, a3_ref, c0_ref, got_ref, a0_hbm, small_ref,
-    s0_ref, s1_ref, s2_ref, s3_ref, e_ref,
+    s0_ref, s2_ref, near_ref, e_ref,
     a0_ref, sem,
 ):
     load = pltpu.make_async_copy(a0_hbm, a0_ref, sem)
     load.start()
     load.wait()
     shard, lead = s0_ref.shape[0], small_ref.shape[0]
-    for d, target in enumerate((s0_ref, s1_ref, s2_ref, s3_ref)):
+    for d, target in enumerate((s0_ref, near_ref.at[:shard], s2_ref, near_ref.at[shard:])):
         at = slice(d * shard, (d + 1) * shard)
         target[...] = pairs_of(a0_ref[at], a1_ref[at], a2_ref[at], a3_ref[at])
     e_ref[:lead] = small_ref[...]
     e_ref[lead:] = total_of(c0_ref[...], got_ref[...])
 
 
+def fold_z_body(got_ref, s0_ref, s2_ref, s0_out, s2_out):
+    size = s0_ref.shape[0]
+    s0_out[...] = total_of(s0_ref[...], got_ref[:size])
+    s2_out[...] = total_of(s2_ref[...], got_ref[size:])
+
+
 def fold_last_body(
-    s0_ref, s1_ref, s2_ref, s3_ref, e0_ref, e1_ref, e2_ref, e3_ref, total_ref, c_ref, small_ref
+    s0_ref, got_ref, e0_ref, e1_ref, e2_ref, e3_ref, total_ref, c_ref, small_ref
 ):
     lead = small_ref.shape[0]
-    total_ref[...] = pairs_of(s0_ref[...], s1_ref[...], s2_ref[...], s3_ref[...])
+    total_ref[...] = total_of(s0_ref[...], got_ref[...])
     small_ref[...] = pairs_of(e0_ref[:lead], e1_ref[:lead], e2_ref[:lead], e3_ref[:lead])
     c_ref[...] = pairs_of(e0_ref[lead:], e1_ref[lead:], e2_ref[lead:], e3_ref[lead:])
 
@@ -661,6 +667,16 @@
             value.reshape(experts, capacity, width), "expert", split_axis=0, concat_axis=0, tiled=True
         ).reshape(slots, width)
 
+    def ordered(value, after):
+        return pl.pallas_call(
+            order_body,
+            out_shape=hbm(value.shape, value.dtype),
+            in_specs=[ANY, ANY],
+            out_specs=ANY,
+            input_output_aliases={0: 0},
+            name="order",
+        )(value, after)
+
     x_other = swap(tokens)
     place, cot_slots = pl.pallas_call(
         functools.partial(prep_body, capacity, experts),
@@ -831,14 +847,7 @@
         half_one, position, grad_low, grad_other, in_hbm(w_out), in_hbm(qkv), in_hbm(probs), in_hbm(context),
         in_hbm(normed),
     )
-    a1 = pl.pallas_call(
-        order_body,
-        out_shape=hbm(a1.shape, BF),
-        in_specs=[ANY, ANY],
-        out_specs=ANY,
-        input_output_aliases={0: 0},
-        name="order",
-    )(a1, scaled_rows)
+    a1 = ordered(a1, scaled_rows)
 
     def moves(flip):
         pairs = [(2 * e + t, 2 * (e ^ flip) + t) for e in range(sources) for t in range(2)]
@@ -906,23 +915,26 @@
         name="token_outputs",
     )(place, scaled_rows, residual, own_gn, got_gn, tokens, gain_a, grad_res, c0)
 
-    *parts_z, part_c = pl.pallas_call(
+    s0, s2, s_near, part_c = pl.pallas_call(
         fold_first_body,
-        out_shape=shape_of(*[((shard, wide), BF)] * 4, ((lead + 4 * shard, local), BF)),
+        out_shape=shape_of(
+            *[((shard, wide), BF)] * 2, ((2 * shard, wide), BF), ((lead + 4 * shard, local), BF)
+        ),
         in_specs=vmem_specs(5) + [ANY] + vmem_specs(1),
-        out_specs=vmem_specs(5),
+        out_specs=vmem_specs(4),
         scratch_shapes=[pltpu.VMEM(big, BF), pltpu.SemaphoreType.DMA],
         compiler_params=params(8),
         cost_estimate=cost(1e3, 1e3),
         name="fold_first",
     )(*got_a, c0, got_c, in_hbm(a0), small)
-    got_z = [along[d](parts_z[d + 1]) for d in range(3)]
+    s0, s2 = fused("fold_z", fold_z_body, [((shard, wide), BF)] * 2, (along[0](s_near), s0, s2))
+    got_z = along[1](s2)
     got_e = [flat[d](part_c) for d in range(3)]
     total, c_full, small = fused(
         "fold_last",
         fold_last_body,
         [((shard, wide), BF), (slab, BF), ((lead, local), BF)],
-        (parts_z[0], *got_z, part_c, *got_e),
+        (s0, got_z, part_c, *got_e),
     )
     for b in range(4, sources.bit_length() - 1):
         further = moves(1 << b)

time: 167 us -> 161 us (0.964)
  waiting for transfers between devices: 50.6 us -> 46.9 us
  starting transfers between devices: 43.1 us -> 39.9 us
    ppermute x19 -> x18, waiting for transfers between devices: 40.4 us -> 36.7 us  [moves(): return lambda value: lax.ppermute(value, ('expert', 'tensor'), pairs)]
    ppermute x19 -> x18, starting transfers between devices: 26.6 us -> 23.4 us  [moves(): return lambda value: lax.ppermute(value, ('expert', 'tensor'), pairs)]
  transfers between devices with their start and end apart: 28 -> 27, of which waited for: 13 -> 16; matrix products, arithmetic and copies ran while one was open for 0% -> 0% of each run, Pallas kernels for 21% -> 22%
where the time goes in v3:
time: 161 us; the launch traced here: 159 us
  Pallas kernels  52.2 us (32%)
  waiting for transfers between devices  46.9 us (29%)
  starting transfers between devices  39.9 us (25%)
  blocking collectives  16.9 us (10%)
  local copies, waits for them, and re-layouts  2.04 us (1%)
    ppermute x18, waiting for transfers between devices, moves(): return lambda value: lax.ppermute(value, ('expert', 'tensor'), pairs)  36.7 us
    ppermute x18, starting transfers between devices, moves(): return lambda value: lax.ppermute(value, ('expert', 'tensor'), pairs)  23.4 us
    all_to_all x1, blocking collectives, exchange(): lax.all_to_all(value.reshape(experts, capacity, width), 'expert', split_a...  16.9 us
    all_to_all x3, starting transfers between devices, exchange(): lax.all_to_all(value.reshape(experts, capacity, width), 'expert', split_a...  15.5 us
    pallas_call x1, Pallas kernels, per_device(): pl.pallas_call(attend_back_body, out_shape=(*shape_of(((3 * heads, 8, 2 *...  9.49 us
    pallas_call x1, Pallas kernels, per_device(): pl.pallas_call(expert_body, out_shape=shape_of(((count, width), BF), ((ex...  9.27 us
    all_to_all x3, waiting for transfers between devices, exchange(): lax.all_to_all(value.reshape(experts, capacity, width), 'expert', split_a...  9.12 us
    pallas_call x1, Pallas kernels, per_device(): pl.pallas_call(attend_body, out_shape=shape_of(((rows, width), F32), ((ro...  8.25 us
  transfers between devices with their start and end apart: 27, of which 16 were waited for; matrix products, arithmetic and copies ran while one was open for 0% of the time, Pallas kernels for 22%

profile of v3, /device:TPU:0, one launch (start us, length us, event | category | flops | bytes accessed | tf_op | source)
XLA Modules:
  0.0 159.1 jit_solution(5674163080361282221)
XLA Ops:
  1.2 2.6 %place_cotangent.1 = (bf16[256,192]{1,0:T(8,128)(2,1)}, bf16[256,768]{1,0:T(8,128)(2,1)}) custom-call(s32[1,192]{1,0:T(1,128)} %bitcast.36, bf16[192,768]{1,0:T(8,128)(2,1)} %cot_hbm.1), custom_call_target="tpu_custom_call" | custom-call | flops 2000000000 | bytes 1000000 | tf_op jit(solution)/shard_map/place_cotangent/pallas_call | solution.py:681
  3.8 7.9 %all-to-all-start = ((bf16[16,16,768]{2,1,0:T(8,128)(2,1)}), bf16[16,16,768]{2,1,0:T(8,128)(2,1)S(1)}, u32[]{:S(2)}, u32[]{:S(2)}) async-start(bf16[16,16,768]{2,1,0:T(8,128)(2,1)} %bitcast.30), calls=%async_computation | async-start | bytes 786432 | tf_op jit(solution)/shard_map/all_to_all | solution.py:666
  11.8 8.2 %attention.1 = (f32[192,768]{1,0:T(8,128)S(1)}, f32[192,768]{1,0:T(8,128)S(1)}, bf16[384,384]{1,0:T(8,128)(2,1)}, bf16[384,1152]{1,0:T(8,128)(2,1)}, bf16[6,384,...) custom-call(s32[1]{0:T(128)} %bitcast.1.half_ref, s32[1,3]{1,0:T(1,128)S(1)} %copy-done.9, bf16[192,768]{1,0:T(8,128)(2,1)S(1)} %copy-done.3, ...), custom_call_target="tpu_custom_call" | custom-call | flops 8000000000 | bytes 4000000 | tf_op jit(solution)/shard_map/attention/pallas_call | solution.py:693
  20.5 4.4 %all-to-all-done = bf16[16,16,768]{2,1,0:T(8,128)(2,1)S(1)} async-done(((bf16[16,16,768]{2,1,0:T(8,128)(2,1)}), bf16[16,16,768]{2,1,0:T(8,128)(2,1)S(1)}, u32[]{:S(2)}, u32[]{:S(2)}) %all-to-all-start) | async-done | bytes 393248 | tf_op jit(solution)/shard_map/all_to_all | solution.py:666
  26.3 16.9 %all_to_all.20 = bf16[16,16,768]{2,1,0:T(8,128)(2,1)S(1)} all-to-all(bf16[16,16,768]{2,1,0:T(8,128)(2,1)S(1)} %bitcast.27), channel_id=1, replica_groups=mesh['expert'=16,'tensor'=2] {'expert'}, dimensions={0} | all-to-all | bytes 786432 | tf_op jit(solution)/shard_map/all_to_all | solution.py:666
  43.1 9.3 %expert.1 = (bf16[256,768]{1,0:T(8,128)(2,1)}, f32[16,768]{1,0:T(8,128)S(1)}, bf16[256,768]{1,0:T(8,128)(2,1)}, bf16[256,768]{1,0:T(8,128)(2,1)}, bf16[256,4608]...) custom-call(s32[1]{0:T(128)} %bitcast.1.half_ref, s32[1]{0:T(128)} %bitcast.2._expert.expert_ref, ...), custom_call_target="tpu_custom_call" | custom-call | flops 10000000000 | bytes 14000000 | tf_op jit(solution)/shard_map/expert/pallas_call | solution.py:743
  52.5 3.8 %all-to-all-start.2 = ((bf16[16,16,768]{2,1,0:T(8,128)(2,1)}), bf16[16,16,768]{2,1,0:T(8,128)(2,1)S(1)}, u32[]{:S(2)}, u32[]{:S(2)}) async-start(bf16[16,16,768]{2,1,0:T(8,128)(2,1)} %bitcast.10), calls=%async_computation.2 | async-start | bytes 786432 | tf_op jit(solution)/shard_map/all_to_all | solution.py:666
  57.4 7.2 %expert_grads.1 = (f32[1536,768]{1,0:T(8,128)}, f32[768,1536]{1,0:T(8,128)}) custom-call(bf16[256,1536]{1,0:T(8,128)(2,1)} %get-tuple-element.77.act_ref, bf16[256,1536]{1,0:T(8,128)(2,1)} %get-tuple-element.78.pre_ref, bf16[256,768]{1,0:T(8,128)(2,1)S(1)} %bitcast.26, bf16[256,768]{1,0:T(8,128)(2,1)} %get-tuple-element.79.gp_ref, ...), custom_call_target="tpu_custom_call" | custom-call | flops 5000000000 | bytes 14000000 | tf_op jit(solution)/shard_map/expert_grads/pallas_call | solution.py:777
  64.6 4.8 %all-to-all-done.2 = bf16[16,16,768]{2,1,0:T(8,128)(2,1)S(1)} async-done(((bf16[16,16,768]{2,1,0:T(8,128)(2,1)}), bf16[16,16,768]{2,1,0:T(8,128)(2,1)S(1)}, u32[]{:S(2)}, u32[]{:S(2)}) %all-to-all-start.2) | async-done | bytes 393248 | tf_op jit(solution)/shard_map/all_to_all | solution.py:666
  71.9 3.8 %all-to-all-start.3 = ((bf16[16,16,768]{2,1,0:T(8,128)(2,1)}), bf16[16,16,768]{2,1,0:T(8,128)(2,1)S(1)}, u32[]{:S(2)}, u32[]{:S(2)}) async-start(bf16[16,16,768]{2,1,0:T(8,128)(2,1)} %bitcast.29), calls=%async_computation.3 | async-start | bytes 786432 | tf_op jit(solution)/shard_map/all_to_all | solution.py:666
  75.7 9.5 %attention_back.1 = (f32[18,8,256]{2,1,0:T(8,128)S(1)}, f32[8,256]{1,0:T(8,128)S(1)}, bf16[192,1152]{1,0:T(8,128)(2,1)}, bf16[192,1152]{1,0:T(8,128)(2,1)}, bf16...) custom-call(s32[1]{0:T(128)} %bitcast.1.half_ref, ...), custom_call_target="tpu_custom_call" | custom-call | flops 10000000000 | bytes 10000000 | tf_op jit(solution)/shard_map/attention_back/pallas_call | solution.py:819
  91.4 3.2 %collective-permute-done.4.got_ref = bf16[384,384]{1,0:T(8,128)(2,1)S(1)} collective-permute-done((bf16[384,384]{1,0:T(8,128)(2,1)}, bf16[384,384]{1,0:T(8,128)(2,1)S(1)}, u32[]{:S(2)}, u32[]{:S(2)}) %collective-permute-start.4) | collective-permute-done | bytes 294944 | tf_op jit(solution)/shard_map/ppermute | solution.py:854
  95.7 2.6 %collective-permute-start.9 = (bf16[192,384]{1,0:T(8,128)(2,1)S(1)}, bf16[192,384]{1,0:T(8,128)(2,1)S(1)}, u32[]{:S(2)}, u32[]{:S(2)}) collective-permute-start(bf16[192,384]{1,0:T(8,128)(2,1)S(1)} %get-tuple-element.105), channel_id=1, source_target_pairs={{0,16},{1,17},{2,18},{3,19},{4,20},{5,21},{6,22},{7,23},{8,24},{9,... | collective-permute-start | bytes 442376 | tf_op jit(solution)/shard_map/ppermute | solution.py:854
  98.3 3.8 %small_grads.1 = (bf16[48,384]{1,0:T(8,128)(2,1)S(1)}, f32[192,768]{1,0:T(8,128)S(1)}, f32[192,768]{1,0:T(8,128)S(1)}) custom-call(s32[1]{0:T(128)} %bitcast.1.half_ref, f32[18,8,256]{2,1,0:T(8,128)S(1)} %get-tuple-element.88.folded_ref, f32[8,256]{1,0:T(8,128)S(1)} %get-tuple-element.89.edge_ref, f32[16,768]{1,0:T(8,128)S(1)} %get-tuple-element.90.router_grad_ref, ...), custom_call_target="tpu_custom_call" | custom-call | flops 1000 | bytes 1000 | tf_op jit(solution)/shard_map/small_grads/pallas_call | solution.py:887
  102.2 2.8 %collective-permute-done.9.got_ref = bf16[192,384]{1,0:T(8,128)(2,1)S(1)} collective-permute-done((bf16[192,384]{1,0:T(8,128)(2,1)S(1)}, bf16[192,384]{1,0:T(8,128)(2,1)S(1)}, u32[]{:S(2)}, u32[]{:S(2)}) %collective-permute-start.9) | collective-permute-done | bytes 147488 | tf_op jit(solution)/shard_map/ppermute | solution.py:854
  105.0 3.6 %collective-permute-done.7.a2_ref = bf16[192,1152]{1,0:T(8,128)(2,1)S(1)} collective-permute-done((bf16[192,1152]{1,0:T(8,128)(2,1)}, bf16[192,1152]{1,0:T(8,128)(2,1)S(1)}, u32[]{:S(2)}, u32[]{:S(2)}) %collective-permute-start.7) | collective-permute-done | bytes 442400 | tf_op jit(solution)/shard_map/ppermute | solution.py:854
  111.6 2.5 %collective-permute-start.14 = (bf16[240,384]{1,0:T(8,128)(2,1)S(1)}, bf16[240,384]{1,0:T(8,128)(2,1)S(1)}, u32[]{:S(2)}, u32[]{:S(2)}) collective-permute-start(bf16[240,384]{1,0:T(8,128)(2,1)S(1)} %get-tuple-element.113.e0_ref), channel_id=1, source_target_pairs={{0,6},{1,7},{2,4},{3,5},{4,2},{5,3},{6,0},{7,1},{8,14},{9,15},{10,... | collective-permute-start | bytes 552968 | tf_op jit(solution)/shard_map/ppermute | solution.py:854
  117.2 2.6 %collective-permute-start.11 = (bf16[48,1152]{1,0:T(8,128)(2,1)S(1)}, bf16[48,1152]{1,0:T(8,128)(2,1)S(1)}, u32[]{:S(2)}, u32[]{:S(2)}) collective-permute-start(bf16[48,1152]{1,0:T(8,128)(2,1)S(1)} %get-tuple-element.112), channel_id=1, source_target_pairs={{0,16},{1,17},{2,18},{3,19},{4,20},{5,21},{6,22},{7,23},{8,24},{9,... | collective-permute-start | bytes 331784 | tf_op jit(solution)/shard_map/ppermute | solution.py:854
  121.6 2.9 %collective-permute-done.11.got_ref = bf16[48,1152]{1,0:T(8,128)(2,1)S(1)} collective-permute-done((bf16[48,1152]{1,0:T(8,128)(2,1)S(1)}, bf16[48,1152]{1,0:T(8,128)(2,1)S(1)}, u32[]{:S(2)}, u32[]{:S(2)}) %collective-permute-start.11) | collective-permute-done | bytes 110624 | tf_op jit(solution)/shard_map/ppermute | solution.py:854
  135.5 2.4 %collective-permute-start.21 = (bf16[192,1152]{1,0:T(8,128)(2,1)S(1)}, bf16[192,1152]{1,0:T(8,128)(2,1)S(1)}, u32[]{:S(2)}, u32[]{:S(2)}) collective-permute-start(bf16[192,1152]{1,0:T(8,128)(2,1)S(1)} %get-tuple-element.117.a0_ref), channel_id=1, source_target_pairs={{0,6},{1,7},{2,4},{3,5},{4,2},{5,3},{6,0},{7,1},{8,14},{9,15},{10,... | collective-permute-start | bytes 1327112 | tf_op jit(solution)/shard_map/ppermute | solution.py:854
  139.0 4.0 %collective-permute-done.22.b_ref.c2_ref = bf16[240,384]{1,0:T(8,128)(2,1)S(1)} collective-permute-done((bf16[240,384]{1,0:T(8,128)(2,1)S(1)}, bf16[240,384]{1,0:T(8,128)(2,1)S(1)}, u32[]{:S(2)}, u32[]{:S(2)}) %collective-permute-start.22) | collective-permute-done | bytes 184352 | tf_op jit(solution)/shard_map/ppermute | solution.py:854
  143.2 6.3 %collective-permute-done.21.a3_ref = bf16[192,1152]{1,0:T(8,128)(2,1)S(1)} collective-permute-done((bf16[192,1152]{1,0:T(8,128)(2,1)S(1)}, bf16[192,1152]{1,0:T(8,128)(2,1)S(1)}, u32[]{:S(2)}, u32[]{:S(2)}) %collective-permute-start.21) | collective-permute-done | bytes 442400 | tf_op jit(solution)/shard_map/ppermute | solution.py:854
  149.5 5.3 %collective-permute-done.20.a2_ref = bf16[192,1152]{1,0:T(8,128)(2,1)S(1)} collective-permute-done((bf16[192,1152]{1,0:T(8,128)(2,1)S(1)}, bf16[192,1152]{1,0:T(8,128)(2,1)S(1)}, u32[]{:S(2)}, u32[]{:S(2)}) %collective-permute-start.20) | collective-permute-done | bytes 442400 | tf_op jit(solution)/shard_map/ppermute | solution.py:854
  155.1 3.9 %unpack.1 = (f32[16,768]{1,0:T(8,128)}, f32[768]{0:T(1024)}, f32[768]{0:T(1024)}, f32[6,32]{1,0:T(8,128)}, f32[3,768,384]{2,1,0:T(8,128)}, /*index=5*/f32[384,768]{1,0:T(8,128)}) custom-call(s32[2]{0:T(128)S(1)} %pad_add_fusion.bits_ref, bf16[192,1152]{1,0:T(8,128)(2,1)S(1)} %get-tuple-element.117.a0_ref, ...), custom_call_target="tpu_custom_call" | custom-call | flops 1000 | bytes 1000 | tf_op jit(solution)/shard_map/unpack/pallas_call | solution.py:957
  (81 shorter events, 33.7 us)
Async XLA Ops:
  0.6 11.1 %collective-permute-start = (bf16[192,768]{1,0:T(8,128)(2,1)}, bf16[192,768]{1,0:T(8,128)(2,1)S(1)}, u32[]{:S(2)}, u32[]{:S(2)}) collective-permute-start(bf16[192,768]{1,0:T(8,128)(2,1)} %x_ref.5), channel_id=1, source_target_pairs={{0,1},{1,0},{2,3},{3,2},{4,5},{5,4},{6,7},{7,6},{8,9},{9,8},{10,11... | collective-permute-start | bytes 884744 | tf_op jit(solution)/shard_map/ppermute | solution.py:663
  3.8 21.1 %all-to-all-start = ((bf16[16,16,768]{2,1,0:T(8,128)(2,1)}), bf16[16,16,768]{2,1,0:T(8,128)(2,1)S(1)}, u32[]{:S(2)}, u32[]{:S(2)}) async-start(bf16[16,16,768]{2,1,0:T(8,128)(2,1)} %bitcast.30), calls=%async_computation | async-start | bytes 786432 | tf_op jit(solution)/shard_map/all_to_all | solution.py:666
  52.4 4.9 %collective-permute-start.2 = (bf16[256,4608]{1,0:T(8,128)(2,1)}, bf16[256,4608]{1,0:T(8,128)(2,1)}, u32[]{:S(2)}, u32[]{:S(2)}) collective-permute-start(bf16[256,4608]{1,0:T(8,128)(2,1)} %get-tuple-element.80), channel_id=1, source_target_pairs={{0,1},{1,0},{2,3},{3,2},{4,5},{5,4},{6,7},{7,6},{8,9},{9,8},{10,11... | collective-permute-start | bytes 7077896 | tf_op jit(solution)/shard_map/ppermute | solution.py:663
  52.5 16.8 %all-to-all-start.2 = ((bf16[16,16,768]{2,1,0:T(8,128)(2,1)}), bf16[16,16,768]{2,1,0:T(8,128)(2,1)S(1)}, u32[]{:S(2)}, u32[]{:S(2)}) async-start(bf16[16,16,768]{2,1,0:T(8,128)(2,1)} %bitcast.10), calls=%async_computation.2 | async-start | bytes 786432 | tf_op jit(solution)/shard_map/all_to_all | solution.py:666
  71.9 18.3 %all-to-all-start.3 = ((bf16[16,16,768]{2,1,0:T(8,128)(2,1)}), bf16[16,16,768]{2,1,0:T(8,128)(2,1)S(1)}, u32[]{:S(2)}, u32[]{:S(2)}) async-start(bf16[16,16,768]{2,1,0:T(8,128)(2,1)} %bitcast.29), calls=%async_computation.3 | async-start | bytes 786432 | tf_op jit(solution)/shard_map/all_to_all | solution.py:666
  85.2 9.4 %collective-permute-start.4 = (bf16[384,384]{1,0:T(8,128)(2,1)}, bf16[384,384]{1,0:T(8,128)(2,1)S(1)}, u32[]{:S(2)}, u32[]{:S(2)}) collective-permute-start(bf16[384,384]{1,0:T(8,128)(2,1)} %get-tuple-element.93), channel_id=1, source_target_pairs={{0,8},{1,9},{2,10},{3,11},{4,12},{5,13},{6,14},{7,15},{8,0},{9,1},... | collective-permute-start | bytes 884744 | tf_op jit(solution)/shard_map/ppermute | solution.py:854
  87.2 21.4 %collective-permute-start.7 = (bf16[192,1152]{1,0:T(8,128)(2,1)}, bf16[192,1152]{1,0:T(8,128)(2,1)S(1)}, u32[]{:S(2)}, u32[]{:S(2)}) collective-permute-start(bf16[192,1152]{1,0:T(8,128)(2,1)} %get-tuple-element.103), channel_id=1, source_target_pairs={{0,4},{1,5},{2,6},{3,7},{4,0},{5,1},{6,2},{7,3},{8,12},{9,13},{10,... | collective-permute-start | bytes 1327112 | tf_op jit(solution)/shard_map/ppermute | solution.py:854
  88.7 20.0 %collective-permute-start.8 = (bf16[192,1152]{1,0:T(8,128)(2,1)}, bf16[192,1152]{1,0:T(8,128)(2,1)S(1)}, u32[]{:S(2)}, u32[]{:S(2)}) collective-permute-start(bf16[192,1152]{1,0:T(8,128)(2,1)} %get-tuple-element.104), channel_id=1, source_target_pairs={{0,6},{1,7},{2,4},{3,5},{4,2},{5,3},{6,0},{7,1},{8,14},{9,15},{10,... | collective-permute-start | bytes 1327112 | tf_op jit(solution)/shard_map/ppermute | solution.py:854
  90.9 19.0 %collective-permute-start.6 = (bf16[192,1152]{1,0:T(8,128)(2,1)}, bf16[192,1152]{1,0:T(8,128)(2,1)S(1)}, u32[]{:S(2)}, u32[]{:S(2)}) collective-permute-start(bf16[192,1152]{1,0:T(8,128)(2,1)} %order.1), channel_id=1, source_target_pairs={{0,2},{1,3},{2,0},{3,1},{4,6},{5,7},{6,4},{7,5},{8,10},{9,11},{10,... | collective-permute-start | bytes 1327112 | tf_op jit(solution)/shard_map/ppermute | solution.py:854
  95.7 9.3 %collective-permute-start.9 = (bf16[192,384]{1,0:T(8,128)(2,1)S(1)}, bf16[192,384]{1,0:T(8,128)(2,1)S(1)}, u32[]{:S(2)}, u32[]{:S(2)}) collective-permute-start(bf16[192,384]{1,0:T(8,128)(2,1)S(1)} %get-tuple-element.105), channel_id=1, source_target_pairs={{0,16},{1,17},{2,18},{3,19},{4,20},{5,21},{6,22},{7,23},{8,24},{9,... | collective-permute-start | bytes 442376 | tf_op jit(solution)/shard_map/ppermute | solution.py:854
  102.1 27.0 %collective-permute-start.5 = (f32[192,768]{1,0:T(8,128)S(1)}, f32[192,768]{1,0:T(8,128)S(1)}, u32[]{:S(2)}, u32[]{:S(2)}) collective-permute-start(f32[192,768]{1,0:T(8,128)S(1)} %get-tuple-element.98), channel_id=1, source_target_pairs={{0,1},{1,0},{2,3},{3,2},{4,5},{5,4},{6,7},{7,6},{8,9},{9,8},{10,11... | collective-permute-start | bytes 1769480 | tf_op jit(solution)/shard_map/ppermute | solution.py:663
  111.2 6.0 %collective-permute-start.10 = (bf16[96,1152]{1,0:T(8,128)(2,1)S(1)}, bf16[96,1152]{1,0:T(8,128)(2,1)S(1)}, u32[]{:S(2)}, u32[]{:S(2)}) collective-permute-start(bf16[96,1152]{1,0:T(8,128)(2,1)S(1)} %get-tuple-element.108), channel_id=1, source_target_pairs={{0,8},{1,9},{2,10},{3,11},{4,12},{5,13},{6,14},{7,15},{8,0},{9,1},... | collective-permute-start | bytes 663560 | tf_op jit(solution)/shard_map/ppermute | solution.py:854
  111.6 8.2 %collective-permute-start.14 = (bf16[240,384]{1,0:T(8,128)(2,1)S(1)}, bf16[240,384]{1,0:T(8,128)(2,1)S(1)}, u32[]{:S(2)}, u32[]{:S(2)}) collective-permute-start(bf16[240,384]{1,0:T(8,128)(2,1)S(1)} %get-tuple-element.113.e0_ref), channel_id=1, source_target_pairs={{0,6},{1,7},{2,4},{3,5},{4,2},{5,3},{6,0},{7,1},{8,14},{9,15},{10,... | collective-permute-start | bytes 552968 | tf_op jit(solution)/shard_map/ppermute | solution.py:854
  114.1 7.4 %collective-permute-start.13 = (bf16[240,384]{1,0:T(8,128)(2,1)S(1)}, bf16[240,384]{1,0:T(8,128)(2,1)S(1)}, u32[]{:S(2)}, u32[]{:S(2)}) collective-permute-start(bf16[240,384]{1,0:T(8,128)(2,1)S(1)} %get-tuple-element.113.e0_ref), channel_id=1, source_target_pairs={{0,4},{1,5},{2,6},{3,7},{4,0},{5,1},{6,2},{7,3},{8,12},{9,13},{10,... | collective-permute-start | bytes 552968 | tf_op jit(solution)/shard_map/ppermute | solution.py:854
  114.7 6.9 %collective-permute-start.12 = (bf16[240,384]{1,0:T(8,128)(2,1)S(1)}, bf16[240,384]{1,0:T(8,128)(2,1)S(1)}, u32[]{:S(2)}, u32[]{:S(2)}) collective-permute-start(bf16[240,384]{1,0:T(8,128)(2,1)S(1)} %get-tuple-element.113.e0_ref), channel_id=1, source_target_pairs={{0,2},{1,3},{2,0},{3,1},{4,6},{5,7},{6,4},{7,5},{8,10},{9,11},{10,... | collective-permute-start | bytes 552968 | tf_op jit(solution)/shard_map/ppermute | solution.py:854
  117.2 7.3 %collective-permute-start.11 = (bf16[48,1152]{1,0:T(8,128)(2,1)S(1)}, bf16[48,1152]{1,0:T(8,128)(2,1)S(1)}, u32[]{:S(2)}, u32[]{:S(2)}) collective-permute-start(bf16[48,1152]{1,0:T(8,128)(2,1)S(1)} %get-tuple-element.112), channel_id=1, source_target_pairs={{0,16},{1,17},{2,18},{3,19},{4,20},{5,21},{6,22},{7,23},{8,24},{9,... | collective-permute-start | bytes 331784 | tf_op jit(solution)/shard_map/ppermute | solution.py:854
  124.6 6.7 %collective-permute-start.17 = (bf16[48,1152]{1,0:T(8,128)(2,1)S(1)}, bf16[48,1152]{1,0:T(8,128)(2,1)S(1)}, u32[]{:S(2)}, u32[]{:S(2)}) collective-permute-start(bf16[48,1152]{1,0:T(8,128)(2,1)S(1)} %get-tuple-element.114.t0_ref), channel_id=1, source_target_pairs={{0,24},{1,25},{2,26},{3,27},{4,28},{5,29},{6,30},{7,31},{8,16},{9,... | collective-permute-start | bytes 331784 | tf_op jit(solution)/shard_map/ppermute | solution.py:854
  126.7 6.9 %collective-permute-start.16 = (bf16[48,1152]{1,0:T(8,128)(2,1)S(1)}, bf16[48,1152]{1,0:T(8,128)(2,1)S(1)}, u32[]{:S(2)}, u32[]{:S(2)}) collective-permute-start(bf16[48,1152]{1,0:T(8,128)(2,1)S(1)} %get-tuple-element.114.t0_ref), channel_id=1, source_target_pairs={{0,16},{1,17},{2,18},{3,19},{4,20},{5,21},{6,22},{7,23},{8,24},{9,... | collective-permute-start | bytes 331784 | tf_op jit(solution)/shard_map/ppermute | solution.py:854
  126.7 6.9 %collective-permute-start.15 = (bf16[48,1152]{1,0:T(8,128)(2,1)S(1)}, bf16[48,1152]{1,0:T(8,128)(2,1)S(1)}, u32[]{:S(2)}, u32[]{:S(2)}) collective-permute-start(bf16[48,1152]{1,0:T(8,128)(2,1)S(1)} %get-tuple-element.114.t0_ref), channel_id=1, source_target_pairs={{0,8},{1,9},{2,10},{3,11},{4,12},{5,13},{6,14},{7,15},{8,0},{9,1},... | collective-permute-start | bytes 331784 | tf_op jit(solution)/shard_map/ppermute | solution.py:854
  134.7 8.3 %collective-permute-start.22 = (bf16[240,384]{1,0:T(8,128)(2,1)S(1)}, bf16[240,384]{1,0:T(8,128)(2,1)S(1)}, u32[]{:S(2)}, u32[]{:S(2)}) collective-permute-start(bf16[240,384]{1,0:T(8,128)(2,1)S(1)} %get-tuple-element.118.a_ref.c0_ref), channel_id=1, source_target_pairs={{0,16},{1,17},{2,18},{3,19},{4,20},{5,21},{6,22},{7,23},{8,24},{9,... | collective-permute-start | bytes 552968 | tf_op jit(solution)/shard_map/ppermute | solution.py:854
  135.5 14.0 %collective-permute-start.21 = (bf16[192,1152]{1,0:T(8,128)(2,1)S(1)}, bf16[192,1152]{1,0:T(8,128)(2,1)S(1)}, u32[]{:S(2)}, u32[]{:S(2)}) collective-permute-start(bf16[192,1152]{1,0:T(8,128)(2,1)S(1)} %get-tuple-element.117.a0_ref), channel_id=1, source_target_pairs={{0,6},{1,7},{2,4},{3,5},{4,2},{5,3},{6,0},{7,1},{8,14},{9,15},{10,... | collective-permute-start | bytes 1327112 | tf_op jit(solution)/shard_map/ppermute | solution.py:854
  137.9 16.9 %collective-permute-start.20 = (bf16[192,1152]{1,0:T(8,128)(2,1)S(1)}, bf16[192,1152]{1,0:T(8,128)(2,1)S(1)}, u32[]{:S(2)}, u32[]{:S(2)}) collective-permute-start(bf16[192,1152]{1,0:T(8,128)(2,1)S(1)} %get-tuple-element.117.a0_ref), channel_id=1, source_target_pairs={{0,4},{1,5},{2,6},{3,7},{4,0},{5,1},{6,2},{7,3},{8,12},{9,13},{10,... | collective-permute-start | bytes 1327112 | tf_op jit(solution)/shard_map/ppermute | solution.py:854
  138.5 16.6 %collective-permute-start.19 = (bf16[192,1152]{1,0:T(8,128)(2,1)S(1)}, bf16[192,1152]{1,0:T(8,128)(2,1)S(1)}, u32[]{:S(2)}, u32[]{:S(2)}) collective-permute-start(bf16[192,1152]{1,0:T(8,128)(2,1)S(1)} %get-tuple-element.117.a0_ref), channel_id=1, source_target_pairs={{0,2},{1,3},{2,0},{3,1},{4,6},{5,7},{6,4},{7,5},{8,10},{9,11},{10,... | collective-permute-start | bytes 1327112 | tf_op jit(solution)/shard_map/ppermute | solution.py:854
  143.1 12.0 %collective-permute-start.23 = (bf16[480,384]{1,0:T(8,128)(2,1)S(1)}, bf16[480,384]{1,0:T(8,128)(2,1)S(1)}, u32[]{:S(2)}, u32[]{:S(2)}) collective-permute-start(bf16[480,384]{1,0:T(8,128)(2,1)S(1)} %stack.13), channel_id=1, source_target_pairs={{0,8},{1,9},{2,10},{3,11},{4,12},{5,13},{6,14},{7,15},{8,0},{9,1},... | collective-permute-start | bytes 1105928 | tf_op jit(solution)/shard_map/ppermute | solution.py:854
  (17 other events, 233.8 us)

commit v4 on v3

--- a/solution.py
+++ b/solution.py
@@ -87,7 +87,9 @@
     return bucket_of(distance) == iota((buckets, 2 * TILE), 0)
 
 
-def prep_body(capacity, experts, routes_ref, cot_ref, place_out, out_ref, place_ref, sem):
+def prep_body(capacity, experts, routes_ref, cot_hbm, place_out, out_ref, place_ref, cot_ref, sem, load_sem):
+    load = pltpu.make_async_copy(cot_hbm, cot_ref, load_sem)
+    load.start()
     rows = cot_ref.shape[0]
     chosen = routes_ref[...]
     hot = chosen == iota((experts, rows), 0)
@@ -99,6 +101,7 @@
     place_ref[...] = place
     store = pltpu.make_async_copy(place_ref, place_out, sem)
     store.start()
+    load.wait()
     out_ref[...] = mm(place, cot_ref[...]).astype(BF)
     store.wait()
 
@@ -591,28 +594,42 @@
     grad_ref[...] = grad_res_ref[...] + passed
 
 
+def unpack_mine_body(bits_ref, a0_ref, qkv_out, wide_ref, sems):
+    put_quarter(0, a0_ref, bits_ref, wide_ref, qkv_out, sems, True)
+
+
+def put_quarter(number, ref, bits_ref, wide_ref, qkv_out, sems, wait=False):
+    shard = ref.shape[0] // 4
+    local = qkv_out.shape[2]
+    wide_ref[...] = ref[...].astype(F32)
+    copies = []
+    for d in range(4):
+        at = pl.multiple_of(((bits_ref[0] ^ number) * 4 + (bits_ref[1] ^ d)) * shard, shard)
+        for c in range(3):
+            copy = pltpu.make_async_copy(
+                wide_ref.at[pl.ds(d * shard, shard), pl.ds(c * local, local)],
+                qkv_out.at[c, pl.ds(at, shard), :],
+                sems.at[d, c],
+            )
+            copy.start()
+            copies.append(copy)
+    if wait:
+        for copy in copies:
+            copy.wait()
+    return copies
+
+
 def unpack_body(
-    bits_ref, a0_ref, a1_ref, a2_ref, a3_ref, c0_ref, c2_ref, near_ref,
+    bits_ref, a1_ref, a2_ref, a3_ref, c0_ref, c2_ref, near_ref, _begun,
     router_ref, norm_gain_ref, moe_gain_ref, bias_ref, qkv_out, w_out_out,
     wide_ref, w_out_ref, qkv_sems, out_sems,
 ):
     local = qkv_out.shape[2]
-    shard = a0_ref.shape[0] // 4
-    plane, depth = bits_ref[0], bits_ref[1]
+    shard = a1_ref.shape[0] // 4
+    depth = bits_ref[1]
     copies = []
-    for number, ref in enumerate((a0_ref, a1_ref, a2_ref, a3_ref)):
-        quarter = plane ^ number
-        wide_ref[number] = ref[...].astype(F32)
-        for d in range(4):
-            at = pl.multiple_of((quarter * 4 + (depth ^ d)) * shard, shard)
-            for c in range(3):
-                copy = pltpu.make_async_copy(
-                    wide_ref.at[number, pl.ds(d * shard, shard), pl.ds(c * local, local)],
-                    qkv_out.at[c, pl.ds(at, shard), :],
-                    qkv_sems.at[number, d, c],
-                )
-                copy.start()
-                copies.append(copy)
+    for number, ref in enumerate((a1_ref, a2_ref, a3_ref)):
+        copies += put_quarter(number + 1, ref, bits_ref, wide_ref.at[number], qkv_out, qkv_sems.at[number])
     size = c0_ref.shape[0]
     others = (c0_ref, near_ref.at[:size], c2_ref, near_ref.at[size:])
     for number, ref in enumerate(others):
@@ -681,12 +698,17 @@
     place, cot_slots = pl.pallas_call(
         functools.partial(prep_body, capacity, experts),
         out_shape=(hbm((slots, rows), BF),) + shape_of(((slots, width), BF)),
-        in_specs=vmem_specs(2),
+        in_specs=vmem_specs(1) + [ANY],
         out_specs=[ANY] + vmem_specs(1),
-        scratch_shapes=[pltpu.VMEM((slots, rows), BF), pltpu.SemaphoreType.DMA],
+        scratch_shapes=[
+            pltpu.VMEM((slots, rows), BF),
+            pltpu.VMEM((rows, width), BF),
+            pltpu.SemaphoreType.DMA,
+            pltpu.SemaphoreType.DMA,
+        ],
         cost_estimate=cost(2e9, 1e6),
         name="place_cotangent",
-    )(routes.reshape(1, rows), cotangent)
+    )(routes.reshape(1, rows), in_hbm(cotangent))
     cot_rows = exchange(cot_slots)
 
     bias_rows = jnp.pad(rel_bias.T, ((0, 8 - heads), (0, 0)))
@@ -954,24 +976,35 @@
     c_far = along[1](c_mine)
     (c_two,) = fused("stack", stack_body, [((2 * (quarter + lead), local), BF)], (c_mine, c_far))
     c_near = along[0](c_two)
+    begun = pl.pallas_call(
+        unpack_mine_body,
+        out_shape=hbm((3, width, local), F32),
+        in_specs=[SMEM] + vmem_specs(1),
+        out_specs=ANY,
+        scratch_shapes=[pltpu.VMEM((quarter, wide), F32), pltpu.SemaphoreType.DMA((4, 3))],
+        compiler_params=params(8),
+        cost_estimate=cost(1e3, 1e3),
+        name="unpack_mine",
+    )(position, mine)
     grad_router, grad_norm_gain, grad_moe_gain, grad_rel, grad_qkv, grad_out = pl.pallas_call(
         unpack_body,
         out_shape=shape_of(
             ((experts, width), F32), ((width,), F32), ((width,), F32), ((heads, buckets), F32)
         )
         + (hbm((3, width, local), F32), hbm((local, width), F32)),
-        in_specs=[SMEM] + vmem_specs(7),
+        in_specs=[SMEM] + vmem_specs(6) + [ANY],
         out_specs=vmem_specs(4) + [ANY] * 2,
+        input_output_aliases={7: 4},
         scratch_shapes=[
-            pltpu.VMEM((4, quarter, wide), F32),
+            pltpu.VMEM((3, quarter, wide), F32),
             pltpu.VMEM((4, quarter, local), F32),
-            pltpu.SemaphoreType.DMA((4, 4, 3)),
+            pltpu.SemaphoreType.DMA((3, 4, 3)),
             pltpu.SemaphoreType.DMA((4,)),
         ],
         compiler_params=params(12),
         cost_estimate=cost(1e3, 1e3),
         name="unpack",
-    )(position, *all_mine, c_mine, c_far, c_near)
+    )(position, *all_mine[1:], c_mine, c_far, c_near, begun)
 
     return (
         output,

time: 161 us -> 160 us (level)
    ppermute x18, waiting for transfers between devices: 36.7 us -> 35.1 us  [moves(): return lambda value: lax.ppermute(value, ('expert', 'tensor'), pairs)]
  transfers between devices with their start and end apart: 27 -> 27, of which waited for: 16 -> 16; matrix products, arithmetic and copies ran while one was open for 0% -> 0% of each run, Pallas kernels for 22% -> 23%
where the time goes in v4:
time: 160 us; the launch traced here: 159 us
  Pallas kernels  53.5 us (33%)
  waiting for transfers between devices  45.3 us (28%)
  starting transfers between devices  39.9 us (25%)
  blocking collectives  16.8 us (10%)
  local copies, waits for them, and re-layouts  2.04 us (1%)
    ppermute x18, waiting for transfers between devices, moves(): return lambda value: lax.ppermute(value, ('expert', 'tensor'), pairs)  35.1 us
    ppermute x18, starting transfers between devices, moves(): return lambda value: lax.ppermute(value, ('expert', 'tensor'), pairs)  23.4 us
    all_to_all x1, blocking collectives, exchange(): lax.all_to_all(value.reshape(experts, capacity, width), 'expert', split_a...  16.8 us
    all_to_all x3, starting transfers between devices, exchange(): lax.all_to_all(value.reshape(experts, capacity, width), 'expert', split_a...  15.5 us
    pallas_call x1, Pallas kernels, per_device(): pl.pallas_call(attend_back_body, out_shape=(*shape_of(((3 * heads, 8, 2 *...  9.49 us
    pallas_call x1, Pallas kernels, per_device(): pl.pallas_call(expert_body, out_shape=shape_of(((count, width), BF), ((ex...  9.27 us
    all_to_all x3, waiting for transfers between devices, exchange(): lax.all_to_all(value.reshape(experts, capacity, width), 'expert', split_a...  9.13 us
    pallas_call x1, Pallas kernels, per_device(): pl.pallas_call(attend_body, out_shape=shape_of(((rows, width), F32), ((ro...  8.24 us
  transfers between devices with their start and end apart: 27, of which 16 were waited for; matrix products, arithmetic and copies ran while one was open for 0% of the time, Pallas kernels for 23%

profile of v4, /device:TPU:0, one launch (start us, length us, event | category | flops | bytes accessed | tf_op | source)
XLA Modules:
  0.0 158.8 jit_solution(7770857675449581917)
XLA Ops:
  1.2 2.7 %place_cotangent.1 = (bf16[256,192]{1,0:T(8,128)(2,1)}, bf16[256,768]{1,0:T(8,128)(2,1)}) custom-call(s32[1,192]{1,0:T(1,128)} %bitcast.36, bf16[192,768]{1,0:T(8,128)(2,1)} %cot_hbm.3), custom_call_target="tpu_custom_call" | custom-call | flops 2000000000 | bytes 1000000 | tf_op jit(solution)/shard_map/place_cotangent/pallas_call | solution.py:698
  3.9 7.9 %all-to-all-start = ((bf16[16,16,768]{2,1,0:T(8,128)(2,1)}), bf16[16,16,768]{2,1,0:T(8,128)(2,1)S(1)}, u32[]{:S(2)}, u32[]{:S(2)}) async-start(bf16[16,16,768]{2,1,0:T(8,128)(2,1)} %bitcast.30), calls=%async_computation | async-start | bytes 786432 | tf_op jit(solution)/shard_map/all_to_all | solution.py:683
  12.0 8.2 %attention.1 = (f32[192,768]{1,0:T(8,128)S(1)}, f32[192,768]{1,0:T(8,128)S(1)}, bf16[384,384]{1,0:T(8,128)(2,1)}, bf16[384,1152]{1,0:T(8,128)(2,1)}, bf16[6,384,...) custom-call(s32[1]{0:T(128)} %bitcast.1.half_ref, s32[1,3]{1,0:T(1,128)S(1)} %copy-done.9, bf16[192,768]{1,0:T(8,128)(2,1)S(1)} %copy-done.3, ...), custom_call_target="tpu_custom_call" | custom-call | flops 8000000000 | bytes 4000000 | tf_op jit(solution)/shard_map/attention/pallas_call | solution.py:715
  20.6 4.4 %all-to-all-done = bf16[16,16,768]{2,1,0:T(8,128)(2,1)S(1)} async-done(((bf16[16,16,768]{2,1,0:T(8,128)(2,1)}), bf16[16,16,768]{2,1,0:T(8,128)(2,1)S(1)}, u32[]{:S(2)}, u32[]{:S(2)}) %all-to-all-start) | async-done | bytes 393248 | tf_op jit(solution)/shard_map/all_to_all | solution.py:683
  26.4 16.8 %all_to_all.20 = bf16[16,16,768]{2,1,0:T(8,128)(2,1)S(1)} all-to-all(bf16[16,16,768]{2,1,0:T(8,128)(2,1)S(1)} %bitcast.27), channel_id=1, replica_groups=mesh['expert'=16,'tensor'=2] {'expert'}, dimensions={0} | all-to-all | bytes 786432 | tf_op jit(solution)/shard_map/all_to_all | solution.py:683
  43.2 9.3 %expert.1 = (bf16[256,768]{1,0:T(8,128)(2,1)}, f32[16,768]{1,0:T(8,128)S(1)}, bf16[256,768]{1,0:T(8,128)(2,1)}, bf16[256,768]{1,0:T(8,128)(2,1)}, bf16[256,4608]...) custom-call(s32[1]{0:T(128)} %bitcast.1.half_ref, s32[1]{0:T(128)} %bitcast.2._expert.expert_ref, ...), custom_call_target="tpu_custom_call" | custom-call | flops 10000000000 | bytes 14000000 | tf_op jit(solution)/shard_map/expert/pallas_call | solution.py:765
  52.6 3.8 %all-to-all-start.2 = ((bf16[16,16,768]{2,1,0:T(8,128)(2,1)}), bf16[16,16,768]{2,1,0:T(8,128)(2,1)S(1)}, u32[]{:S(2)}, u32[]{:S(2)}) async-start(bf16[16,16,768]{2,1,0:T(8,128)(2,1)} %bitcast.10), calls=%async_computation.2 | async-start | bytes 786432 | tf_op jit(solution)/shard_map/all_to_all | solution.py:683
  57.5 7.2 %expert_grads.1 = (f32[1536,768]{1,0:T(8,128)}, f32[768,1536]{1,0:T(8,128)}) custom-call(bf16[256,1536]{1,0:T(8,128)(2,1)} %get-tuple-element.77.act_ref, bf16[256,1536]{1,0:T(8,128)(2,1)} %get-tuple-element.78.pre_ref, bf16[256,768]{1,0:T(8,128)(2,1)S(1)} %bitcast.26, bf16[256,768]{1,0:T(8,128)(2,1)} %get-tuple-element.79.gp_ref, ...), custom_call_target="tpu_custom_call" | custom-call | flops 5000000000 | bytes 14000000 | tf_op jit(solution)/shard_map/expert_grads/pallas_call | solution.py:799
  64.7 4.8 %all-to-all-done.2 = bf16[16,16,768]{2,1,0:T(8,128)(2,1)S(1)} async-done(((bf16[16,16,768]{2,1,0:T(8,128)(2,1)}), bf16[16,16,768]{2,1,0:T(8,128)(2,1)S(1)}, u32[]{:S(2)}, u32[]{:S(2)}) %all-to-all-start.2) | async-done | bytes 393248 | tf_op jit(solution)/shard_map/all_to_all | solution.py:683
  72.0 3.8 %all-to-all-start.3 = ((bf16[16,16,768]{2,1,0:T(8,128)(2,1)}), bf16[16,16,768]{2,1,0:T(8,128)(2,1)S(1)}, u32[]{:S(2)}, u32[]{:S(2)}) async-start(bf16[16,16,768]{2,1,0:T(8,128)(2,1)} %bitcast.29), calls=%async_computation.3 | async-start | bytes 786432 | tf_op jit(solution)/shard_map/all_to_all | solution.py:683
  75.8 9.5 %attention_back.1 = (f32[18,8,256]{2,1,0:T(8,128)S(1)}, f32[8,256]{1,0:T(8,128)S(1)}, bf16[192,1152]{1,0:T(8,128)(2,1)}, bf16[192,1152]{1,0:T(8,128)(2,1)}, bf16...) custom-call(s32[1]{0:T(128)} %bitcast.1.half_ref, ...), custom_call_target="tpu_custom_call" | custom-call | flops 10000000000 | bytes 10000000 | tf_op jit(solution)/shard_map/attention_back/pallas_call | solution.py:841
  91.5 3.2 %collective-permute-done.4.got_ref = bf16[384,384]{1,0:T(8,128)(2,1)S(1)} collective-permute-done((bf16[384,384]{1,0:T(8,128)(2,1)}, bf16[384,384]{1,0:T(8,128)(2,1)S(1)}, u32[]{:S(2)}, u32[]{:S(2)}) %collective-permute-start.4) | collective-permute-done | bytes 294944 | tf_op jit(solution)/shard_map/ppermute | solution.py:876
  95.8 2.6 %collective-permute-start.9 = (bf16[192,384]{1,0:T(8,128)(2,1)S(1)}, bf16[192,384]{1,0:T(8,128)(2,1)S(1)}, u32[]{:S(2)}, u32[]{:S(2)}) collective-permute-start(bf16[192,384]{1,0:T(8,128)(2,1)S(1)} %get-tuple-element.105), channel_id=1, source_target_pairs={{0,16},{1,17},{2,18},{3,19},{4,20},{5,21},{6,22},{7,23},{8,24},{9,... | collective-permute-start | bytes 442376 | tf_op jit(solution)/shard_map/ppermute | solution.py:876
  98.4 3.8 %small_grads.1 = (bf16[48,384]{1,0:T(8,128)(2,1)S(1)}, f32[192,768]{1,0:T(8,128)S(1)}, f32[192,768]{1,0:T(8,128)S(1)}) custom-call(s32[1]{0:T(128)} %bitcast.1.half_ref, f32[18,8,256]{2,1,0:T(8,128)S(1)} %get-tuple-element.88.folded_ref, f32[8,256]{1,0:T(8,128)S(1)} %get-tuple-element.89.edge_ref, f32[16,768]{1,0:T(8,128)S(1)} %get-tuple-element.90.router_grad_ref, ...), custom_call_target="tpu_custom_call" | custom-call | flops 1000 | bytes 1000 | tf_op jit(solution)/shard_map/small_grads/pallas_call | solution.py:909
  102.3 2.8 %collective-permute-done.9.got_ref = bf16[192,384]{1,0:T(8,128)(2,1)S(1)} collective-permute-done((bf16[192,384]{1,0:T(8,128)(2,1)S(1)}, bf16[192,384]{1,0:T(8,128)(2,1)S(1)}, u32[]{:S(2)}, u32[]{:S(2)}) %collective-permute-start.9) | collective-permute-done | bytes 147488 | tf_op jit(solution)/shard_map/ppermute | solution.py:876
  105.1 3.6 %collective-permute-done.7.a2_ref = bf16[192,1152]{1,0:T(8,128)(2,1)S(1)} collective-permute-done((bf16[192,1152]{1,0:T(8,128)(2,1)}, bf16[192,1152]{1,0:T(8,128)(2,1)S(1)}, u32[]{:S(2)}, u32[]{:S(2)}) %collective-permute-start.7) | collective-permute-done | bytes 442400 | tf_op jit(solution)/shard_map/ppermute | solution.py:876
  111.7 2.5 %collective-permute-start.14 = (bf16[240,384]{1,0:T(8,128)(2,1)S(1)}, bf16[240,384]{1,0:T(8,128)(2,1)S(1)}, u32[]{:S(2)}, u32[]{:S(2)}) collective-permute-start(bf16[240,384]{1,0:T(8,128)(2,1)S(1)} %get-tuple-element.113.e0_ref), channel_id=1, source_target_pairs={{0,6},{1,7},{2,4},{3,5},{4,2},{5,3},{6,0},{7,1},{8,14},{9,15},{10,... | collective-permute-start | bytes 552968 | tf_op jit(solution)/shard_map/ppermute | solution.py:876
  117.3 2.6 %collective-permute-start.11 = (bf16[48,1152]{1,0:T(8,128)(2,1)S(1)}, bf16[48,1152]{1,0:T(8,128)(2,1)S(1)}, u32[]{:S(2)}, u32[]{:S(2)}) collective-permute-start(bf16[48,1152]{1,0:T(8,128)(2,1)S(1)} %get-tuple-element.112), channel_id=1, source_target_pairs={{0,16},{1,17},{2,18},{3,19},{4,20},{5,21},{6,22},{7,23},{8,24},{9,... | collective-permute-start | bytes 331784 | tf_op jit(solution)/shard_map/ppermute | solution.py:876
  121.7 2.9 %collective-permute-done.11.got_ref = bf16[48,1152]{1,0:T(8,128)(2,1)S(1)} collective-permute-done((bf16[48,1152]{1,0:T(8,128)(2,1)S(1)}, bf16[48,1152]{1,0:T(8,128)(2,1)S(1)}, u32[]{:S(2)}, u32[]{:S(2)}) %collective-permute-start.11) | collective-permute-done | bytes 110624 | tf_op jit(solution)/shard_map/ppermute | solution.py:876
  135.6 2.4 %collective-permute-start.21 = (bf16[192,1152]{1,0:T(8,128)(2,1)S(1)}, bf16[192,1152]{1,0:T(8,128)(2,1)S(1)}, u32[]{:S(2)}, u32[]{:S(2)}) collective-permute-start(bf16[192,1152]{1,0:T(8,128)(2,1)S(1)} %get-tuple-element.117.a0_ref), channel_id=1, source_target_pairs={{0,6},{1,7},{2,4},{3,5},{4,2},{5,3},{6,0},{7,1},{8,14},{9,15},{10,... | collective-permute-start | bytes 1327112 | tf_op jit(solution)/shard_map/ppermute | solution.py:876
  139.1 4.0 %collective-permute-done.22.b_ref.c2_ref = bf16[240,384]{1,0:T(8,128)(2,1)S(1)} collective-permute-done((bf16[240,384]{1,0:T(8,128)(2,1)S(1)}, bf16[240,384]{1,0:T(8,128)(2,1)S(1)}, u32[]{:S(2)}, u32[]{:S(2)}) %collective-permute-start.22) | collective-permute-done | bytes 184352 | tf_op jit(solution)/shard_map/ppermute | solution.py:876
  144.9 4.7 %collective-permute-done.21.a3_ref = bf16[192,1152]{1,0:T(8,128)(2,1)S(1)} collective-permute-done((bf16[192,1152]{1,0:T(8,128)(2,1)S(1)}, bf16[192,1152]{1,0:T(8,128)(2,1)S(1)}, u32[]{:S(2)}, u32[]{:S(2)}) %collective-permute-start.21) | collective-permute-done | bytes 442400 | tf_op jit(solution)/shard_map/ppermute | solution.py:876
  149.6 5.3 %collective-permute-done.20.a2_ref = bf16[192,1152]{1,0:T(8,128)(2,1)S(1)} collective-permute-done((bf16[192,1152]{1,0:T(8,128)(2,1)S(1)}, bf16[192,1152]{1,0:T(8,128)(2,1)S(1)}, u32[]{:S(2)}, u32[]{:S(2)}) %collective-permute-start.20) | collective-permute-done | bytes 442400 | tf_op jit(solution)/shard_map/ppermute | solution.py:876
  155.2 3.5 %unpack.1 = (f32[16,768]{1,0:T(8,128)}, f32[768]{0:T(1024)}, f32[768]{0:T(1024)}, f32[6,32]{1,0:T(8,128)}, f32[3,768,384]{2,1,0:T(8,128)}, /*index=5*/f32[384,768]{1,0:T(8,128)}) custom-call(s32[2]{0:T(128)S(1)} %pad_add_fusion.bits_ref, bf16[192,1152]{1,0:T(8,128)(2,1)S(1)} %collective-permute-done.19.a1_ref, ...), custom_call_target="tpu_custom_call", output_to_operand_aliasing={{4}: (7, {})} | custom-call | flops 1000 | bytes 1000 | tf_op jit(solution)/shard_map/unpack/pallas_call | solution.py:989
  (82 shorter events, 35.3 us)
Async XLA Ops:
  0.6 11.2 %collective-permute-start = (bf16[192,768]{1,0:T(8,128)(2,1)}, bf16[192,768]{1,0:T(8,128)(2,1)S(1)}, u32[]{:S(2)}, u32[]{:S(2)}) collective-permute-start(bf16[192,768]{1,0:T(8,128)(2,1)} %x_ref.5), channel_id=1, source_target_pairs={{0,1},{1,0},{2,3},{3,2},{4,5},{5,4},{6,7},{7,6},{8,9},{9,8},{10,11... | collective-permute-start | bytes 884744 | tf_op jit(solution)/shard_map/ppermute | solution.py:680
  3.9 21.1 %all-to-all-start = ((bf16[16,16,768]{2,1,0:T(8,128)(2,1)}), bf16[16,16,768]{2,1,0:T(8,128)(2,1)S(1)}, u32[]{:S(2)}, u32[]{:S(2)}) async-start(bf16[16,16,768]{2,1,0:T(8,128)(2,1)} %bitcast.30), calls=%async_computation | async-start | bytes 786432 | tf_op jit(solution)/shard_map/all_to_all | solution.py:683
  52.5 4.9 %collective-permute-start.2 = (bf16[256,4608]{1,0:T(8,128)(2,1)}, bf16[256,4608]{1,0:T(8,128)(2,1)}, u32[]{:S(2)}, u32[]{:S(2)}) collective-permute-start(bf16[256,4608]{1,0:T(8,128)(2,1)} %get-tuple-element.80), channel_id=1, source_target_pairs={{0,1},{1,0},{2,3},{3,2},{4,5},{5,4},{6,7},{7,6},{8,9},{9,8},{10,11... | collective-permute-start | bytes 7077896 | tf_op jit(solution)/shard_map/ppermute | solution.py:680
  52.6 16.8 %all-to-all-start.2 = ((bf16[16,16,768]{2,1,0:T(8,128)(2,1)}), bf16[16,16,768]{2,1,0:T(8,128)(2,1)S(1)}, u32[]{:S(2)}, u32[]{:S(2)}) async-start(bf16[16,16,768]{2,1,0:T(8,128)(2,1)} %bitcast.10), calls=%async_computation.2 | async-start | bytes 786432 | tf_op jit(solution)/shard_map/all_to_all | solution.py:683
  72.0 18.3 %all-to-all-start.3 = ((bf16[16,16,768]{2,1,0:T(8,128)(2,1)}), bf16[16,16,768]{2,1,0:T(8,128)(2,1)S(1)}, u32[]{:S(2)}, u32[]{:S(2)}) async-start(bf16[16,16,768]{2,1,0:T(8,128)(2,1)} %bitcast.29), calls=%async_computation.3 | async-start | bytes 786432 | tf_op jit(solution)/shard_map/all_to_all | solution.py:683
  85.3 9.4 %collective-permute-start.4 = (bf16[384,384]{1,0:T(8,128)(2,1)}, bf16[384,384]{1,0:T(8,128)(2,1)S(1)}, u32[]{:S(2)}, u32[]{:S(2)}) collective-permute-start(bf16[384,384]{1,0:T(8,128)(2,1)} %get-tuple-element.93), channel_id=1, source_target_pairs={{0,8},{1,9},{2,10},{3,11},{4,12},{5,13},{6,14},{7,15},{8,0},{9,1},... | collective-permute-start | bytes 884744 | tf_op jit(solution)/shard_map/ppermute | solution.py:876
  87.3 21.4 %collective-permute-start.7 = (bf16[192,1152]{1,0:T(8,128)(2,1)}, bf16[192,1152]{1,0:T(8,128)(2,1)S(1)}, u32[]{:S(2)}, u32[]{:S(2)}) collective-permute-start(bf16[192,1152]{1,0:T(8,128)(2,1)} %get-tuple-element.103), channel_id=1, source_target_pairs={{0,4},{1,5},{2,6},{3,7},{4,0},{5,1},{6,2},{7,3},{8,12},{9,13},{10,... | collective-permute-start | bytes 1327112 | tf_op jit(solution)/shard_map/ppermute | solution.py:876
  88.8 20.0 %collective-permute-start.8 = (bf16[192,1152]{1,0:T(8,128)(2,1)}, bf16[192,1152]{1,0:T(8,128)(2,1)S(1)}, u32[]{:S(2)}, u32[]{:S(2)}) collective-permute-start(bf16[192,1152]{1,0:T(8,128)(2,1)} %get-tuple-element.104), channel_id=1, source_target_pairs={{0,6},{1,7},{2,4},{3,5},{4,2},{5,3},{6,0},{7,1},{8,14},{9,15},{10,... | collective-permute-start | bytes 1327112 | tf_op jit(solution)/shard_map/ppermute | solution.py:876
  91.0 19.0 %collective-permute-start.6 = (bf16[192,1152]{1,0:T(8,128)(2,1)}, bf16[192,1152]{1,0:T(8,128)(2,1)S(1)}, u32[]{:S(2)}, u32[]{:S(2)}) collective-permute-start(bf16[192,1152]{1,0:T(8,128)(2,1)} %order.1), channel_id=1, source_target_pairs={{0,2},{1,3},{2,0},{3,1},{4,6},{5,7},{6,4},{7,5},{8,10},{9,11},{10,... | collective-permute-start | bytes 1327112 | tf_op jit(solution)/shard_map/ppermute | solution.py:876
  95.8 9.3 %collective-permute-start.9 = (bf16[192,384]{1,0:T(8,128)(2,1)S(1)}, bf16[192,384]{1,0:T(8,128)(2,1)S(1)}, u32[]{:S(2)}, u32[]{:S(2)}) collective-permute-start(bf16[192,384]{1,0:T(8,128)(2,1)S(1)} %get-tuple-element.105), channel_id=1, source_target_pairs={{0,16},{1,17},{2,18},{3,19},{4,20},{5,21},{6,22},{7,23},{8,24},{9,... | collective-permute-start | bytes 442376 | tf_op jit(solution)/shard_map/ppermute | solution.py:876
  102.2 27.0 %collective-permute-start.5 = (f32[192,768]{1,0:T(8,128)S(1)}, f32[192,768]{1,0:T(8,128)S(1)}, u32[]{:S(2)}, u32[]{:S(2)}) collective-permute-start(f32[192,768]{1,0:T(8,128)S(1)} %get-tuple-element.98), channel_id=1, source_target_pairs={{0,1},{1,0},{2,3},{3,2},{4,5},{5,4},{6,7},{7,6},{8,9},{9,8},{10,11... | collective-permute-start | bytes 1769480 | tf_op jit(solution)/shard_map/ppermute | solution.py:680
  111.3 6.0 %collective-permute-start.10 = (bf16[96,1152]{1,0:T(8,128)(2,1)S(1)}, bf16[96,1152]{1,0:T(8,128)(2,1)S(1)}, u32[]{:S(2)}, u32[]{:S(2)}) collective-permute-start(bf16[96,1152]{1,0:T(8,128)(2,1)S(1)} %get-tuple-element.108), channel_id=1, source_target_pairs={{0,8},{1,9},{2,10},{3,11},{4,12},{5,13},{6,14},{7,15},{8,0},{9,1},... | collective-permute-start | bytes 663560 | tf_op jit(solution)/shard_map/ppermute | solution.py:876
  111.7 8.2 %collective-permute-start.14 = (bf16[240,384]{1,0:T(8,128)(2,1)S(1)}, bf16[240,384]{1,0:T(8,128)(2,1)S(1)}, u32[]{:S(2)}, u32[]{:S(2)}) collective-permute-start(bf16[240,384]{1,0:T(8,128)(2,1)S(1)} %get-tuple-element.113.e0_ref), channel_id=1, source_target_pairs={{0,6},{1,7},{2,4},{3,5},{4,2},{5,3},{6,0},{7,1},{8,14},{9,15},{10,... | collective-permute-start | bytes 552968 | tf_op jit(solution)/shard_map/ppermute | solution.py:876
  114.2 7.4 %collective-permute-start.13 = (bf16[240,384]{1,0:T(8,128)(2,1)S(1)}, bf16[240,384]{1,0:T(8,128)(2,1)S(1)}, u32[]{:S(2)}, u32[]{:S(2)}) collective-permute-start(bf16[240,384]{1,0:T(8,128)(2,1)S(1)} %get-tuple-element.113.e0_ref), channel_id=1, source_target_pairs={{0,4},{1,5},{2,6},{3,7},{4,0},{5,1},{6,2},{7,3},{8,12},{9,13},{10,... | collective-permute-start | bytes 552968 | tf_op jit(solution)/shard_map/ppermute | solution.py:876
  114.8 6.9 %collective-permute-start.12 = (bf16[240,384]{1,0:T(8,128)(2,1)S(1)}, bf16[240,384]{1,0:T(8,128)(2,1)S(1)}, u32[]{:S(2)}, u32[]{:S(2)}) collective-permute-start(bf16[240,384]{1,0:T(8,128)(2,1)S(1)} %get-tuple-element.113.e0_ref), channel_id=1, source_target_pairs={{0,2},{1,3},{2,0},{3,1},{4,6},{5,7},{6,4},{7,5},{8,10},{9,11},{10,... | collective-permute-start | bytes 552968 | tf_op jit(solution)/shard_map/ppermute | solution.py:876
  117.3 7.3 %collective-permute-start.11 = (bf16[48,1152]{1,0:T(8,128)(2,1)S(1)}, bf16[48,1152]{1,0:T(8,128)(2,1)S(1)}, u32[]{:S(2)}, u32[]{:S(2)}) collective-permute-start(bf16[48,1152]{1,0:T(8,128)(2,1)S(1)} %get-tuple-element.112), channel_id=1, source_target_pairs={{0,16},{1,17},{2,18},{3,19},{4,20},{5,21},{6,22},{7,23},{8,24},{9,... | collective-permute-start | bytes 331784 | tf_op jit(solution)/shard_map/ppermute | solution.py:876
  124.7 6.7 %collective-permute-start.17 = (bf16[48,1152]{1,0:T(8,128)(2,1)S(1)}, bf16[48,1152]{1,0:T(8,128)(2,1)S(1)}, u32[]{:S(2)}, u32[]{:S(2)}) collective-permute-start(bf16[48,1152]{1,0:T(8,128)(2,1)S(1)} %get-tuple-element.114.t0_ref), channel_id=1, source_target_pairs={{0,24},{1,25},{2,26},{3,27},{4,28},{5,29},{6,30},{7,31},{8,16},{9,... | collective-permute-start | bytes 331784 | tf_op jit(solution)/shard_map/ppermute | solution.py:876
  126.8 6.9 %collective-permute-start.16 = (bf16[48,1152]{1,0:T(8,128)(2,1)S(1)}, bf16[48,1152]{1,0:T(8,128)(2,1)S(1)}, u32[]{:S(2)}, u32[]{:S(2)}) collective-permute-start(bf16[48,1152]{1,0:T(8,128)(2,1)S(1)} %get-tuple-element.114.t0_ref), channel_id=1, source_target_pairs={{0,16},{1,17},{2,18},{3,19},{4,20},{5,21},{6,22},{7,23},{8,24},{9,... | collective-permute-start | bytes 331784 | tf_op jit(solution)/shard_map/ppermute | solution.py:876
  126.8 6.9 %collective-permute-start.15 = (bf16[48,1152]{1,0:T(8,128)(2,1)S(1)}, bf16[48,1152]{1,0:T(8,128)(2,1)S(1)}, u32[]{:S(2)}, u32[]{:S(2)}) collective-permute-start(bf16[48,1152]{1,0:T(8,128)(2,1)S(1)} %get-tuple-element.114.t0_ref), channel_id=1, source_target_pairs={{0,8},{1,9},{2,10},{3,11},{4,12},{5,13},{6,14},{7,15},{8,0},{9,1},... | collective-permute-start | bytes 331784 | tf_op jit(solution)/shard_map/ppermute | solution.py:876
  134.8 8.3 %collective-permute-start.22 = (bf16[240,384]{1,0:T(8,128)(2,1)S(1)}, bf16[240,384]{1,0:T(8,128)(2,1)S(1)}, u32[]{:S(2)}, u32[]{:S(2)}) collective-permute-start(bf16[240,384]{1,0:T(8,128)(2,1)S(1)} %get-tuple-element.118.a_ref.c0_ref), channel_id=1, source_target_pairs={{0,16},{1,17},{2,18},{3,19},{4,20},{5,21},{6,22},{7,23},{8,24},{9,... | collective-permute-start | bytes 552968 | tf_op jit(solution)/shard_map/ppermute | solution.py:876
  135.6 14.0 %collective-permute-start.21 = (bf16[192,1152]{1,0:T(8,128)(2,1)S(1)}, bf16[192,1152]{1,0:T(8,128)(2,1)S(1)}, u32[]{:S(2)}, u32[]{:S(2)}) collective-permute-start(bf16[192,1152]{1,0:T(8,128)(2,1)S(1)} %get-tuple-element.117.a0_ref), channel_id=1, source_target_pairs={{0,6},{1,7},{2,4},{3,5},{4,2},{5,3},{6,0},{7,1},{8,14},{9,15},{10,... | collective-permute-start | bytes 1327112 | tf_op jit(solution)/shard_map/ppermute | solution.py:876
  138.0 16.9 %collective-permute-start.20 = (bf16[192,1152]{1,0:T(8,128)(2,1)S(1)}, bf16[192,1152]{1,0:T(8,128)(2,1)S(1)}, u32[]{:S(2)}, u32[]{:S(2)}) collective-permute-start(bf16[192,1152]{1,0:T(8,128)(2,1)S(1)} %get-tuple-element.117.a0_ref), channel_id=1, source_target_pairs={{0,4},{1,5},{2,6},{3,7},{4,0},{5,1},{6,2},{7,3},{8,12},{9,13},{10,... | collective-permute-start | bytes 1327112 | tf_op jit(solution)/shard_map/ppermute | solution.py:876
  138.6 16.6 %collective-permute-start.19 = (bf16[192,1152]{1,0:T(8,128)(2,1)S(1)}, bf16[192,1152]{1,0:T(8,128)(2,1)S(1)}, u32[]{:S(2)}, u32[]{:S(2)}) collective-permute-start(bf16[192,1152]{1,0:T(8,128)(2,1)S(1)} %get-tuple-element.117.a0_ref), channel_id=1, source_target_pairs={{0,2},{1,3},{2,0},{3,1},{4,6},{5,7},{6,4},{7,5},{8,10},{9,11},{10,... | collective-permute-start | bytes 1327112 | tf_op jit(solution)/shard_map/ppermute | solution.py:876
  143.2 12.0 %collective-permute-start.23 = (bf16[480,384]{1,0:T(8,128)(2,1)S(1)}, bf16[480,384]{1,0:T(8,128)(2,1)S(1)}, u32[]{:S(2)}, u32[]{:S(2)}) collective-permute-start(bf16[480,384]{1,0:T(8,128)(2,1)S(1)} %stack.13), channel_id=1, source_target_pairs={{0,8},{1,9},{2,10},{3,11},{4,12},{5,13},{6,14},{7,15},{8,0},{9,1},... | collective-permute-start | bytes 1105928 | tf_op jit(solution)/shard_map/ppermute | solution.py:876
  (17 other events, 234.2 us)
